TPU v7x, 32 devices: a whole 2x2x4 slice. The times are simulated.
32 devices in a mesh: queue: 4 (over y, core), seq: 8 (over z, x).
Axes of the slice: x: 2, y: 2, z: 4, core: 2. Of those that a mesh axis runs over, the one named last changes fastest.
Arguments:
- latents: float32 [16, 16, 1024], P('queue', None, 'seq'), may hold values from -6 to 6
- step_index: int32 [16], P('queue'), may hold values from 0 to 29, as said below
- levels: float32 [31], replicated, may hold values from 0 to 1, as said below
- modulation: float32 [30, 5, 1152], replicated, may hold values from -4 to 4
- embed_weight: bfloat16 [16, 1152], replicated, may hold values from -1.5 to 1.5
- position: bfloat16 [1024, 1152], P('seq'), may hold values from -3 to 3
- qkv_weight: bfloat16 [1152, 3456], replicated, may hold values from -0.1875 to 0.1875
- q_gain: float32 [72], replicated, may hold values from 1 to 2.5
- k_gain: float32 [72], replicated, may hold values from 1 to 2.5
- text_kv: bfloat16 [2, 128, 1152], P(None, None, 'seq'), may hold values from -6 to 6
- out_weight: bfloat16 [1152, 1152], replicated, may hold values from -0.1875 to 0.1875
- final_weight: bfloat16 [1152, 16], replicated, may hold values from -0.1875 to 0.1875
- new_noise: float32 [16, 1024], P(None, 'seq'), may hold values from -6 to 6
Outputs:
- advanced: float32 [16, 16, 1024], P('queue', None, 'seq')
- velocity: float32 [16, 16, 1024], P('queue', None, 'seq')
Inputs may be any that keep to these rules, and one draw needn't show every extreme that they name: `step_index`: frame 0 has index 0 and the last frame 30 - 1; frame j otherwise has j * 30 // 16 or one more, at most 29. levels rise strictly from exactly 0 at index 0 to exactly 1 at index 30.
All inputs are finite; a program needn't handle non-finite values.
Results may differ from a plain program's by a relative error of at most 0.0044.
Values may be sent and summed in bfloat16 or wider, within the bound.
No kernel may reach another device: no remote copies, remote signals or barrier semaphores. Data moves between devices by JAX's collectives and lax.ppermute only.
A program may use at most 128 MiB of HBM per device.

v0:
```python
import math

import jax
import jax.numpy as jnp
from jax import lax
from jax.sharding import PartitionSpec as P

EPSILON = 1e-06


def passed_along(block, axis, distance):
    devices = range(lax.axis_size(axis))
    route = [(i - distance, i) for i in devices if i - distance in devices]
    return lax.ppermute(block, axis, route)


def layer_norm(values):
    center = values - jnp.mean(values, axis=-1, keepdims=True)
    return center * lax.rsqrt(jnp.mean(center * center, axis=-1, keepdims=True) + EPSILON)


def head_norm(values, gain_vector):
    widened = values.astype(jnp.float32)
    scaled = (
        widened
        * lax.rsqrt(jnp.mean(widened * widened, axis=-1, keepdims=True) + EPSILON)
        * gain_vector
    )
    return scaled.astype(jnp.bfloat16)


def text_mix(query_block, text_keys, text_values, factor):
    text_scores = (
        jnp.einsum("fqhe,khe->fhqk", query_block, text_keys, preferred_element_type=jnp.float32)
        * factor
    )
    text_weights = jnp.exp(text_scores)
    text_numerator = jnp.einsum(
        "fhqk,khe->fqhe",
        text_weights.astype(jnp.bfloat16),
        text_values,
        preferred_element_type=jnp.float32,
    )
    text_sum = jnp.moveaxis(jnp.sum(text_weights, axis=-1), 1, 2)[..., None]
    return text_numerator / text_sum


def frame_attention(queries, keys_all, values_all, text_keys, text_values):
    frame_count, token_count, head_count, head_width = queries.shape
    factor = 1.0 / math.sqrt(head_width)
    block_rows = 512
    block_count = token_count // block_rows
    grouped = jnp.moveaxis(
        queries.reshape(frame_count, block_count, block_rows, head_count, head_width), 1, 0
    )

    def one_block(query_block):
        scores = (
            jnp.einsum("fqhe,fkhe->fhqk", query_block, keys_all, preferred_element_type=jnp.float32)
            * factor
        )
        weights = jnp.exp(scores)
        numerator = jnp.einsum(
            "fhqk,fkhe->fqhe",
            weights.astype(jnp.bfloat16),
            values_all,
            preferred_element_type=jnp.float32,
        )
        weight_sum = jnp.moveaxis(jnp.sum(weights, axis=-1), 1, 2)[..., None]
        return numerator / weight_sum + text_mix(query_block, text_keys, text_values, factor)

    mixture = lax.map(one_block, grouped)
    return jnp.moveaxis(mixture, 0, 1).reshape(frame_count, token_count, head_count, head_width)


def body(
    latents,
    step_index,
    levels,
    modulation,
    embed_weight,
    position,
    qkv_weight,
    q_gain,
    k_gain,
    text_kv,
    out_weight,
    final_weight,
    new_noise,
):
    highest = lax.Precision.HIGHEST
    frame_count = latents.shape[0]
    tok_local = latents.shape[2]
    steps_count = modulation.shape[0]
    model_width = modulation.shape[2]
    head_width = q_gain.shape[0]
    select = (step_index[:, None] == jnp.arange(steps_count, dtype=jnp.int32)[None, :]).astype(
        jnp.float32
    )
    frame_mods = jnp.dot(
        select, modulation.reshape(steps_count, 5 * model_width), precision=highest
    ).reshape(frame_count, 5, 1, model_width)
    level_low = jnp.dot(select, levels[:steps_count], precision=highest)
    level_high = jnp.dot(select, levels[1:], precision=highest)
    step_size = level_high - level_low
    text_len = text_kv.shape[1]
    text_keys = head_norm(text_kv[0].reshape(text_len, -1, head_width), k_gain)
    text_values = text_kv[1].reshape(text_len, -1, head_width)
    hidden = jnp.einsum("fcn,cd->fnd", latents, embed_weight.astype(jnp.float32), precision=highest)
    hidden = hidden + position.astype(jnp.float32)[None]
    normed = (layer_norm(hidden) * (1.0 + frame_mods[:, 1]) + frame_mods[:, 0]).astype(jnp.bfloat16)
    projected = jnp.dot(
        normed.reshape(frame_count * tok_local, model_width),
        qkv_weight,
        preferred_element_type=jnp.float32,
    )
    projected = projected.astype(jnp.bfloat16).reshape(frame_count, tok_local, 3 * model_width)
    queries = projected[:, :, :model_width]
    keys_raw = projected[:, :, model_width : 2 * model_width]
    values_raw = projected[:, :, 2 * model_width :]
    key_part, value_part = (
        lax.all_to_all(keys_raw, "seq", split_axis=2, concat_axis=1, tiled=True),
        lax.all_to_all(values_raw, "seq", split_axis=2, concat_axis=1, tiled=True),
    )
    all_tokens, local_width = (key_part.shape[1], key_part.shape[2])
    local_heads = local_width // head_width
    key_hat = head_norm(key_part.reshape(frame_count, all_tokens, local_heads, head_width), k_gain)
    value_four = value_part.reshape(frame_count, all_tokens, local_heads, head_width)
    query_part = lax.all_to_all(queries, "seq", split_axis=2, concat_axis=0, tiled=True)
    stacked, item_count, width_here = query_part.shape
    sources = stacked // frame_count
    arranged = jnp.moveaxis(query_part.reshape(sources, frame_count, item_count, width_here), 0, 1)
    arranged = arranged.reshape(frame_count, sources * item_count, local_heads, head_width)
    mixture = frame_attention(
        head_norm(arranged, q_gain), key_hat, value_four, text_keys, text_values
    )
    mixture = mixture.astype(jnp.bfloat16).reshape(frame_count, sources, item_count, width_here)
    mixture = jnp.moveaxis(mixture, 1, 0).reshape(stacked, item_count, width_here)
    attention = lax.all_to_all(mixture, "seq", split_axis=0, concat_axis=2, tiled=True)
    branch = jnp.dot(
        attention.reshape(frame_count * tok_local, model_width),
        out_weight,
        preferred_element_type=jnp.float32,
    )
    hidden_two = hidden + frame_mods[:, 2] * branch.reshape(frame_count, tok_local, model_width)
    normed_two = (layer_norm(hidden_two) * (1.0 + frame_mods[:, 4]) + frame_mods[:, 3]).astype(
        jnp.bfloat16
    )
    velocity = jnp.einsum(
        "fnd,dc->fcn", normed_two, final_weight, preferred_element_type=jnp.float32
    )
    updated = latents + velocity * step_size[:, None, None]
    arrived = passed_along(updated[0], "queue", -1)
    at_end = lax.axis_index("queue") == lax.axis_size("queue") - 1
    arrived = jnp.where(at_end, new_noise, arrived)
    advanced = jnp.concatenate([updated[1:], arrived[None]], axis=0)
    return (advanced, velocity)


def solution(mesh):
    in_specs = (
        P("queue", None, "seq"),
        P("queue"),
        P(),
        P(),
        P(),
        P("seq", None),
        P(),
        P(),
        P(),
        P(None, None, "seq"),
        P(),
        P(),
        P(None, "seq"),
    )
    out_specs = (P("queue", None, "seq"), P("queue", None, "seq"))
    return jax.shard_map(body, mesh=mesh, in_specs=in_specs, out_specs=out_specs, check_vma=False)
```

profile of v0, /device:TPU:1, one launch (start us, length us, event | category | flops | bytes accessed | tf_op | source)
XLA Modules:
  0.0 236.5 jit_solution(16979283981727054826)
XLA Ops:
  10.9 8.4 %convolution_convert_fusion = bf16[512,3456]{1,0:T(8,128)(2,1)S(1)} fusion(bf16[512,1152]{1,0:T(8,128)(2,1)S(1)} %bitcast.188, bf16[1152,3456]{1,0:T(8,128)(2,1)} %param.21), kind=kOutput, calls=%fused_computation.21 | convolution fusion | flops 4078632960 | bytes 12681216 | tf_op jit(solution)/shard_map/dot_general | solution.py:112
  21.3 3.4 %copy.77 = bf16[4,128,1152]{1,0,2:T(4,128)(2,1)} copy(bf16[4,128,1152]{2,1,0:T(8,128)(2,1)} %get-tuple-element.80) | data formatting | bytes 2359296
  24.7 6.4 %all-to-all-start.1 = ((bf16[4,128,1152]{1,0,2:T(4,128)(2,1)}), bf16[4,128,1152]{1,0,2:T(4,128)(2,1)}, u32[]{:S(2)}, u32[]{:S(2)}) async-start(bf16[4,128,1152]{1,0,2:T(4,128)(2,1)} %copy.77), calls=%async_computation.1 | async-start | bytes 2359296 | tf_op jit(solution)/shard_map/all_to_all | solution.py:122
  31.1 3.4 %copy.76 = bf16[4,128,1152]{1,0,2:T(4,128)(2,1)} copy(bf16[4,128,1152]{2,1,0:T(8,128)(2,1)} %get-tuple-element.81) | data formatting | bytes 2359296
  34.5 24.4 %all-to-all-done.1 = bf16[4,128,1152]{1,0,2:T(4,128)(2,1)} async-done(((bf16[4,128,1152]{1,0,2:T(4,128)(2,1)}), bf16[4,128,1152]{1,0,2:T(4,128)(2,1)}, u32[]{:S(2)}, u32[]{:S(2)}) %all-to-all-start.1) | async-done | bytes 1179680 | tf_op jit(solution)/shard_map/all_to_all | solution.py:122
  58.9 4.7 %all-to-all-start = ((bf16[4,128,1152]{1,0,2:T(4,128)(2,1)}), bf16[4,128,1152]{1,0,2:T(4,128)(2,1)}, u32[]{:S(2)}, u32[]{:S(2)}) async-start(bf16[4,128,1152]{1,0,2:T(4,128)(2,1)} %copy.76), calls=%async_computation | async-start | bytes 2359296 | tf_op jit(solution)/shard_map/all_to_all | solution.py:129
  63.6 3.4 %copy.78 = bf16[4,128,1152]{1,0,2:T(4,128)(2,1)} copy(bf16[4,128,1152]{2,1,0:T(8,128)(2,1)} %get-tuple-element.79) | data formatting | bytes 2359296
  69.5 21.4 %all-to-all-done = bf16[4,128,1152]{1,0,2:T(4,128)(2,1)} async-done(((bf16[4,128,1152]{1,0,2:T(4,128)(2,1)}), bf16[4,128,1152]{1,0,2:T(4,128)(2,1)}, u32[]{:S(2)}, u32[]{:S(2)}) %all-to-all-start) | async-done | bytes 1179680 | tf_op jit(solution)/shard_map/all_to_all | solution.py:129
  90.9 5.1 %all-to-all-start.2 = ((bf16[4,128,1152]{1,0,2:T(4,128)(2,1)}), bf16[4,128,1152]{1,0,2:T(4,128)(2,1)}, u32[]{:S(2)}, u32[]{:S(2)}) async-start(bf16[4,128,1152]{1,0,2:T(4,128)(2,1)} %copy.78), calls=%async_computation.2 | async-start | bytes 2359296 | tf_op jit(solution)/shard_map/all_to_all | solution.py:123
  101.3 3.3 %reshape.149 = f32[4,1024,2,72]{1,3,2,0:T(8,128)} reshape(f32[4,8,128,144]{2,1,3,0:T(8,128)} %copy.63) | data formatting | bytes 4718592 | tf_op jit(solution)/shard_map/convert_element_type | solution.py:23
  104.6 3.8 %copy.60 = f32[4,8,128,144]{2,1,3,0:T(8,128)} copy(f32[4,8,128,144]{2,3,1,0:T(8,128)} %bitcast.177) | data formatting | bytes 4718592 | tf_op jit(solution)/shard_map/mul | solution.py:26
  108.4 3.3 %mul.145 = f32[4,1024,2,72]{1,3,2,0:T(8,128)} reshape(f32[4,8,128,144]{2,1,3,0:T(8,128)} %copy.60) | data formatting | bytes 4718592 | tf_op jit(solution)/shard_map/mul | solution.py:26
  117.4 3.8 %reshape.148 = f32[4,2,512,2,72]{2,1,4,3,0:T(2,128)} reshape(f32[4,8,128,144]{2,1,3,0:T(8,128)} %copy.59) | data formatting | bytes 4718592 | tf_op jit(solution)/shard_map/convert_element_type | solution.py:23
  121.1 3.1 %fusion.21 = bf16[2,4,512,2,72]{2,0,4,3,1:T(2,128)(2,1)S(1)} fusion(f32[72]{0:T(128)S(1)} %copy-done.12, f32[4,2,512,2,72]{2,1,4,3,0:T(2,128)} %reshape.148, f32[4,2,512,2]{2,1,3,0:T(2,128)S(1)} %rsqrt.45), kind=kLoop, calls=%fused_computation.38 | loop fusion | flops 1769472 | bytes 3572000 | tf_op jit(solution)/shard_map/transpose | solution.py:53
  133.2 47.0 %while.10 = (s32[]{:T(128)}, bf16[2,4,512,2,72]{2,4,3,1,0:T(8,128)(2,1)}, bf16[2,4,512,2,72]{2,4,3,1,0:T(8,128)(2,1)}, bf16[4,1024,2,72]{1,3,2,0:T(8,128)(2,1)},...) while((s32[]{:T(128)}, ...), condition=%wide.region_8.9_spmd, body=%wide.region_5.8_spmd.sunk | while | flops 1378705408 | bytes 51816048 | solution.py:72
  133.2 10.3 %fusion.64 = (f32[4,2,512]{2,1,0:T(2,128)S(1)}, f32[4,2,512,1024]{3,2,1,0:T(8,128)}) fusion(bf16[4,1024,2,72]{1,3,2,0:T(8,128)(2,1)} %get-tuple-element.165, bf16[2,4,512,2,72]{2,4,3,1,0:T(8,128)(2,1)} %get-tuple-element.164, s32[]{:T(128)} %get-tuple-element.154), kind=kOutput, calls=%fused_computation.1.clone.1 | convolution fusion | flops 612364288 | bytes 18563584 | tf_op jit(solution)/shard_map/while/body/eval_jaxpr/fqhe,fkhe->fhqk/dot_general | solution.py:59
  143.5 9.9 %fusion.65 = f32[4,512,2,72]{1,3,2,0:T(8,128)} fusion(bf16[4,1024,2,72]{1,3,2,0:T(8,128)(2,1)} %get-tuple-element.166, f32[4,2,512,1024]{3,2,1,0:T(8,128)} %get-tuple-element.142), kind=kOutput, calls=%fused_computation.8.clone.1 | convolution fusion | flops 612368384 | bytes 19136512 | tf_op jit(solution)/shard_map/while/body/eval_jaxpr/fhqk,fkhe->fqhe/dot_general | solution.py:63
  156.7 10.3 %fusion.64 = (f32[4,2,512]{2,1,0:T(2,128)S(1)}, f32[4,2,512,1024]{3,2,1,0:T(8,128)}) fusion(bf16[4,1024,2,72]{1,3,2,0:T(8,128)(2,1)} %get-tuple-element.165, bf16[2,4,512,2,72]{2,4,3,1,0:T(8,128)(2,1)} %get-tuple-element.164, s32[]{:T(128)} %get-tuple-element.154), kind=kOutput, calls=%fused_computation.1.clone.1 | convolution fusion | flops 612364288 | bytes 18563584 | tf_op jit(solution)/shard_map/while/body/eval_jaxpr/fqhe,fkhe->fhqk/dot_general | solution.py:59
  167.0 9.9 %fusion.65 = f32[4,512,2,72]{1,3,2,0:T(8,128)} fusion(bf16[4,1024,2,72]{1,3,2,0:T(8,128)(2,1)} %get-tuple-element.166, f32[4,2,512,1024]{3,2,1,0:T(8,128)} %get-tuple-element.142), kind=kOutput, calls=%fused_computation.8.clone.1 | convolution fusion | flops 612368384 | bytes 19136512 | tf_op jit(solution)/shard_map/while/body/eval_jaxpr/fhqk,fkhe->fqhe/dot_general | solution.py:63
  180.2 3.5 %copy.68 = bf16[4,2,512,2,72]{2,1,4,3,0:T(2,128)(2,1)} copy(bf16[4,2,512,2,72]{2,4,3,0,1:T(8,128)(2,1)} %bitcast.128) | data formatting | bytes 2359296 | tf_op jit(solution)/shard_map/convert_element_type | solution.py:137
  183.7 3.9 %convert_element_type.99 = bf16[4,8,128,144]{2,1,3,0:T(8,128)(2,1)} reshape(bf16[4,2,512,2,72]{2,1,4,3,0:T(2,128)(2,1)} %copy.68) | data formatting | bytes 2359296 | tf_op jit(solution)/shard_map/convert_element_type | solution.py:137
  190.1 5.4 %all-to-all-start.3 = ((bf16[32,128,144]{1,2,0:T(8,128)(2,1)}), bf16[32,128,144]{1,2,0:T(8,128)(2,1)}, u32[]{:S(2)}, u32[]{:S(2)}) async-start(bf16[32,128,144]{1,2,0:T(8,128)(2,1)} %bitcast.180), calls=%async_computation.3 | async-start | bytes 2359296 | tf_op jit(solution)/shard_map/all_to_all | solution.py:139
  195.9 26.5 %all-to-all-done.3 = bf16[32,128,144]{1,2,0:T(8,128)(2,1)} async-done(((bf16[32,128,144]{1,2,0:T(8,128)(2,1)}), bf16[32,128,144]{1,2,0:T(8,128)(2,1)}, u32[]{:S(2)}, u32[]{:S(2)}) %all-to-all-start.3) | async-done | bytes 1179680 | tf_op jit(solution)/shard_map/all_to_all | solution.py:139
  228.5 4.9 %collective-permute-start = (f32[16,128]{1,0:T(8,128)S(1)}, f32[16,128]{1,0:T(8,128)S(1)}, u32[]{:S(2)}, u32[]{:S(2)}) collective-permute-start(f32[16,128]{1,0:T(8,128)S(1)} %slice_bitcast_fusion.3), channel_id=1, source_target_pairs={{8,0},{16,8},{24,16},{9,1},{17,9},{25,17},{10,2},{18,10},{26,18},{... | collective-permute-start | bytes 24584 | tf_op jit(solution)/shard_map/ppermute | solution.py:14
  (89 shorter events, 53.0 us)
Async XLA Ops:
  0.6 223.2 %copy-start = (bf16[1152,1152]{1,0:T(8,128)(2,1)S(1)}, bf16[1152,1152]{1,0:T(8,128)(2,1)}, u32[]{:S(2)}) copy-start(bf16[1152,1152]{1,0:T(8,128)(2,1)} %param.25) | copy-start | bytes 7962628
  1.8 2.6 %copy-start.6 = (f32[30,5,1152]{2,0,1:T(8,128)S(1)}, f32[30,5,1152]{2,0,1:T(8,128)}, u32[]{:S(2)}) copy-start(f32[30,5,1152]{2,0,1:T(8,128)} %param.18) | copy-start | bytes 2073604
  4.0 1.4 copy-start.1
  5.5 1.3 copy-start.11
  24.7 34.2 %all-to-all-start.1 = ((bf16[4,128,1152]{1,0,2:T(4,128)(2,1)}), bf16[4,128,1152]{1,0,2:T(4,128)(2,1)}, u32[]{:S(2)}, u32[]{:S(2)}) async-start(bf16[4,128,1152]{1,0,2:T(4,128)(2,1)} %copy.77), calls=%async_computation.1 | async-start | bytes 2359296 | tf_op jit(solution)/shard_map/all_to_all | solution.py:122
  34.4 32.5 %copy-start.7 = (bf16[2,128,144]{1,2,0:T(8,128)(2,1)S(1)}, bf16[2,128,144]{1,2,0:T(8,128)(2,1)}, u32[]{:S(2)}) copy-start(bf16[2,128,144]{1,2,0:T(8,128)(2,1)} %param.24) | copy-start | bytes 221188
  34.4 32.6 %copy-start.10 = (f32[72]{0:T(128)S(1)}, f32[72]{0:T(128)}, u32[]{:S(2)}) copy-start(f32[72]{0:T(128)} %param.23) | copy-start | bytes 868
  58.9 32.1 %all-to-all-start = ((bf16[4,128,1152]{1,0,2:T(4,128)(2,1)}), bf16[4,128,1152]{1,0,2:T(4,128)(2,1)}, u32[]{:S(2)}, u32[]{:S(2)}) async-start(bf16[4,128,1152]{1,0,2:T(4,128)(2,1)} %copy.76), calls=%async_computation | async-start | bytes 2359296 | tf_op jit(solution)/shard_map/all_to_all | solution.py:129
  90.9 36.4 %all-to-all-start.2 = ((bf16[4,128,1152]{1,0,2:T(4,128)(2,1)}), bf16[4,128,1152]{1,0,2:T(4,128)(2,1)}, u32[]{:S(2)}, u32[]{:S(2)}) async-start(bf16[4,128,1152]{1,0,2:T(4,128)(2,1)} %copy.78), calls=%async_computation.2 | async-start | bytes 2359296 | tf_op jit(solution)/shard_map/all_to_all | solution.py:123
  96.0 2.9 %copy-start.5 = (bf16[4,128,1152]{1,2,0:T(8,128)(2,1)S(1)}, bf16[4,128,1152]{1,2,0:T(8,128)(2,1)}, u32[]{:S(2)}) copy-start(bf16[4,128,1152]{1,2,0:T(8,128)(2,1)} %copy.62) | copy-start | bytes 3538948
  117.4 3.8 %copy-start.12 = (f32[72]{0:T(128)S(1)}, f32[72]{0:T(128)}, u32[]{:S(2)}) copy-start(f32[72]{0:T(128)} %param.22) | copy-start | bytes 868
  121.1 4.3 %copy-start.4 = (f32[4,1024,2,72]{1,3,2,0:T(8,128)S(1)}, f32[4,1024,2,72]{1,3,2,0:T(8,128)}, u32[]{:S(2)}) copy-start(f32[4,1024,2,72]{1,3,2,0:T(8,128)} %reshape.149) | copy-start | bytes 7077892
  153.4 2.1 copy-start.3
  176.9 2.1 copy-start.3
  187.6 7.9 %copy-start.14 = (f32[31]{0:T(128)S(1)}, f32[31]{0:T(128)}, u32[]{:S(2)}) copy-start(f32[31]{0:T(128)} %param.17) | copy-start | bytes 376
  190.1 32.3 %all-to-all-start.3 = ((bf16[32,128,144]{1,2,0:T(8,128)(2,1)}), bf16[32,128,144]{1,2,0:T(8,128)(2,1)}, u32[]{:S(2)}, u32[]{:S(2)}) async-start(bf16[32,128,144]{1,2,0:T(8,128)(2,1)} %bitcast.180), calls=%async_computation.3 | async-start | bytes 2359296 | tf_op jit(solution)/shard_map/all_to_all | solution.py:139
  222.4 2.0 copy-start.2
  226.4 0.8 copy-start.8
  226.5 0.8 copy-start.13
  226.5 9.4 %copy-start.9 = (f32[16,128]{1,0:T(8,128)S(1)}, f32[16,128]{1,0:T(8,128)}, u32[]{:S(2)}) copy-start(f32[16,128]{1,0:T(8,128)} %param.27) | copy-start | bytes 24580
  228.5 7.3 %collective-permute-start = (f32[16,128]{1,0:T(8,128)S(1)}, f32[16,128]{1,0:T(8,128)S(1)}, u32[]{:S(2)}, u32[]{:S(2)}) collective-permute-start(f32[16,128]{1,0:T(8,128)S(1)} %slice_bitcast_fusion.3), channel_id=1, source_target_pairs={{8,0},{16,8},{24,16},{9,1},{17,9},{25,17},{10,2},{18,10},{26,18},{... | collective-permute-start | bytes 24584 | tf_op jit(solution)/shard_map/ppermute | solution.py:14
where the time goes:
time: 238 us; the launch traced here: 236 us
  waiting for transfers between devices  74.7 us (31%)
  matrix products  62.3 us (26%)
  local copies, waits for them, and re-layouts  54.7 us (23%)
  starting transfers between devices  26.4 us (11%)
  other arithmetic  17.3 us (7%)
    all_to_all x1, waiting for transfers between devices, body(): lax.all_to_all(mixture, 'seq', split_axis=0, concat_axis=2, tiled=True)  26.5 us
    all_to_all x1, waiting for transfers between devices, body(): lax.all_to_all(keys_raw, 'seq', split_axis=2, concat_axis=1, tiled=True)  24.4 us
    all_to_all x1, waiting for transfers between devices, body(): lax.all_to_all(queries, 'seq', split_axis=2, concat_axis=0, tiled=True)  21.4 us
    dot_general x2, matrix products, one_block(): jnp.einsum('fqhe,fkhe->fhqk', query_block, keys_all, preferred_element_ty...  20.7 us
    dot_general x2, matrix products, one_block(): jnp.einsum('fhqk,fkhe->fqhe', weights.astype(jnp.bfloat16), values_all, p...  19.8 us
    unnamed x34, local copies, waits for them, and re-layouts  12.2 us
    convert_element_type x4, local copies, waits for them, and re-layouts, head_norm(): widened = values.astype(jnp.float32)  11.4 us
    dot_general x1, matrix products, body(): jnp.dot(normed.reshape(frame_count * tok_local, model_width), qkv_weight,...  8.42 us
  transfers between devices with their start and end apart: 5, of which 4 were waited for; matrix products, arithmetic and copies ran while one was open for 17% of the time, Pallas kernels for 0%

commit v1 on v0

v1 whole, which is shorter than its diff:
```python
import functools
import math

import jax
import jax.numpy as jnp
from jax import lax
from jax.experimental import pallas as pl
from jax.experimental.pallas import tpu as pltpu
from jax.sharding import PartitionSpec as P

EPSILON = 1e-06
LANES = 128
ROWS = 16
F32 = jnp.float32
BF16 = jnp.bfloat16
VMEM_LIMIT = 56 * 1024 * 1024
NT = (((1,), (1,)), ((), ()))
TN = (((0,), (0,)), ((), ()))


def dot(a, b, dims=(((1,), (0,)), ((), ()))):
    return lax.dot_general(a, b, dims, preferred_element_type=F32)


def split_parts(values):
    high = values.astype(BF16)
    low = (values - high.astype(F32)).astype(BF16)
    return high, low


def prep_kernel(frames, share, position_ref, latents_ref, *payload_refs):
    tokens, width = position_ref.shape
    half = tokens // 2
    pieces = half // ROWS
    core = lax.rem(lax.axis_index("queue"), 2)
    own_frame = lax.div(lax.axis_index("seq"), share)
    for piece in range(pieces):
        start = pl.multiple_of(core * half + piece * ROWS, ROWS)
        rows = position_ref[pl.ds(start, ROWS), :]
        for payload_ref in payload_refs:
            payload_ref[:, piece * width : (piece + 1) * width] = rows
    for d, payload_ref in enumerate(payload_refs):
        values = latents_ref[jnp.bitwise_xor(own_frame, d)]
        high, low = split_parts(values)
        base = pieces * width
        payload_ref[:, base : base + tokens] = high
        payload_ref[:, base + tokens : base + 2 * tokens] = low


def prep(position, latents, frames, share):
    tokens, width = position.shape
    columns = tokens // 2 // ROWS * width + 2 * tokens
    return pl.pallas_call(
        functools.partial(prep_kernel, frames, share),
        out_shape=[jax.ShapeDtypeStruct((ROWS, columns), BF16)] * frames,
        name="prep",
    )(position, latents)


def unpack(block, mine_ref, other_ref, position_scr, latents_scr, width, tokens):
    half = tokens // 2
    pieces = half // ROWS
    core = lax.rem(lax.axis_index("queue"), 2)
    for ref, place in ((mine_ref, core), (other_ref, 1 - core)):
        for piece in range(pieces):
            start = pl.multiple_of(block * tokens + place * half + piece * ROWS, ROWS)
            position_scr[pl.ds(start, ROWS), :] = ref[:, piece * width : (piece + 1) * width]
    base = pieces * width
    latents_scr[block, 0:ROWS, :] = mine_ref[:, base : base + tokens]
    latents_scr[block, ROWS : 2 * ROWS, :] = mine_ref[:, base + tokens : base + 2 * tokens]


def normalize(values, scale, shift):
    center = values - jnp.mean(values, axis=-1, keepdims=True)
    variance = jnp.mean(center * center, axis=-1, keepdims=True)
    return (center * lax.rsqrt(variance + EPSILON) * scale + shift).astype(BF16)


def embed_blocks(blocks, position_scr, latents_scr, embed_ref, mods_ref, normed_scr, hidden_ref):
    tokens = latents_scr.shape[2]
    embed = jnp.concatenate([embed_ref[...], embed_ref[...]], axis=0)
    scale = 1.0 + mods_ref[1:2, :]
    shift = mods_ref[0:1, :]

    def one(block, carry):
        rows = pl.ds(pl.multiple_of(block * tokens, tokens), tokens)
        hidden = dot(latents_scr[block], embed, TN) + position_scr[rows, :].astype(F32)
        if hidden_ref is not None:
            hidden_ref[rows, :] = hidden
        normed_scr[rows, :] = normalize(hidden, scale, shift)
        return carry

    lax.fori_loop(0, blocks, one, 0)


def head_sums(width, head):
    column = lax.broadcasted_iota(jnp.int32, (width, LANES), 0)
    first = lax.broadcasted_iota(jnp.int32, (width, LANES), 1) * head
    return jnp.where((column >= first) & (column < first + head), 1.0, 0.0).astype(BF16)


def head_spread(width, head):
    column = lax.broadcasted_iota(jnp.int32, (LANES, width), 1)
    first = lax.broadcasted_iota(jnp.int32, (LANES, width), 0) * head
    one = jnp.where((column >= first) & (column < first + head), 1.0, 0.0).astype(BF16)
    return jnp.concatenate([one, one], axis=0)


def spread(values, spread_matrix):
    high, low = split_parts(values)
    return dot(jnp.concatenate([high, low], axis=1), spread_matrix)


def head_norm(values, gain, head, sums_matrix, spread_matrix):
    wide = values.astype(F32)
    squares = dot((wide * wide).astype(BF16), sums_matrix) * (1.0 / head)
    factor = spread(lax.rsqrt(squares + EPSILON), spread_matrix)
    return (wide * factor * gain).astype(BF16)


def project(normed_scr, weight_ref, first, last, out_ref, chunk=256):
    for start in range(first, last, chunk):
        end = min(start + chunk, last)
        out_ref[:, start - first : end - first] = dot(
            normed_scr[...], weight_ref[:, start:end]
        ).astype(BF16)


def norm_rows(source, columns, target, gain, head, sums_matrix, spread_matrix, step=128):
    def one(i, carry):
        rows = pl.ds(pl.multiple_of(i * step, step), step)
        target[rows, :] = head_norm(
            source[rows, columns], gain, head, sums_matrix, spread_matrix
        )
        return carry

    lax.fori_loop(0, target.shape[0] // step, one, 0)


def window(first, last, width):
    start = first // LANES * LANES
    end = min(-(-last // LANES) * LANES, width)
    return start, end


def lane_mask(shape, first, last):
    lane = lax.broadcasted_iota(jnp.int32, shape, 1)
    return (lane >= first) & (lane < last)


def keep(values, first, last):
    return jnp.where(lane_mask(values.shape, first, last), values, jnp.zeros_like(values))


def attend_self(q_ref, k_scr, v_ref, v_base, num_ref, sum_ref, head, heads, fresh, q_step):
    queries, width = q_ref.shape
    keys = k_scr.shape[0]

    def tile(i, carry):
        rows = pl.ds(pl.multiple_of(i * q_step, q_step), q_step)
        sums = jnp.zeros((q_step, LANES), F32)
        for h in range(heads):
            first, last = h * head, (h + 1) * head
            start, end = window(first, last, width)
            in_first, in_last = first - start, last - start
            q = keep(q_ref[rows, start:end], in_first, in_last)
            scores = dot(q, k_scr[:, start:end], NT)
            weights = jnp.exp2(scores).astype(BF16)
            v = keep(v_ref[:, v_base + start : v_base + end], in_first, in_last)
            mark = lane_mask((keys, LANES), h, h + 1)
            if end - start == LANES:
                ones = jnp.where(mark, 1.0, 0.0).astype(BF16)
                both = dot(weights, jnp.concatenate([v, ones], axis=1))
                sums = sums + both[:, LANES:]
                num_ref[rows, start:end] += both[:, :LANES]
            else:
                lead = jnp.where(mark, jnp.ones((), BF16), v[:, :LANES])
                both = dot(weights, jnp.concatenate([lead, v[:, LANES:]], axis=1))
                tops = lane_mask((q_step, LANES), 0, heads)
                left = both[:, :LANES]
                sums = sums + jnp.where(tops, left, 0.0)
                num_ref[rows, start : start + LANES] += jnp.where(tops, 0.0, left)
                num_ref[rows, start + LANES : end] += both[:, LANES:]
        sum_ref[rows, :] += sums
        return carry

    lax.fori_loop(0, queries // q_step, tile, 0)


def attend_text(q_ref, tk_scr, tv_scr, num_ref, sum_ref, head, heads, q_step):
    queries, width = q_ref.shape
    keys = tk_scr.shape[0]

    def tile(i, carry):
        rows = pl.ds(pl.multiple_of(i * q_step, q_step), q_step)
        sums = jnp.zeros((q_step, LANES), F32)
        for pair in range(0, heads, 2):
            first, middle, last = pair * head, (pair + 1) * head, (pair + 2) * head
            start, end = window(first, last, width)
            spans = ((first - start, middle - start), (middle - start, last - start))
            k = jnp.concatenate([keep(tk_scr[:, start:end], *span) for span in spans], axis=0)
            v = jnp.concatenate([keep(tv_scr[:, start:end], *span) for span in spans], axis=0)
            ones = jnp.concatenate(
                [
                    jnp.where(lane_mask((keys, LANES), h, h + 1), 1.0, 0.0).astype(BF16)
                    for h in (pair, pair + 1)
                ],
                axis=0,
            )
            weights = jnp.exp2(dot(q_ref[rows, start:end], k, NT)).astype(BF16)
            num_ref[rows, start:end] += dot(weights, v)
            sums = sums + dot(weights, ones)
        sum_ref[rows, :] = sums
        return carry

    lax.fori_loop(0, queries // q_step, tile, 0)


def own_kernel(
    frames, head, heads, *refs
):
    mine = refs[:frames]
    other = refs[frames : 2 * frames]
    (embed_ref, mods_ref, weight_ref, gains_ref, q_ref, hidden_ref, num_ref, sum_ref) = refs[
        2 * frames : 2 * frames + 8
    ]
    position_scr, latents_scr, normed_scr, proj_scr, k_scr = refs[2 * frames + 8 :]
    width = embed_ref.shape[1]
    tokens = latents_scr.shape[2]
    for block in range(frames):
        unpack(block, mine[block], other[block], position_scr, latents_scr, width, tokens)
    embed_blocks(
        frames, position_scr, latents_scr, embed_ref, mods_ref, normed_scr, hidden_ref
    )
    project(normed_scr, weight_ref, 0, 3 * width, proj_scr)
    sums_matrix = head_sums(width, head)
    spread_matrix = head_spread(width, head)
    norm_rows(
        proj_scr, slice(0, width), q_ref, gains_ref[0:1, :], head, sums_matrix, spread_matrix
    )
    norm_rows(
        proj_scr,
        slice(width, 2 * width),
        k_scr,
        gains_ref[1:2, :],
        head,
        sums_matrix,
        spread_matrix,
    )
    num_ref[...] = jnp.zeros_like(num_ref)
    sum_ref[...] = jnp.zeros_like(sum_ref)
    attend_self(q_ref, k_scr, proj_scr, 2 * width, num_ref, sum_ref, head, heads, True, 256)


def rest_kernel(frames, head, heads, columns, *refs):
    count = frames * columns
    mine = refs[:count]
    other = refs[count : 2 * count]
    (
        embed_ref,
        mods_ref,
        weight_ref,
        gains_ref,
        q_ref,
        hidden_ref,
        num_in_ref,
        sum_in_ref,
        text_ref,
        out_weight_ref,
        final_weight_ref,
    ) = refs[2 * count : 2 * count + 11]
    velocity_refs = refs[2 * count + 11 : 2 * count + 11 + frames]
    (
        position_scr,
        latents_scr,
        normed_scr,
        proj_scr,
        k_scr,
        num_ref,
        sum_ref,
        tk_scr,
        tv_scr,
        tnum_scr,
        tsum_scr,
        attention_scr,
    ) = refs[2 * count + 11 + frames :]
    width = embed_ref.shape[1]
    tokens = latents_scr.shape[2]
    sums_matrix = head_sums(width, head)
    spread_matrix = head_spread(width, head)
    num_ref[...] = num_in_ref[...]
    sum_ref[...] = sum_in_ref[...]
    for column in range(columns):
        for block in range(frames):
            index = column * frames + block
            unpack(block, mine[index], other[index], position_scr, latents_scr, width, tokens)
        embed_blocks(frames, position_scr, latents_scr, embed_ref, mods_ref, normed_scr, None)
        project(normed_scr, weight_ref, width, 3 * width, proj_scr)
        norm_rows(
            proj_scr,
            slice(0, width),
            k_scr,
            gains_ref[1:2, :],
            head,
            sums_matrix,
            spread_matrix,
        )
        attend_self(q_ref, k_scr, proj_scr, width, num_ref, sum_ref, head, heads, False, 256)

    shards, _, text_len, part = text_ref.shape
    for shard in range(shards):
        tk_scr[:, shard * part : (shard + 1) * part] = text_ref[shard, 0]
        tv_scr[:, shard * part : (shard + 1) * part] = text_ref[shard, 1]
    norm_rows(
        tk_scr, slice(0, width), tk_scr, gains_ref[1:2, :], head, sums_matrix, spread_matrix
    )
    tnum_scr[...] = jnp.zeros_like(tnum_scr)
    attend_text(q_ref, tk_scr, tv_scr, tnum_scr, tsum_scr, head, heads, 256)

    def mix(i, carry):
        rows = pl.ds(pl.multiple_of(i * LANES, LANES), LANES)
        used = lane_mask((LANES, LANES), 0, heads)
        own = spread(jnp.where(used, 1.0 / sum_ref[rows, :], 0.0), spread_matrix)
        text = spread(jnp.where(used, 1.0 / tsum_scr[rows, :], 0.0), spread_matrix)
        attention_scr[rows, :] = (
            num_ref[rows, :] * own + tnum_scr[rows, :] * text
        ).astype(BF16)
        return carry

    lax.fori_loop(0, q_ref.shape[0] // LANES, mix, 0)
    num_ref[...] = dot(attention_scr[...], out_weight_ref[...])
    gate = mods_ref[2:3, :]
    shift = mods_ref[3:4, :]
    scale = 1.0 + mods_ref[4:5, :]
    for block in range(frames):
        rows = slice(block * tokens, (block + 1) * tokens)
        hidden = hidden_ref[rows, :] + gate * num_ref[rows, :]
        normed = normalize(hidden, scale, shift)
        velocity_refs[block][...] = dot(
            final_weight_ref[...], normed, (((0,), (1,)), ((), ()))
        )


def finish_kernel(
    frames,
    share,
    step_ref,
    levels_ref,
    latents_ref,
    *refs,
):
    arrived = refs[:frames]
    velocity_ref, moved_ref, first_ref = refs[frames:]
    own_frame = lax.div(lax.axis_index("seq"), share)
    for d in range(frames):
        frame = jnp.bitwise_xor(own_frame, d)
        velocity_ref[frame] = arrived[d][...]
    for frame in range(frames):
        index = step_ref[frame]
        size = levels_ref[index + 1] - levels_ref[index]
        updated = latents_ref[frame] + size * velocity_ref[frame]
        if frame == 0:
            first_ref[...] = updated
        else:
            moved_ref[frame - 1] = updated
    moved_ref[frames - 1] = jnp.zeros_like(first_ref)


def vmem(count):
    return [pl.BlockSpec(memory_space=pltpu.VMEM)] * count


def body(
    latents,
    step_index,
    levels,
    modulation,
    embed_weight,
    position,
    qkv_weight,
    q_gain,
    k_gain,
    text_kv,
    out_weight,
    final_weight,
    new_noise,
):
    frames, channels, tokens = latents.shape
    width = embed_weight.shape[1]
    head = q_gain.shape[0]
    heads = width // head
    seq = lax.axis_size("seq")
    queue = lax.axis_size("queue")
    share = seq // frames
    queries = frames * tokens
    own_frame = lax.axis_index("seq") // share

    def over_frames(value, d):
        return lax.ppermute(value, "seq", [(i, i ^ (d * share)) for i in range(seq)])

    def over_columns(value, d):
        return lax.ppermute(value, "seq", [(i, i ^ d) for i in range(seq)])

    def over_cores(value):
        return lax.ppermute(value, "queue", [(i, i ^ 1) for i in range(queue)])

    text = lax.all_gather(text_kv, "seq", axis=0, tiled=False)
    index = lax.dynamic_index_in_dim(step_index, own_frame, 0, keepdims=False)
    mods = lax.dynamic_index_in_dim(modulation, index, 0, keepdims=False)
    factor = math.log2(math.e) / math.sqrt(head)
    gains = jnp.stack([jnp.tile(q_gain * factor, heads), jnp.tile(k_gain, heads)])

    sent = prep(position, latents, frames, share)
    mine = [sent[0]] + [over_frames(sent[d], d) for d in range(1, frames)]
    other = [over_cores(value) for value in mine]
    columns = share - 1
    mine_far = [over_columns(value, d) for d in range(1, share) for value in mine]
    other_far = [over_cores(value) for value in mine_far]

    params = pltpu.CompilerParams(vmem_limit_bytes=VMEM_LIMIT)
    blocks = [
        pltpu.VMEM((queries, width), BF16),
        pltpu.VMEM((frames, 2 * channels, tokens), BF16),
        pltpu.VMEM((queries, width), BF16),
    ]
    q_hat, hidden, num, sums = pl.pallas_call(
        functools.partial(own_kernel, frames, head, heads),
        out_shape=[
            jax.ShapeDtypeStruct((queries, width), BF16),
            jax.ShapeDtypeStruct((queries, width), F32),
            jax.ShapeDtypeStruct((queries, width), F32),
            jax.ShapeDtypeStruct((queries, LANES), F32),
        ],
        in_specs=vmem(2 * frames + 4),
        out_specs=vmem(4),
        scratch_shapes=blocks
        + [pltpu.VMEM((queries, 3 * width), BF16), pltpu.VMEM((queries, width), BF16)],
        compiler_params=params,
        name="own_column",
    )(*mine, *other, embed_weight, mods, qkv_weight, gains)

    text_len = text.shape[2]
    velocities = pl.pallas_call(
        functools.partial(rest_kernel, frames, head, heads, columns),
        out_shape=[jax.ShapeDtypeStruct((channels, tokens), F32)] * frames,
        in_specs=vmem(2 * frames * columns + 11),
        out_specs=vmem(frames),
        scratch_shapes=blocks
        + [
            pltpu.VMEM((queries, 2 * width), BF16),
            pltpu.VMEM((queries, width), BF16),
            pltpu.VMEM((queries, width), F32),
            pltpu.VMEM((queries, LANES), F32),
            pltpu.VMEM((text_len, width), BF16),
            pltpu.VMEM((text_len, width), BF16),
            pltpu.VMEM((queries, width), F32),
            pltpu.VMEM((queries, LANES), F32),
            pltpu.VMEM((queries, width), BF16),
        ],
        compiler_params=params,
        name="rest",
    )(
        *mine_far,
        *other_far,
        embed_weight,
        mods,
        qkv_weight,
        gains,
        q_hat,
        hidden,
        num,
        sums,
        text,
        out_weight,
        final_weight,
    )

    arrived = [velocities[0]] + [over_frames(velocities[d], d) for d in range(1, frames)]
    smem = pl.BlockSpec(memory_space=pltpu.SMEM)
    velocity, moved, first = pl.pallas_call(
        functools.partial(finish_kernel, frames, share),
        out_shape=[
            jax.ShapeDtypeStruct((frames, channels, tokens), F32),
            jax.ShapeDtypeStruct((frames, channels, tokens), F32),
            jax.ShapeDtypeStruct((channels, tokens), F32),
        ],
        in_specs=[smem, smem] + vmem(frames + 1),
        out_specs=vmem(3),
        name="finish",
    )(step_index, levels, latents, *arrived)
    came = lax.ppermute(first, "queue", [(i, i - 1) for i in range(1, queue)])
    at_end = lax.axis_index("queue") == queue - 1
    came = jnp.where(at_end, new_noise, came)
    advanced = lax.dynamic_update_slice_in_dim(moved, came[None], frames - 1, 0)
    return (advanced, velocity)


def solution(mesh):
    in_specs = (
        P("queue", None, "seq"),
        P("queue"),
        P(),
        P(),
        P(),
        P("seq", None),
        P(),
        P(),
        P(),
        P(None, None, "seq"),
        P(),
        P(),
        P(None, "seq"),
    )
    out_specs = (P("queue", None, "seq"), P("queue", None, "seq"))
    return jax.shard_map(body, mesh=mesh, in_specs=in_specs, out_specs=out_specs, check_vma=False)
```

time: 238 us -> 130 us (0.55)
  waiting for transfers between devices: 74.7 us -> 8.36 us
  matrix products: 62.3 us -> 0 us
  Pallas kernels: 0 us -> 54.1 us
  local copies, waits for them, and re-layouts: 54.7 us -> 6.95 us
  blocking collectives: 0 us -> 28.6 us
  other arithmetic: 17.3 us -> 1.87 us
    all_to_all x4 -> x0, waiting for transfers between devices: 72.3 us -> none  [the longest x1 26.5 us: body(): lax.all_to_all(mixture, 'seq', split_axis=0, concat_axis=2, tiled=True)]
    dot_general x15 -> x0, matrix products: 62.3 us -> none  [the longest x2 20.7 us: one_block(): jnp.einsum('fqhe,fkhe->fhqk', query_block, keys_all, preferred_element_ty...]
    pallas_call x0 -> x4, Pallas kernels: none -> 54.1 us  [the longest x1 29.1 us: body(): pl.pallas_call(functools.partial(rest_kernel, frames, head, heads, column...]
    all_gather x0 -> x1, blocking collectives: none -> 28.6 us  [body(): text = lax.all_gather(text_kv, 'seq', axis=0, tiled=False)]
    ppermute x1 -> x19, starting transfers between devices: 4.88 us -> 27.3 us  [the longest x8 12.3 us: over_cores(): return lax.ppermute(value, 'queue', [(i, i ^ 1) for i in range(queue)])]
    all_to_all x4 -> x0, starting transfers between devices: 21.6 us -> none  [the longest x1 6.36 us: body(): lax.all_to_all(keys_raw, 'seq', split_axis=2, concat_axis=1, tiled=True)]
    convert_element_type x6 -> x0, local copies, waits for them, and re-layouts: 18.8 us -> none  [the longest x4 11.4 us: head_norm(): widened = values.astype(jnp.float32)]
    unnamed x34 -> x44, local copies, waits for them, and re-layouts: 12.2 us -> 3.57 us
  transfers between devices with their start and end apart: 5 -> 19, of which waited for: 4 -> 4; matrix products, arithmetic and copies ran while one was open for 17% -> 5% of each run, Pallas kernels for 0% -> 17%
where the time goes in v1:
time: 130 us
  Pallas kernels  54.1 us (42%)
  blocking collectives  28.6 us (22%)
  starting transfers between devices  27.3 us (21%)
  waiting for transfers between devices  8.36 us (6%)
  local copies, waits for them, and re-layouts  6.95 us (5%)
  between operations  2.8 us (2%)
  other arithmetic  1.87 us (1%)
    pallas_call x1, Pallas kernels, body(): pl.pallas_call(functools.partial(rest_kernel, frames, head, heads, column...  29.1 us
    all_gather x1, blocking collectives, body(): text = lax.all_gather(text_kv, 'seq', axis=0, tiled=False)  28.6 us
    pallas_call x1, Pallas kernels, body(): pl.pallas_call(functools.partial(own_kernel, frames, head, heads), out_sh...  21.7 us
    ppermute x8, starting transfers between devices, over_cores(): return lax.ppermute(value, 'queue', [(i, i ^ 1) for i in range(queue)])  12.3 us
    ppermute x6, starting transfers between devices, over_frames(): return lax.ppermute(value, 'seq', [(i, i ^ d * share) for i in range(seq)])  7.16 us
    ppermute x6, waiting for transfers between devices, over_frames(): return lax.ppermute(value, 'seq', [(i, i ^ d * share) for i in range(seq)])  5.68 us
    ppermute x4, starting transfers between devices, over_columns(): return lax.ppermute(value, 'seq', [(i, i ^ d) for i in range(seq)])  4.18 us
    ppermute x1, starting transfers between devices, body(): came = lax.ppermute(first, 'queue', [(i, i - 1) for i in range(1, queue)])  3.68 us
  transfers between devices with their start and end apart: 19, of which 4 were waited for; matrix products, arithmetic and copies ran while one was open for 5% of the time, Pallas kernels for 17%

profile of v1, /device:TPU:1, one launch (start us, length us, event | category | flops | bytes accessed | tf_op | source)
XLA Modules:
  0.0 130.0 jit_solution(4114809455232652527)
XLA Ops:
  0.7 1.9 %prep.1 = (bf16[16,4864]{1,0:T(8,128)(2,1)}, bf16[16,4864]{1,0:T(8,128)(2,1)}, bf16[16,4864]{1,0:T(8,128)(2,1)}, bf16[16,4864]{1,0:T(8,128)(2,1)}) custom-call(bf16[128,1152]{1,0:T(8,128)(2,1)} %position_ref.1, f32[4,16,128]{2,1,0:T(8,128)} %latents_ref.3), custom_call_target="tpu_custom_call" | custom-call | tf_op jit(solution)/shard_map/prep/pallas_call | solution.py:53
  2.6 2.7 %collective-permute-start = (bf16[16,4864]{1,0:T(8,128)(2,1)}, bf16[16,4864]{1,0:T(8,128)(2,1)S(1)}, u32[]{:S(2)}, u32[]{:S(2)}) collective-permute-start(bf16[16,4864]{1,0:T(8,128)(2,1)} %get-tuple-element.17.refs_0_), channel_id=1, source_target_pairs={{0,1},{1,0},{2,3},{3,2},{4,5},{5,4},{6,7},{7,6},{8,9},{9,8},{10,11... | collective-permute-start | bytes 466952 | tf_op jit(solution)/shard_map/ppermute | solution.py:402
  5.3 1.3 collective-permute-start.1
  6.6 2.3 %collective-permute-start.3 = (bf16[16,4864]{1,0:T(8,128)(2,1)}, bf16[16,4864]{1,0:T(8,128)(2,1)S(1)}, u32[]{:S(2)}, u32[]{:S(2)}) collective-permute-start(bf16[16,4864]{1,0:T(8,128)(2,1)} %get-tuple-element.19), channel_id=1, source_target_pairs={{0,4},{1,5},{2,6},{3,7},{4,0},{5,1},{6,2},{7,3},{8,12},{9,13},{10,... | collective-permute-start | bytes 466952 | tf_op jit(solution)/shard_map/ppermute | solution.py:399
  8.9 1.2 dynamic_slice.8
  12.1 0.6 copy.25
  12.7 0.7 broadcast_multiply_fusion
  13.5 0.7 tile.5
  14.3 1.1 collective-permute-start.12
  15.4 4.1 %collective-permute-done.5.refs_3_ = bf16[16,4864]{1,0:T(8,128)(2,1)S(1)} collective-permute-done((bf16[16,4864]{1,0:T(8,128)(2,1)}, bf16[16,4864]{1,0:T(8,128)(2,1)S(1)}, u32[]{:S(2)}, u32[]{:S(2)}) %collective-permute-start.5) | collective-permute-done | bytes 155680 | tf_op jit(solution)/shard_map/ppermute | solution.py:399
  19.6 2.8 %collective-permute-start.13 = (bf16[16,4864]{1,0:T(8,128)(2,1)S(1)}, bf16[16,4864]{1,0:T(8,128)(2,1)S(1)}, u32[]{:S(2)}, u32[]{:S(2)}) collective-permute-start(bf16[16,4864]{1,0:T(8,128)(2,1)S(1)} %collective-permute-done.3.refs_2_), channel_id=1, source_target_pairs={{0,8},{8,0},{16,24},{24,16},{1,9},{9,1},{17,25},{25,17},{2,10},{10... | collective-permute-start | bytes 466952 | tf_op jit(solution)/shard_map/ppermute | solution.py:405
  22.4 1.2 collective-permute-start.4
  23.9 28.6 %all-gather = bf16[16,128,144]{1,2,0:T(8,128)(2,1)S(1)} all-gather(bf16[2,128,144]{1,2,0:T(8,128)(2,1)} %param.22), channel_id=2, replica_groups=mesh['queue'=4,'seq'=8] {'seq'}, dimensions={0}, use_global_device_ids=true | all-gather | bytes 663552 | tf_op jit(solution)/shard_map/all_gather | solution.py:407
  52.5 1.3 copy.21
  53.8 0.9 copy.22.refs_18_
  54.7 7.3 %collective-permute-start.14 = (bf16[16,4864]{1,0:T(8,128)(2,1)S(1)}, bf16[16,4864]{1,0:T(8,128)(2,1)S(1)}, u32[]{:S(2)}, u32[]{:S(2)}) collective-permute-start(bf16[16,4864]{1,0:T(8,128)(2,1)S(1)} %collective-permute-done.5.refs_3_), channel_id=1, source_target_pairs={{0,8},{8,0},{16,24},{24,16},{1,9},{9,1},{17,25},{25,17},{2,10},{10... | collective-permute-start | bytes 466952 | tf_op jit(solution)/shard_map/ppermute | solution.py:405
  63.6 0.6 copy-done.15
  64.3 21.7 %own_column.1 = (bf16[512,1152]{1,0:T(8,128)(2,1)}, f32[512,1152]{1,0:T(8,128)}, f32[512,1152]{1,0:T(8,128)}, f32[512,128]{1,0:T(8,128)}) custom-call(bf16[16,4864]{1,0:T(8,128)(2,1)} %get-tuple-element.17.refs_0_, bf16[16,4864]{1,0:T(8,128)(2,1)} %copy-done.3, bf16[16,4864]{1,0:T(8,128)(2,1)} %copy-done.4, bf16[16,4864]{1,0:T(8,128)(2,1)} %copy-done.5, ...), custom_call_target="tpu_custom_call" | custom-call | tf_op jit(solution)/shard_map/own_column/pallas_call | solution.py:426
  86.9 29.1 %rest.1 = (f32[16,128]{1,0:T(8,128)}, f32[16,128]{1,0:T(8,128)}, f32[16,128]{1,0:T(8,128)}, f32[16,128]{1,0:T(8,128)}) custom-call(bf16[16,4864]{1,0:T(8,128)(2,1)} %copy-done.1, bf16[16,4864]{1,0:T(8,128)(2,1)} %copy-done.6, bf16[16,4864]{1,0:T(8,128)(2,1)} %copy-done.7, bf16[16,4864]{1,0:T(8,128)(2,1)} %copy-done.9, bf16[16,4864]{1,0:T(8,128)(2,1)} %copy-done.11, ...), custom_call_target="tpu_custom_call" | custom-call | tf_op jit(solution)/shard_map/rest/pallas_call | solution.py:443
  116.5 3.0 %collective-permute-start.17 = (f32[16,128]{1,0:T(8,128)}, f32[16,128]{1,0:T(8,128)S(1)}, u32[]{:S(2)}, u32[]{:S(2)}) collective-permute-start(f32[16,128]{1,0:T(8,128)} %get-tuple-element.28), channel_id=1, source_target_pairs={{0,6},{1,7},{2,4},{3,5},{4,2},{5,3},{6,0},{7,1},{8,14},{9,15},{10,... | collective-permute-start | bytes 24584 | tf_op jit(solution)/shard_map/ppermute | solution.py:399
  119.7 1.4 %collective-permute-done.17.refs_3_ = f32[16,128]{1,0:T(8,128)S(1)} collective-permute-done((f32[16,128]{1,0:T(8,128)}, f32[16,128]{1,0:T(8,128)S(1)}, u32[]{:S(2)}, u32[]{:S(2)}) %collective-permute-start.17) | collective-permute-done | bytes 8224 | tf_op jit(solution)/shard_map/ppermute | solution.py:399
  121.6 1.5 %finish.1 = (f32[4,16,128]{2,1,0:T(8,128)}, f32[4,16,128]{2,1,0:T(8,128)}, f32[16,128]{1,0:T(8,128)}) custom-call(s32[4]{0:T(128)} %step_ref.1, f32[31]{0:T(128)} %levels_ref.1, f32[4,16,128]{2,1,0:T(8,128)} %latents_ref.3, f32[16,128]{1,0:T(8,128)} %get-tuple-element.25.refs_0_, f32[16,128]{1,0:T(8,128)} %copy-done.18, f32[16,128]{1,0:T(8,128)} %copy-done.19, ...), custom_call_target="tpu_custom_call" | custom-call | tf_op jit(solution)/shard_map/finish/pallas_call | solution.py:480
  123.1 3.7 %collective-permute-start.18 = (f32[16,128]{1,0:T(8,128)}, f32[16,128]{1,0:T(8,128)S(1)}, u32[]{:S(2)}, u32[]{:S(2)}) collective-permute-start(f32[16,128]{1,0:T(8,128)} %get-tuple-element.30), channel_id=1, source_target_pairs={{8,0},{16,8},{24,16},{9,1},{17,9},{25,17},{10,2},{18,10},{26,18},{... | collective-permute-start | bytes 24584 | tf_op jit(solution)/shard_map/ppermute | solution.py:491
  126.8 2.6 %collective-permute-done.18 = f32[16,128]{1,0:T(8,128)S(1)} collective-permute-done((f32[16,128]{1,0:T(8,128)}, f32[16,128]{1,0:T(8,128)S(1)}, u32[]{:S(2)}, u32[]{:S(2)}) %collective-permute-start.18) | collective-permute-done | bytes 8224 | tf_op jit(solution)/shard_map/ppermute | solution.py:491
  (73 shorter events, 5.0 us)
Async XLA Ops:
  0.6 53.1 %copy-start.16 = (bf16[1152,16]{0,1:T(8,128)(2,1)S(1)}, bf16[1152,16]{0,1:T(8,128)(2,1)}, u32[]{:S(2)}) copy-start(bf16[1152,16]{0,1:T(8,128)(2,1)} %param.24) | copy-start | bytes 110596
  2.6 19.8 %collective-permute-start.11 = (bf16[16,4864]{1,0:T(8,128)(2,1)}, bf16[16,4864]{1,0:T(8,128)(2,1)S(1)}, u32[]{:S(2)}, u32[]{:S(2)}) collective-permute-start(bf16[16,4864]{1,0:T(8,128)(2,1)} %get-tuple-element.17.refs_0_), channel_id=1, source_target_pairs={{0,8},{8,0},{16,24},{24,16},{1,9},{9,1},{17,25},{25,17},{2,10},{10... | collective-permute-start | bytes 466952 | tf_op jit(solution)/shard_map/ppermute | solution.py:405
  2.6 21.0 %collective-permute-start = (bf16[16,4864]{1,0:T(8,128)(2,1)}, bf16[16,4864]{1,0:T(8,128)(2,1)S(1)}, u32[]{:S(2)}, u32[]{:S(2)}) collective-permute-start(bf16[16,4864]{1,0:T(8,128)(2,1)} %get-tuple-element.17.refs_0_), channel_id=1, source_target_pairs={{0,1},{1,0},{2,3},{3,2},{4,5},{5,4},{6,7},{7,6},{8,9},{9,8},{10,11... | collective-permute-start | bytes 466952 | tf_op jit(solution)/shard_map/ppermute | solution.py:402
  5.3 9.0 %collective-permute-start.1 = (bf16[16,4864]{1,0:T(8,128)(2,1)}, bf16[16,4864]{1,0:T(8,128)(2,1)S(1)}, u32[]{:S(2)}, u32[]{:S(2)}) collective-permute-start(bf16[16,4864]{1,0:T(8,128)(2,1)} %get-tuple-element.18), channel_id=1, source_target_pairs={{0,2},{1,3},{2,0},{3,1},{4,6},{5,7},{6,4},{7,5},{8,10},{9,11},{10,... | collective-permute-start | bytes 466952 | tf_op jit(solution)/shard_map/ppermute | solution.py:399
  6.6 8.8 %collective-permute-start.3 = (bf16[16,4864]{1,0:T(8,128)(2,1)}, bf16[16,4864]{1,0:T(8,128)(2,1)S(1)}, u32[]{:S(2)}, u32[]{:S(2)}) collective-permute-start(bf16[16,4864]{1,0:T(8,128)(2,1)} %get-tuple-element.19), channel_id=1, source_target_pairs={{0,4},{1,5},{2,6},{3,7},{4,0},{5,1},{6,2},{7,3},{8,12},{9,13},{10,... | collective-permute-start | bytes 466952 | tf_op jit(solution)/shard_map/ppermute | solution.py:399
  8.9 10.7 %collective-permute-start.5 = (bf16[16,4864]{1,0:T(8,128)(2,1)}, bf16[16,4864]{1,0:T(8,128)(2,1)S(1)}, u32[]{:S(2)}, u32[]{:S(2)}) collective-permute-start(bf16[16,4864]{1,0:T(8,128)(2,1)} %get-tuple-element.20), channel_id=1, source_target_pairs={{0,6},{1,7},{2,4},{3,5},{4,2},{5,3},{6,0},{7,1},{8,14},{9,15},{10,... | collective-permute-start | bytes 466952 | tf_op jit(solution)/shard_map/ppermute | solution.py:399
  14.3 49.3 %copy-start.3 = (bf16[16,4864]{1,0:T(8,128)(2,1)}, bf16[16,4864]{1,0:T(8,128)(2,1)S(1)}, u32[]{:S(2)}) copy-start(bf16[16,4864]{1,0:T(8,128)(2,1)S(1)} %collective-permute-done.1.refs_1_) | copy-start | bytes 466948
  14.3 40.4 %collective-permute-start.12 = (bf16[16,4864]{1,0:T(8,128)(2,1)S(1)}, bf16[16,4864]{1,0:T(8,128)(2,1)S(1)}, u32[]{:S(2)}, u32[]{:S(2)}) collective-permute-start(bf16[16,4864]{1,0:T(8,128)(2,1)S(1)} %collective-permute-done.1.refs_1_), channel_id=1, source_target_pairs={{0,8},{8,0},{16,24},{24,16},{1,9},{9,1},{17,25},{25,17},{2,10},{10... | collective-permute-start | bytes 466952 | tf_op jit(solution)/shard_map/ppermute | solution.py:405
  15.4 48.2 %copy-start.4 = (bf16[16,4864]{1,0:T(8,128)(2,1)}, bf16[16,4864]{1,0:T(8,128)(2,1)S(1)}, u32[]{:S(2)}) copy-start(bf16[16,4864]{1,0:T(8,128)(2,1)S(1)} %collective-permute-done.3.refs_2_) | copy-start | bytes 466948
  15.4 47.1 %collective-permute-start.2 = (bf16[16,4864]{1,0:T(8,128)(2,1)S(1)}, bf16[16,4864]{1,0:T(8,128)(2,1)S(1)}, u32[]{:S(2)}, u32[]{:S(2)}) collective-permute-start(bf16[16,4864]{1,0:T(8,128)(2,1)S(1)} %collective-permute-done.1.refs_1_), channel_id=1, source_target_pairs={{0,1},{1,0},{2,3},{3,2},{4,5},{5,4},{6,7},{7,6},{8,9},{9,8},{10,11... | collective-permute-start | bytes 466952 | tf_op jit(solution)/shard_map/ppermute | solution.py:402
  19.6 44.0 %copy-start.5 = (bf16[16,4864]{1,0:T(8,128)(2,1)}, bf16[16,4864]{1,0:T(8,128)(2,1)S(1)}, u32[]{:S(2)}) copy-start(bf16[16,4864]{1,0:T(8,128)(2,1)S(1)} %collective-permute-done.5.refs_3_) | copy-start | bytes 466948
  19.6 42.3 %collective-permute-start.13 = (bf16[16,4864]{1,0:T(8,128)(2,1)S(1)}, bf16[16,4864]{1,0:T(8,128)(2,1)S(1)}, u32[]{:S(2)}, u32[]{:S(2)}) collective-permute-start(bf16[16,4864]{1,0:T(8,128)(2,1)S(1)} %collective-permute-done.3.refs_2_), channel_id=1, source_target_pairs={{0,8},{8,0},{16,24},{24,16},{1,9},{9,1},{17,25},{25,17},{2,10},{10... | collective-permute-start | bytes 466952 | tf_op jit(solution)/shard_map/ppermute | solution.py:405
  22.4 40.2 %collective-permute-start.4 = (bf16[16,4864]{1,0:T(8,128)(2,1)S(1)}, bf16[16,4864]{1,0:T(8,128)(2,1)S(1)}, u32[]{:S(2)}, u32[]{:S(2)}) collective-permute-start(bf16[16,4864]{1,0:T(8,128)(2,1)S(1)} %collective-permute-done.3.refs_2_), channel_id=1, source_target_pairs={{0,1},{1,0},{2,3},{3,2},{4,5},{5,4},{6,7},{7,6},{8,9},{9,8},{10,11... | collective-permute-start | bytes 466952 | tf_op jit(solution)/shard_map/ppermute | solution.py:402
  23.6 62.4 %copy-start.1 = (bf16[16,4864]{1,0:T(8,128)(2,1)}, bf16[16,4864]{1,0:T(8,128)(2,1)S(1)}, u32[]{:S(2)}) copy-start(bf16[16,4864]{1,0:T(8,128)(2,1)S(1)} %collective-permute-done.refs_0_) | copy-start | bytes 466948
  23.6 38.4 %collective-permute-start.6 = (bf16[16,4864]{1,0:T(8,128)(2,1)S(1)}, bf16[16,4864]{1,0:T(8,128)(2,1)S(1)}, u32[]{:S(2)}, u32[]{:S(2)}) collective-permute-start(bf16[16,4864]{1,0:T(8,128)(2,1)S(1)} %collective-permute-done.5.refs_3_), channel_id=1, source_target_pairs={{0,1},{1,0},{2,3},{3,2},{4,5},{5,4},{6,7},{7,6},{8,9},{9,8},{10,11... | collective-permute-start | bytes 466952 | tf_op jit(solution)/shard_map/ppermute | solution.py:402
  54.7 8.9 %collective-permute-start.14 = (bf16[16,4864]{1,0:T(8,128)(2,1)S(1)}, bf16[16,4864]{1,0:T(8,128)(2,1)S(1)}, u32[]{:S(2)}, u32[]{:S(2)}) collective-permute-start(bf16[16,4864]{1,0:T(8,128)(2,1)S(1)} %collective-permute-done.5.refs_3_), channel_id=1, source_target_pairs={{0,8},{8,0},{16,24},{24,16},{1,9},{9,1},{17,25},{25,17},{2,10},{10... | collective-permute-start | bytes 466952 | tf_op jit(solution)/shard_map/ppermute | solution.py:405
  61.9 24.1 %collective-permute-start.7 = (bf16[16,4864]{1,0:T(8,128)(2,1)S(1)}, bf16[16,4864]{1,0:T(8,128)(2,1)S(1)}, u32[]{:S(2)}, u32[]{:S(2)}) collective-permute-start(bf16[16,4864]{1,0:T(8,128)(2,1)S(1)} %collective-permute-done.refs_0_), channel_id=1, source_target_pairs={{0,8},{8,0},{16,24},{24,16},{1,9},{9,1},{17,25},{25,17},{2,10},{10... | collective-permute-start | bytes 466952 | tf_op jit(solution)/shard_map/ppermute | solution.py:405
  62.0 24.0 %collective-permute-start.10 = (bf16[16,4864]{1,0:T(8,128)(2,1)S(1)}, bf16[16,4864]{1,0:T(8,128)(2,1)S(1)}, u32[]{:S(2)}, u32[]{:S(2)}) collective-permute-start(bf16[16,4864]{1,0:T(8,128)(2,1)S(1)} %collective-permute-done.6.refs_3_), channel_id=1, source_target_pairs={{0,8},{8,0},{16,24},{24,16},{1,9},{9,1},{17,25},{25,17},{2,10},{10... | collective-permute-start | bytes 466952 | tf_op jit(solution)/shard_map/ppermute | solution.py:405
  62.5 23.6 %collective-permute-start.8 = (bf16[16,4864]{1,0:T(8,128)(2,1)S(1)}, bf16[16,4864]{1,0:T(8,128)(2,1)S(1)}, u32[]{:S(2)}, u32[]{:S(2)}) collective-permute-start(bf16[16,4864]{1,0:T(8,128)(2,1)S(1)} %collective-permute-done.2.refs_1_), channel_id=1, source_target_pairs={{0,8},{8,0},{16,24},{24,16},{1,9},{9,1},{17,25},{25,17},{2,10},{10... | collective-permute-start | bytes 466952 | tf_op jit(solution)/shard_map/ppermute | solution.py:405
  62.6 23.5 %collective-permute-start.9 = (bf16[16,4864]{1,0:T(8,128)(2,1)S(1)}, bf16[16,4864]{1,0:T(8,128)(2,1)S(1)}, u32[]{:S(2)}, u32[]{:S(2)}) collective-permute-start(bf16[16,4864]{1,0:T(8,128)(2,1)S(1)} %collective-permute-done.4.refs_2_), channel_id=1, source_target_pairs={{0,8},{8,0},{16,24},{24,16},{1,9},{9,1},{17,25},{25,17},{2,10},{10... | collective-permute-start | bytes 466952 | tf_op jit(solution)/shard_map/ppermute | solution.py:405
  116.0 3.6 %collective-permute-start.15 = (f32[16,128]{1,0:T(8,128)}, f32[16,128]{1,0:T(8,128)S(1)}, u32[]{:S(2)}, u32[]{:S(2)}) collective-permute-start(f32[16,128]{1,0:T(8,128)} %get-tuple-element.26), channel_id=1, source_target_pairs={{0,2},{1,3},{2,0},{3,1},{4,6},{5,7},{6,4},{7,5},{8,10},{9,11},{10,... | collective-permute-start | bytes 24584 | tf_op jit(solution)/shard_map/ppermute | solution.py:399
  116.0 3.7 %collective-permute-start.16 = (f32[16,128]{1,0:T(8,128)}, f32[16,128]{1,0:T(8,128)S(1)}, u32[]{:S(2)}, u32[]{:S(2)}) collective-permute-start(f32[16,128]{1,0:T(8,128)} %get-tuple-element.27), channel_id=1, source_target_pairs={{0,4},{1,5},{2,6},{3,7},{4,0},{5,1},{6,2},{7,3},{8,12},{9,13},{10,... | collective-permute-start | bytes 24584 | tf_op jit(solution)/shard_map/ppermute | solution.py:399
  116.5 4.5 %collective-permute-start.17 = (f32[16,128]{1,0:T(8,128)}, f32[16,128]{1,0:T(8,128)S(1)}, u32[]{:S(2)}, u32[]{:S(2)}) collective-permute-start(f32[16,128]{1,0:T(8,128)} %get-tuple-element.28), channel_id=1, source_target_pairs={{0,6},{1,7},{2,4},{3,5},{4,2},{5,3},{6,0},{7,1},{8,14},{9,15},{10,... | collective-permute-start | bytes 24584 | tf_op jit(solution)/shard_map/ppermute | solution.py:399
  123.1 6.3 %collective-permute-start.18 = (f32[16,128]{1,0:T(8,128)}, f32[16,128]{1,0:T(8,128)S(1)}, u32[]{:S(2)}, u32[]{:S(2)}) collective-permute-start(f32[16,128]{1,0:T(8,128)} %get-tuple-element.30), channel_id=1, source_target_pairs={{8,0},{16,8},{24,16},{9,1},{17,9},{25,17},{10,2},{18,10},{26,18},{... | collective-permute-start | bytes 24584 | tf_op jit(solution)/shard_map/ppermute | solution.py:491
  (16 other events, 183.9 us)

commit v2 on v1

--- a/solution.py
+++ b/solution.py
@@ -13,7 +13,7 @@
 ROWS = 16
 F32 = jnp.float32
 BF16 = jnp.bfloat16
-VMEM_LIMIT = 56 * 1024 * 1024
+VMEM_LIMIT = 32 * 1024 * 1024
 NT = (((1,), (1,)), ((), ()))
 TN = (((0,), (0,)), ((), ()))
 
@@ -28,8 +28,9 @@
     return high, low
 
 
-def prep_kernel(frames, share, position_ref, latents_ref, *payload_refs):
+def prep_kernel(frames, share, position_ref, latents_ref, text_ref, *payload_refs):
     tokens, width = position_ref.shape
+    _, text_len, part = text_ref.shape
     half = tokens // 2
     pieces = half // ROWS
     core = lax.rem(lax.axis_index("queue"), 2)
@@ -45,16 +46,22 @@
         base = pieces * width
         payload_ref[:, base : base + tokens] = high
         payload_ref[:, base + tokens : base + 2 * tokens] = low
-
-
-def prep(position, latents, frames, share):
+    base = pieces * width + 2 * tokens
+    for piece in range(text_len // ROWS):
+        rows = text_ref[core, piece * ROWS : (piece + 1) * ROWS, :]
+        for payload_ref in payload_refs:
+            payload_ref[:, base + piece * part : base + (piece + 1) * part] = rows
+
+
+def prep(position, latents, text_kv, frames, share):
     tokens, width = position.shape
-    columns = tokens // 2 // ROWS * width + 2 * tokens
+    _, text_len, part = text_kv.shape
+    columns = tokens // 2 // ROWS * width + 2 * tokens + text_len // ROWS * part
     return pl.pallas_call(
         functools.partial(prep_kernel, frames, share),
         out_shape=[jax.ShapeDtypeStruct((ROWS, columns), BF16)] * frames,
         name="prep",
-    )(position, latents)
+    )(position, latents, text_kv)
 
 
 def unpack(block, mine_ref, other_ref, position_scr, latents_scr, width, tokens):
@@ -70,6 +77,25 @@
     latents_scr[block, ROWS : 2 * ROWS, :] = mine_ref[:, base + tokens : base + 2 * tokens]
 
 
+def unpack_text(shard, mine_ref, other_ref, base, part, text_scr):
+    _, text_len, padded = text_scr.shape
+    core = lax.rem(lax.axis_index("queue"), 2)
+    first = shard * part
+    start = pl.multiple_of(lax.div(first, LANES) * LANES, LANES)
+    for ref, place in ((mine_ref, core), (other_ref, 1 - core)):
+        rows = jnp.concatenate(
+            [
+                ref[:, base + piece * part : base + (piece + 1) * part]
+                for piece in range(text_len // ROWS)
+            ],
+            axis=0,
+        ).astype(F32)
+        space = -(-(part + LANES) // LANES) * LANES
+        wide = jnp.concatenate([rows, jnp.zeros((text_len, space - part), F32)], axis=1)
+        moved = pltpu.roll(wide, first - start, 1).astype(BF16)
+        text_scr[place, :, pl.ds(start, space)] += moved
+
+
 def normalize(values, scale, shift):
     center = values - jnp.mean(values, axis=-1, keepdims=True)
     variance = jnp.mean(center * center, axis=-1, keepdims=True)
@@ -90,7 +116,7 @@
         normed_scr[rows, :] = normalize(hidden, scale, shift)
         return carry
 
-    lax.fori_loop(0, blocks, one, 0)
+    lax.fori_loop(0, blocks, one, 0, unroll=True)
 
 
 def head_sums(width, head):
@@ -134,7 +160,7 @@
         )
         return carry
 
-    lax.fori_loop(0, target.shape[0] // step, one, 0)
+    lax.fori_loop(0, target.shape[0] // step, one, 0, unroll=True)
 
 
 def window(first, last, width):
@@ -184,7 +210,7 @@
         sum_ref[rows, :] += sums
         return carry
 
-    lax.fori_loop(0, queries // q_step, tile, 0)
+    lax.fori_loop(0, queries // q_step, tile, 0, unroll=True)
 
 
 def attend_text(q_ref, tk_scr, tv_scr, num_ref, sum_ref, head, heads, q_step):
@@ -213,7 +239,7 @@
         sum_ref[rows, :] = sums
         return carry
 
-    lax.fori_loop(0, queries // q_step, tile, 0)
+    lax.fori_loop(0, queries // q_step, tile, 0, unroll=True)
 
 
 def own_kernel(
@@ -252,8 +278,8 @@
     attend_self(q_ref, k_scr, proj_scr, 2 * width, num_ref, sum_ref, head, heads, True, 256)
 
 
-def rest_kernel(frames, head, heads, columns, *refs):
-    count = frames * columns
+def rest_kernel(frames, head, heads, columns, part, *refs):
+    count = frames * (columns + 1)
     mine = refs[:count]
     other = refs[count : 2 * count]
     (
@@ -265,11 +291,10 @@
         hidden_ref,
         num_in_ref,
         sum_in_ref,
-        text_ref,
         out_weight_ref,
         final_weight_ref,
-    ) = refs[2 * count : 2 * count + 11]
-    velocity_refs = refs[2 * count + 11 : 2 * count + 11 + frames]
+    ) = refs[2 * count : 2 * count + 10]
+    velocity_refs = refs[2 * count + 10 : 2 * count + 10 + frames]
     (
         position_scr,
         latents_scr,
@@ -278,12 +303,12 @@
         k_scr,
         num_ref,
         sum_ref,
+        text_scr,
         tk_scr,
-        tv_scr,
         tnum_scr,
         tsum_scr,
         attention_scr,
-    ) = refs[2 * count + 11 + frames :]
+    ) = refs[2 * count + 10 + frames :]
     width = embed_ref.shape[1]
     tokens = latents_scr.shape[2]
     sums_matrix = head_sums(width, head)
@@ -292,7 +317,7 @@
     sum_ref[...] = sum_in_ref[...]
     for column in range(columns):
         for block in range(frames):
-            index = column * frames + block
+            index = (column + 1) * frames + block
             unpack(block, mine[index], other[index], position_scr, latents_scr, width, tokens)
         embed_blocks(frames, position_scr, latents_scr, embed_ref, mods_ref, normed_scr, None)
         project(normed_scr, weight_ref, width, 3 * width, proj_scr)
@@ -307,15 +332,25 @@
         )
         attend_self(q_ref, k_scr, proj_scr, width, num_ref, sum_ref, head, heads, False, 256)
 
-    shards, _, text_len, part = text_ref.shape
-    for shard in range(shards):
-        tk_scr[:, shard * part : (shard + 1) * part] = text_ref[shard, 0]
-        tv_scr[:, shard * part : (shard + 1) * part] = text_ref[shard, 1]
+    text_scr[...] = jnp.zeros_like(text_scr)
+    base = tokens // 2 // ROWS * width + 2 * tokens
+    place = lax.axis_index("seq")
+    for column in range(columns + 1):
+        for block in range(frames):
+            shard = jnp.bitwise_xor(place, block * (columns + 1) + column)
+            index = column * frames + block
+            unpack_text(shard, mine[index], other[index], base, part, text_scr)
     norm_rows(
-        tk_scr, slice(0, width), tk_scr, gains_ref[1:2, :], head, sums_matrix, spread_matrix
+        text_scr.at[0],
+        slice(0, width),
+        tk_scr,
+        gains_ref[1:2, :],
+        head,
+        sums_matrix,
+        spread_matrix,
     )
     tnum_scr[...] = jnp.zeros_like(tnum_scr)
-    attend_text(q_ref, tk_scr, tv_scr, tnum_scr, tsum_scr, head, heads, 256)
+    attend_text(q_ref, tk_scr, text_scr.at[1], tnum_scr, tsum_scr, head, heads, 256)
 
     def mix(i, carry):
         rows = pl.ds(pl.multiple_of(i * LANES, LANES), LANES)
@@ -404,13 +439,14 @@
     def over_cores(value):
         return lax.ppermute(value, "queue", [(i, i ^ 1) for i in range(queue)])
 
-    text = lax.all_gather(text_kv, "seq", axis=0, tiled=False)
     index = lax.dynamic_index_in_dim(step_index, own_frame, 0, keepdims=False)
     mods = lax.dynamic_index_in_dim(modulation, index, 0, keepdims=False)
     factor = math.log2(math.e) / math.sqrt(head)
     gains = jnp.stack([jnp.tile(q_gain * factor, heads), jnp.tile(k_gain, heads)])
 
-    sent = prep(position, latents, frames, share)
+    near = functools.partial(pltpu.with_memory_space_constraint, memory_space=pltpu.VMEM)
+    qkv_weight, out_weight = near(qkv_weight), near(out_weight)
+    sent = prep(position, latents, text_kv, frames, share)
     mine = [sent[0]] + [over_frames(sent[d], d) for d in range(1, frames)]
     other = [over_cores(value) for value in mine]
     columns = share - 1
@@ -426,10 +462,10 @@
     q_hat, hidden, num, sums = pl.pallas_call(
         functools.partial(own_kernel, frames, head, heads),
         out_shape=[
-            jax.ShapeDtypeStruct((queries, width), BF16),
-            jax.ShapeDtypeStruct((queries, width), F32),
-            jax.ShapeDtypeStruct((queries, width), F32),
-            jax.ShapeDtypeStruct((queries, LANES), F32),
+            pltpu.VMEM((queries, width), BF16),
+            pltpu.VMEM((queries, width), F32),
+            pltpu.VMEM((queries, width), F32),
+            pltpu.VMEM((queries, LANES), F32),
         ],
         in_specs=vmem(2 * frames + 4),
         out_specs=vmem(4),
@@ -439,11 +475,11 @@
         name="own_column",
     )(*mine, *other, embed_weight, mods, qkv_weight, gains)
 
-    text_len = text.shape[2]
+    text_len = text_kv.shape[1]
     velocities = pl.pallas_call(
-        functools.partial(rest_kernel, frames, head, heads, columns),
+        functools.partial(rest_kernel, frames, head, heads, columns, text_kv.shape[2]),
         out_shape=[jax.ShapeDtypeStruct((channels, tokens), F32)] * frames,
-        in_specs=vmem(2 * frames * columns + 11),
+        in_specs=vmem(2 * frames * share + 10),
         out_specs=vmem(frames),
         scratch_shapes=blocks
         + [
@@ -451,7 +487,7 @@
             pltpu.VMEM((queries, width), BF16),
             pltpu.VMEM((queries, width), F32),
             pltpu.VMEM((queries, LANES), F32),
-            pltpu.VMEM((text_len, width), BF16),
+            pltpu.VMEM((2, text_len, width + 2 * LANES), BF16),
             pltpu.VMEM((text_len, width), BF16),
             pltpu.VMEM((queries, width), F32),
             pltpu.VMEM((queries, LANES), F32),
@@ -460,7 +496,9 @@
         compiler_params=params,
         name="rest",
     )(
+        *mine,
         *mine_far,
+        *other,
         *other_far,
         embed_weight,
         mods,
@@ -470,7 +508,6 @@
         hidden,
         num,
         sums,
-        text,
         out_weight,
         final_weight,
     )

time: 130 us -> 94 us (0.72)
  blocking collectives: 28.6 us -> 0 us
  Pallas kernels: 54.1 us -> 35.7 us
  waiting for transfers between devices: 8.36 us -> 13.1 us
  local copies, waits for them, and re-layouts: 6.95 us -> 11 us
  starting transfers between devices: 27.3 us -> 29.7 us
    all_gather x1 -> x0, blocking collectives: 28.6 us -> none  [body(): text = lax.all_gather(text_kv, 'seq', axis=0, tiled=False)]
    pallas_call x1, Pallas kernels: 29.1 us -> 19 us  [body(): pl.pallas_call(functools.partial(rest_kernel, frames, head, heads, column...]
    pallas_call x1, Pallas kernels: 21.7 us -> 13.2 us  [body(): pl.pallas_call(functools.partial(own_kernel, frames, head, heads), out_sh...]
    unnamed x44 -> x23, local copies, waits for them, and re-layouts: 3.57 us -> 8.88 us
    ppermute x6, waiting for transfers between devices: 5.68 us -> 10.4 us  [over_frames(): return lax.ppermute(value, 'seq', [(i, i ^ d * share) for i in range(seq)])]
    ppermute x8, starting transfers between devices: 12.3 us -> 14.8 us  [over_cores(): return lax.ppermute(value, 'queue', [(i, i ^ 1) for i in range(queue)])]
  transfers between devices with their start and end apart: 19 -> 19, of which waited for: 4 -> 5; matrix products, arithmetic and copies ran while one was open for 5% -> 4% of each run, Pallas kernels for 17% -> 14%
where the time goes in v2:
time: 94 us; the launch traced here: 93.5 us
  Pallas kernels  35.7 us (38%)
  starting transfers between devices  29.7 us (32%)
  waiting for transfers between devices  13.1 us (14%)
  local copies, waits for them, and re-layouts  11 us (12%)
  between operations  2.73 us (3%)
  other arithmetic  1.27 us (1%)
    pallas_call x1, Pallas kernels, body(): pl.pallas_call(functools.partial(rest_kernel, frames, head, heads, column...  19 us
    ppermute x8, starting transfers between devices, over_cores(): return lax.ppermute(value, 'queue', [(i, i ^ 1) for i in range(queue)])  14.8 us
    pallas_call x1, Pallas kernels, body(): pl.pallas_call(functools.partial(own_kernel, frames, head, heads), out_sh...  13.2 us
    ppermute x6, waiting for transfers between devices, over_frames(): return lax.ppermute(value, 'seq', [(i, i ^ d * share) for i in range(seq)])  10.4 us
    unnamed x23, local copies, waits for them, and re-layouts  8.88 us
    ppermute x6, starting transfers between devices, over_frames(): return lax.ppermute(value, 'seq', [(i, i ^ d * share) for i in range(seq)])  7.15 us
    ppermute x4, starting transfers between devices, over_columns(): return lax.ppermute(value, 'seq', [(i, i ^ d) for i in range(seq)])  4.21 us
    ppermute x1, starting transfers between devices, body(): came = lax.ppermute(first, 'queue', [(i, i - 1) for i in range(1, queue)])  3.6 us
  transfers between devices with their start and end apart: 19, of which 5 were waited for; matrix products, arithmetic and copies ran while one was open for 4% of the time, Pallas kernels for 14%

profile of v2, /device:TPU:1, one launch (start us, length us, event | category | flops | bytes accessed | tf_op | source)
XLA Modules:
  0.0 93.5 jit_solution(12355148275050051373)
XLA Ops:
  0.6 1.7 %copy.17.text_ref = bf16[2,128,144]{2,1,0:T(8,128)(2,1)} copy(bf16[2,128,144]{1,2,0:T(8,128)(2,1)} %param.22) | data formatting | bytes 147456 | tf_op args[9]
  2.4 2.0 %prep.1 = (bf16[16,6016]{1,0:T(8,128)(2,1)}, bf16[16,6016]{1,0:T(8,128)(2,1)}, bf16[16,6016]{1,0:T(8,128)(2,1)}, bf16[16,6016]{1,0:T(8,128)(2,1)}) custom-call(bf16[128,1152]{1,0:T(8,128)(2,1)} %position_ref.1, f32[4,16,128]{2,1,0:T(8,128)} %latents_ref.3, bf16[2,128,144]{2,1,0:T(8,128)(2,1)} %copy.17.text_ref), custom_call_target="tpu_custom_call" | custom-call | tf_op jit(solution)/shard_map/prep/pallas_call | solution.py:60
  4.4 2.7 %collective-permute-start.3 = (bf16[16,6016]{1,0:T(8,128)(2,1)}, bf16[16,6016]{1,0:T(8,128)(2,1)S(1)}, u32[]{:S(2)}, u32[]{:S(2)}) collective-permute-start(bf16[16,6016]{1,0:T(8,128)(2,1)} %get-tuple-element.17.refs_0_), channel_id=1, source_target_pairs={{0,1},{1,0},{2,3},{3,2},{4,5},{5,4},{6,7},{7,6},{8,9},{9,8},{10,11... | collective-permute-start | bytes 577544 | tf_op jit(solution)/shard_map/ppermute | solution.py:437
  7.1 1.3 %collective-permute-start = (bf16[16,6016]{1,0:T(8,128)(2,1)}, bf16[16,6016]{1,0:T(8,128)(2,1)S(1)}, u32[]{:S(2)}, u32[]{:S(2)}) collective-permute-start(bf16[16,6016]{1,0:T(8,128)(2,1)} %get-tuple-element.18), channel_id=1, source_target_pairs={{0,2},{1,3},{2,0},{3,1},{4,6},{5,7},{6,4},{7,5},{8,10},{9,11},{10,... | collective-permute-start | bytes 577544 | tf_op jit(solution)/shard_map/ppermute | solution.py:434
  8.4 2.3 %collective-permute-start.1 = (bf16[16,6016]{1,0:T(8,128)(2,1)}, bf16[16,6016]{1,0:T(8,128)(2,1)S(1)}, u32[]{:S(2)}, u32[]{:S(2)}) collective-permute-start(bf16[16,6016]{1,0:T(8,128)(2,1)} %get-tuple-element.19), channel_id=1, source_target_pairs={{0,4},{1,5},{2,6},{3,7},{4,0},{5,1},{6,2},{7,3},{8,12},{9,13},{10,... | collective-permute-start | bytes 577544 | tf_op jit(solution)/shard_map/ppermute | solution.py:434
  10.7 1.2 %dynamic_slice.8 = s32[1]{0:T(128)} dynamic-slice(s32[4]{0:T(128)} %step_ref.1, s32[]{:T(128)S(6)} %select_n.22), dynamic_slice_sizes={1} | dynamic-slice | bytes 12 | tf_op jit(solution)/shard_map/jit(dynamic_index_in_dim)/dynamic_slice | solution.py:442
  15.4 1.6 %collective-permute-done.refs_1_ = bf16[16,6016]{1,0:T(8,128)(2,1)S(1)} collective-permute-done((bf16[16,6016]{1,0:T(8,128)(2,1)}, bf16[16,6016]{1,0:T(8,128)(2,1)S(1)}, u32[]{:S(2)}, u32[]{:S(2)}) %collective-permute-start) | collective-permute-done | bytes 192544 | tf_op jit(solution)/shard_map/ppermute | solution.py:434
  17.0 1.1 %collective-permute-start.8 = (bf16[16,6016]{1,0:T(8,128)(2,1)S(1)}, bf16[16,6016]{1,0:T(8,128)(2,1)S(1)}, u32[]{:S(2)}, u32[]{:S(2)}) collective-permute-start(bf16[16,6016]{1,0:T(8,128)(2,1)S(1)} %collective-permute-done.refs_1_), channel_id=1, source_target_pairs={{0,8},{8,0},{16,24},{24,16},{1,9},{9,1},{17,25},{25,17},{2,10},{10... | collective-permute-start | bytes 577544 | tf_op jit(solution)/shard_map/ppermute | solution.py:440
  18.2 5.6 %collective-permute-done.2.refs_3_ = bf16[16,6016]{1,0:T(8,128)(2,1)S(1)} collective-permute-done((bf16[16,6016]{1,0:T(8,128)(2,1)}, bf16[16,6016]{1,0:T(8,128)(2,1)S(1)}, u32[]{:S(2)}, u32[]{:S(2)}) %collective-permute-start.2) | collective-permute-done | bytes 192544 | tf_op jit(solution)/shard_map/ppermute | solution.py:434
  23.8 2.8 %collective-permute-start.9 = (bf16[16,6016]{1,0:T(8,128)(2,1)S(1)}, bf16[16,6016]{1,0:T(8,128)(2,1)S(1)}, u32[]{:S(2)}, u32[]{:S(2)}) collective-permute-start(bf16[16,6016]{1,0:T(8,128)(2,1)S(1)} %collective-permute-done.1.refs_2_), channel_id=1, source_target_pairs={{0,8},{8,0},{16,24},{24,16},{1,9},{9,1},{17,25},{25,17},{2,10},{10... | collective-permute-start | bytes 577544 | tf_op jit(solution)/shard_map/ppermute | solution.py:440
  26.5 1.2 %collective-permute-start.5 = (bf16[16,6016]{1,0:T(8,128)(2,1)S(1)}, bf16[16,6016]{1,0:T(8,128)(2,1)S(1)}, u32[]{:S(2)}, u32[]{:S(2)}) collective-permute-start(bf16[16,6016]{1,0:T(8,128)(2,1)S(1)} %collective-permute-done.1.refs_2_), channel_id=1, source_target_pairs={{0,1},{1,0},{2,3},{3,2},{4,5},{5,4},{6,7},{7,6},{8,9},{9,8},{10,11... | collective-permute-start | bytes 577544 | tf_op jit(solution)/shard_map/ppermute | solution.py:437
  28.1 1.0 %copy.19.refs_25_ = bf16[1152,16]{1,0:T(8,128)(2,1)S(1)} copy(bf16[1152,16]{0,1:T(8,128)(2,1)} %param.24) | data formatting | bytes 73728 | tf_op args[11]
  29.7 3.9 %collective-permute-start.11 = (bf16[16,6016]{1,0:T(8,128)(2,1)S(1)}, bf16[16,6016]{1,0:T(8,128)(2,1)S(1)}, u32[]{:S(2)}, u32[]{:S(2)}) collective-permute-start(bf16[16,6016]{1,0:T(8,128)(2,1)S(1)} %collective-permute-done.3.refs_4_), channel_id=1, source_target_pairs={{0,8},{8,0},{16,24},{24,16},{1,9},{9,1},{17,25},{25,17},{2,10},{10... | collective-permute-start | bytes 577544 | tf_op jit(solution)/shard_map/ppermute | solution.py:440
  33.6 4.1 %collective-permute-start.13 = (bf16[16,6016]{1,0:T(8,128)(2,1)S(1)}, bf16[16,6016]{1,0:T(8,128)(2,1)S(1)}, u32[]{:S(2)}, u32[]{:S(2)}) collective-permute-start(bf16[16,6016]{1,0:T(8,128)(2,1)S(1)} %collective-permute-done.5.refs_6_), channel_id=1, source_target_pairs={{0,8},{8,0},{16,24},{24,16},{1,9},{9,1},{17,25},{25,17},{2,10},{10... | collective-permute-start | bytes 577544 | tf_op jit(solution)/shard_map/ppermute | solution.py:440
  37.7 2.1 %collective-permute-start.14 = (bf16[16,6016]{1,0:T(8,128)(2,1)S(1)}, bf16[16,6016]{1,0:T(8,128)(2,1)S(1)}, u32[]{:S(2)}, u32[]{:S(2)}) collective-permute-start(bf16[16,6016]{1,0:T(8,128)(2,1)S(1)} %collective-permute-done.6.refs_7_), channel_id=1, source_target_pairs={{0,8},{8,0},{16,24},{24,16},{1,9},{9,1},{17,25},{25,17},{2,10},{10... | collective-permute-start | bytes 577544 | tf_op jit(solution)/shard_map/ppermute | solution.py:440
  39.9 3.3 %copy-done.1 = bf16[1152,3456]{1,0:T(8,128)(2,1)S(1)} copy-done((bf16[1152,3456]{1,0:T(8,128)(2,1)S(1)}, bf16[1152,3456]{1,0:T(8,128)(2,1)}, u32[]{:S(2)}) %copy-start.1) | copy-done | bytes 7962648
  44.9 13.2 %own_column.1 = (bf16[512,1152]{1,0:T(8,128)(2,1)S(1)}, f32[512,1152]{1,0:T(8,128)S(1)}, f32[512,1152]{1,0:T(8,128)S(1)}, f32[512,128]{1,0:T(8,128)S(1)}) custom-call(bf16[16,6016]{1,0:T(8,128)(2,1)S(1)} %copy-done.3, bf16[16,6016]{1,0:T(8,128)(2,1)S(1)} %collective-permute-done.refs_1_, bf16[16,6016]{1,0:T(8,128)(2,1)S(1)} %collective-permute-done.1.refs_2_, ...), custom_call_target="tpu_custom_call" | custom-call | tf_op jit(solution)/shard_map/own_column/pallas_call | solution.py:462
  58.2 19.0 %rest.1 = (f32[16,128]{1,0:T(8,128)S(1)}, f32[16,128]{1,0:T(8,128)S(1)}, f32[16,128]{1,0:T(8,128)S(1)}, f32[16,128]{1,0:T(8,128)S(1)}) custom-call(bf16[16,6016]{1,0:T(8,128)(2,1)S(1)} %copy-done.3, bf16[16,6016]{1,0:T(8,128)(2,1)S(1)} %collective-permute-done.refs_1_, bf16[16,6016]{1,0:T(8,128)(2,1)S(1)} %collective-permute-done.1.refs_2_, ...), custom_call_target="tpu_custom_call" | custom-call | tf_op jit(solution)/shard_map/rest/pallas_call | solution.py:479
  78.7 1.6 %collective-permute-start.16 = (f32[16,128]{1,0:T(8,128)S(1)}, f32[16,128]{1,0:T(8,128)S(1)}, u32[]{:S(2)}, u32[]{:S(2)}) collective-permute-start(f32[16,128]{1,0:T(8,128)S(1)} %get-tuple-element.27), channel_id=1, source_target_pairs={{0,4},{1,5},{2,6},{3,7},{4,0},{5,1},{6,2},{7,3},{8,12},{9,13},{10,... | collective-permute-start | bytes 24584 | tf_op jit(solution)/shard_map/ppermute | solution.py:434
  80.3 1.0 %collective-permute-start.17 = (f32[16,128]{1,0:T(8,128)S(1)}, f32[16,128]{1,0:T(8,128)S(1)}, u32[]{:S(2)}, u32[]{:S(2)}) collective-permute-start(f32[16,128]{1,0:T(8,128)S(1)} %get-tuple-element.28), channel_id=1, source_target_pairs={{0,6},{1,7},{2,4},{3,5},{4,2},{5,3},{6,0},{7,1},{8,14},{9,15},{10,... | collective-permute-start | bytes 24584 | tf_op jit(solution)/shard_map/ppermute | solution.py:434
  82.1 2.5 %collective-permute-done.17.refs_3_ = f32[16,128]{1,0:T(8,128)S(1)} collective-permute-done((f32[16,128]{1,0:T(8,128)S(1)}, f32[16,128]{1,0:T(8,128)S(1)}, u32[]{:S(2)}, u32[]{:S(2)}) %collective-permute-start.17) | collective-permute-done | bytes 8224 | tf_op jit(solution)/shard_map/ppermute | solution.py:434
  85.2 1.5 %finish.1 = (f32[4,16,128]{2,1,0:T(8,128)}, f32[4,16,128]{2,1,0:T(8,128)}, f32[16,128]{1,0:T(8,128)}) custom-call(s32[4]{0:T(128)} %step_ref.1, f32[31]{0:T(128)} %levels_ref.1, f32[4,16,128]{2,1,0:T(8,128)} %latents_ref.3, f32[16,128]{1,0:T(8,128)} %copy-done.5, f32[16,128]{1,0:T(8,128)} %copy-done.7, f32[16,128]{1,0:T(8,128)} %copy-done.8, f32[16,128]{1,0:T(8,128)} %copy-done.9), custom_call_target="tpu_custom_call" | custom-call | tf_op jit(solution)/shard_map/finish/pallas_call | solution.py:517
  86.6 3.6 %collective-permute-start.18 = (f32[16,128]{1,0:T(8,128)}, f32[16,128]{1,0:T(8,128)S(1)}, u32[]{:S(2)}, u32[]{:S(2)}) collective-permute-start(f32[16,128]{1,0:T(8,128)} %get-tuple-element.30), channel_id=1, source_target_pairs={{8,0},{16,8},{24,16},{9,1},{17,9},{25,17},{10,2},{18,10},{26,18},{... | collective-permute-start | bytes 24584 | tf_op jit(solution)/shard_map/ppermute | solution.py:528
  90.2 2.6 %collective-permute-done.18 = f32[16,128]{1,0:T(8,128)S(1)} collective-permute-done((f32[16,128]{1,0:T(8,128)}, f32[16,128]{1,0:T(8,128)S(1)}, u32[]{:S(2)}, u32[]{:S(2)}) %collective-permute-start.18) | collective-permute-done | bytes 8224 | tf_op jit(solution)/shard_map/ppermute | solution.py:528
  (50 shorter events, 7.9 us)
Async XLA Ops:
  0.6 27.4 %copy-start = (f32[30,5,1152]{2,0,1:T(8,128)S(1)}, f32[30,5,1152]{2,0,1:T(8,128)}, u32[]{:S(2)}) copy-start(f32[30,5,1152]{2,0,1:T(8,128)} %param.16) | copy-start | bytes 2073604
  4.4 22.2 %collective-permute-start.7 = (bf16[16,6016]{1,0:T(8,128)(2,1)}, bf16[16,6016]{1,0:T(8,128)(2,1)S(1)}, u32[]{:S(2)}, u32[]{:S(2)}) collective-permute-start(bf16[16,6016]{1,0:T(8,128)(2,1)} %get-tuple-element.17.refs_0_), channel_id=1, source_target_pairs={{0,8},{8,0},{16,24},{24,16},{1,9},{9,1},{17,25},{25,17},{2,10},{10... | collective-permute-start | bytes 577544 | tf_op jit(solution)/shard_map/ppermute | solution.py:440
  4.4 23.3 %collective-permute-start.3 = (bf16[16,6016]{1,0:T(8,128)(2,1)}, bf16[16,6016]{1,0:T(8,128)(2,1)S(1)}, u32[]{:S(2)}, u32[]{:S(2)}) collective-permute-start(bf16[16,6016]{1,0:T(8,128)(2,1)} %get-tuple-element.17.refs_0_), channel_id=1, source_target_pairs={{0,1},{1,0},{2,3},{3,2},{4,5},{5,4},{6,7},{7,6},{8,9},{9,8},{10,11... | collective-permute-start | bytes 577544 | tf_op jit(solution)/shard_map/ppermute | solution.py:437
  7.1 9.9 %collective-permute-start = (bf16[16,6016]{1,0:T(8,128)(2,1)}, bf16[16,6016]{1,0:T(8,128)(2,1)S(1)}, u32[]{:S(2)}, u32[]{:S(2)}) collective-permute-start(bf16[16,6016]{1,0:T(8,128)(2,1)} %get-tuple-element.18), channel_id=1, source_target_pairs={{0,2},{1,3},{2,0},{3,1},{4,6},{5,7},{6,4},{7,5},{8,10},{9,11},{10,... | collective-permute-start | bytes 577544 | tf_op jit(solution)/shard_map/ppermute | solution.py:434
  8.4 9.7 %collective-permute-start.1 = (bf16[16,6016]{1,0:T(8,128)(2,1)}, bf16[16,6016]{1,0:T(8,128)(2,1)S(1)}, u32[]{:S(2)}, u32[]{:S(2)}) collective-permute-start(bf16[16,6016]{1,0:T(8,128)(2,1)} %get-tuple-element.19), channel_id=1, source_target_pairs={{0,4},{1,5},{2,6},{3,7},{4,0},{5,1},{6,2},{7,3},{8,12},{9,13},{10,... | collective-permute-start | bytes 577544 | tf_op jit(solution)/shard_map/ppermute | solution.py:434
  10.7 13.1 %collective-permute-start.2 = (bf16[16,6016]{1,0:T(8,128)(2,1)}, bf16[16,6016]{1,0:T(8,128)(2,1)S(1)}, u32[]{:S(2)}, u32[]{:S(2)}) collective-permute-start(bf16[16,6016]{1,0:T(8,128)(2,1)} %get-tuple-element.20), channel_id=1, source_target_pairs={{0,6},{1,7},{2,4},{3,5},{4,2},{5,3},{6,0},{7,1},{8,14},{9,15},{10,... | collective-permute-start | bytes 577544 | tf_op jit(solution)/shard_map/ppermute | solution.py:434
  17.0 12.0 %collective-permute-start.8 = (bf16[16,6016]{1,0:T(8,128)(2,1)S(1)}, bf16[16,6016]{1,0:T(8,128)(2,1)S(1)}, u32[]{:S(2)}, u32[]{:S(2)}) collective-permute-start(bf16[16,6016]{1,0:T(8,128)(2,1)S(1)} %collective-permute-done.refs_1_), channel_id=1, source_target_pairs={{0,8},{8,0},{16,24},{24,16},{1,9},{9,1},{17,25},{25,17},{2,10},{10... | collective-permute-start | bytes 577544 | tf_op jit(solution)/shard_map/ppermute | solution.py:440
  18.1 11.6 %collective-permute-start.4 = (bf16[16,6016]{1,0:T(8,128)(2,1)S(1)}, bf16[16,6016]{1,0:T(8,128)(2,1)S(1)}, u32[]{:S(2)}, u32[]{:S(2)}) collective-permute-start(bf16[16,6016]{1,0:T(8,128)(2,1)S(1)} %collective-permute-done.refs_1_), channel_id=1, source_target_pairs={{0,1},{1,0},{2,3},{3,2},{4,5},{5,4},{6,7},{7,6},{8,9},{9,8},{10,11... | collective-permute-start | bytes 577544 | tf_op jit(solution)/shard_map/ppermute | solution.py:437
  23.8 9.8 %collective-permute-start.9 = (bf16[16,6016]{1,0:T(8,128)(2,1)S(1)}, bf16[16,6016]{1,0:T(8,128)(2,1)S(1)}, u32[]{:S(2)}, u32[]{:S(2)}) collective-permute-start(bf16[16,6016]{1,0:T(8,128)(2,1)S(1)} %collective-permute-done.1.refs_2_), channel_id=1, source_target_pairs={{0,8},{8,0},{16,24},{24,16},{1,9},{9,1},{17,25},{25,17},{2,10},{10... | collective-permute-start | bytes 577544 | tf_op jit(solution)/shard_map/ppermute | solution.py:440
  26.5 7.1 %collective-permute-start.5 = (bf16[16,6016]{1,0:T(8,128)(2,1)S(1)}, bf16[16,6016]{1,0:T(8,128)(2,1)S(1)}, u32[]{:S(2)}, u32[]{:S(2)}) collective-permute-start(bf16[16,6016]{1,0:T(8,128)(2,1)S(1)} %collective-permute-done.1.refs_2_), channel_id=1, source_target_pairs={{0,1},{1,0},{2,3},{3,2},{4,5},{5,4},{6,7},{7,6},{8,9},{9,8},{10,11... | collective-permute-start | bytes 577544 | tf_op jit(solution)/shard_map/ppermute | solution.py:437
  27.8 10.0 %collective-permute-start.6 = (bf16[16,6016]{1,0:T(8,128)(2,1)S(1)}, bf16[16,6016]{1,0:T(8,128)(2,1)S(1)}, u32[]{:S(2)}, u32[]{:S(2)}) collective-permute-start(bf16[16,6016]{1,0:T(8,128)(2,1)S(1)} %collective-permute-done.2.refs_3_), channel_id=1, source_target_pairs={{0,1},{1,0},{2,3},{3,2},{4,5},{5,4},{6,7},{7,6},{8,9},{9,8},{10,11... | collective-permute-start | bytes 577544 | tf_op jit(solution)/shard_map/ppermute | solution.py:437
  29.0 10.8 %collective-permute-start.10 = (bf16[16,6016]{1,0:T(8,128)(2,1)S(1)}, bf16[16,6016]{1,0:T(8,128)(2,1)S(1)}, u32[]{:S(2)}, u32[]{:S(2)}) collective-permute-start(bf16[16,6016]{1,0:T(8,128)(2,1)S(1)} %collective-permute-done.2.refs_3_), channel_id=1, source_target_pairs={{0,8},{8,0},{16,24},{24,16},{1,9},{9,1},{17,25},{25,17},{2,10},{10... | collective-permute-start | bytes 577544 | tf_op jit(solution)/shard_map/ppermute | solution.py:440
  29.7 28.4 %collective-permute-start.11 = (bf16[16,6016]{1,0:T(8,128)(2,1)S(1)}, bf16[16,6016]{1,0:T(8,128)(2,1)S(1)}, u32[]{:S(2)}, u32[]{:S(2)}) collective-permute-start(bf16[16,6016]{1,0:T(8,128)(2,1)S(1)} %collective-permute-done.3.refs_4_), channel_id=1, source_target_pairs={{0,8},{8,0},{16,24},{24,16},{1,9},{9,1},{17,25},{25,17},{2,10},{10... | collective-permute-start | bytes 577544 | tf_op jit(solution)/shard_map/ppermute | solution.py:440
  33.6 24.5 %collective-permute-start.12 = (bf16[16,6016]{1,0:T(8,128)(2,1)S(1)}, bf16[16,6016]{1,0:T(8,128)(2,1)S(1)}, u32[]{:S(2)}, u32[]{:S(2)}) collective-permute-start(bf16[16,6016]{1,0:T(8,128)(2,1)S(1)} %collective-permute-done.4.refs_5_), channel_id=1, source_target_pairs={{0,8},{8,0},{16,24},{24,16},{1,9},{9,1},{17,25},{25,17},{2,10},{10... | collective-permute-start | bytes 577544 | tf_op jit(solution)/shard_map/ppermute | solution.py:440
  33.6 24.5 %collective-permute-start.13 = (bf16[16,6016]{1,0:T(8,128)(2,1)S(1)}, bf16[16,6016]{1,0:T(8,128)(2,1)S(1)}, u32[]{:S(2)}, u32[]{:S(2)}) collective-permute-start(bf16[16,6016]{1,0:T(8,128)(2,1)S(1)} %collective-permute-done.5.refs_6_), channel_id=1, source_target_pairs={{0,8},{8,0},{16,24},{24,16},{1,9},{9,1},{17,25},{25,17},{2,10},{10... | collective-permute-start | bytes 577544 | tf_op jit(solution)/shard_map/ppermute | solution.py:440
  37.7 20.4 %collective-permute-start.14 = (bf16[16,6016]{1,0:T(8,128)(2,1)S(1)}, bf16[16,6016]{1,0:T(8,128)(2,1)S(1)}, u32[]{:S(2)}, u32[]{:S(2)}) collective-permute-start(bf16[16,6016]{1,0:T(8,128)(2,1)S(1)} %collective-permute-done.6.refs_7_), channel_id=1, source_target_pairs={{0,8},{8,0},{16,24},{24,16},{1,9},{9,1},{17,25},{25,17},{2,10},{10... | collective-permute-start | bytes 577544 | tf_op jit(solution)/shard_map/ppermute | solution.py:440
  39.9 3.3 %copy-start.1 = (bf16[1152,3456]{1,0:T(8,128)(2,1)S(1)}, bf16[1152,3456]{1,0:T(8,128)(2,1)}, u32[]{:S(2)}) copy-start(bf16[1152,3456]{1,0:T(8,128)(2,1)} %refs_18_.1) | copy-start | bytes 23887876
  44.9 13.3 %copy-start.2 = (bf16[1152,1152]{1,0:T(8,128)(2,1)S(1)}, bf16[1152,1152]{1,0:T(8,128)(2,1)}, u32[]{:S(2)}) copy-start(bf16[1152,1152]{1,0:T(8,128)(2,1)} %refs_24_.1) | copy-start | bytes 7962628
  58.2 34.7 %copy-start.6 = (f32[16,128]{1,0:T(8,128)S(1)}, f32[16,128]{1,0:T(8,128)}, u32[]{:S(2)}) copy-start(f32[16,128]{1,0:T(8,128)} %param.25) | copy-start | bytes 24580
  77.8 3.6 %collective-permute-start.15 = (f32[16,128]{1,0:T(8,128)S(1)}, f32[16,128]{1,0:T(8,128)S(1)}, u32[]{:S(2)}, u32[]{:S(2)}) collective-permute-start(f32[16,128]{1,0:T(8,128)S(1)} %get-tuple-element.26), channel_id=1, source_target_pairs={{0,2},{1,3},{2,0},{3,1},{4,6},{5,7},{6,4},{7,5},{8,10},{9,11},{10,... | collective-permute-start | bytes 24584 | tf_op jit(solution)/shard_map/ppermute | solution.py:434
  78.7 3.4 %collective-permute-start.16 = (f32[16,128]{1,0:T(8,128)S(1)}, f32[16,128]{1,0:T(8,128)S(1)}, u32[]{:S(2)}, u32[]{:S(2)}) collective-permute-start(f32[16,128]{1,0:T(8,128)S(1)} %get-tuple-element.27), channel_id=1, source_target_pairs={{0,4},{1,5},{2,6},{3,7},{4,0},{5,1},{6,2},{7,3},{8,12},{9,13},{10,... | collective-permute-start | bytes 24584 | tf_op jit(solution)/shard_map/ppermute | solution.py:434
  80.3 4.3 %collective-permute-start.17 = (f32[16,128]{1,0:T(8,128)S(1)}, f32[16,128]{1,0:T(8,128)S(1)}, u32[]{:S(2)}, u32[]{:S(2)}) collective-permute-start(f32[16,128]{1,0:T(8,128)S(1)} %get-tuple-element.28), channel_id=1, source_target_pairs={{0,6},{1,7},{2,4},{3,5},{4,2},{5,3},{6,0},{7,1},{8,14},{9,15},{10,... | collective-permute-start | bytes 24584 | tf_op jit(solution)/shard_map/ppermute | solution.py:434
  81.3 3.3 %copy-start.7 = (f32[16,128]{1,0:T(8,128)}, f32[16,128]{1,0:T(8,128)S(1)}, u32[]{:S(2)}) copy-start(f32[16,128]{1,0:T(8,128)S(1)} %collective-permute-done.15.refs_1_) | copy-start | bytes 24580
  86.6 6.3 %collective-permute-start.18 = (f32[16,128]{1,0:T(8,128)}, f32[16,128]{1,0:T(8,128)S(1)}, u32[]{:S(2)}, u32[]{:S(2)}) collective-permute-start(f32[16,128]{1,0:T(8,128)} %get-tuple-element.30), channel_id=1, source_target_pairs={{8,0},{16,8},{24,16},{9,1},{17,9},{25,17},{10,2},{18,10},{26,18},{... | collective-permute-start | bytes 24584 | tf_op jit(solution)/shard_map/ppermute | solution.py:528
  (5 other events, 5.4 us)

commit v3 on v0

v3 whole, which is shorter than its diff:
```python
import functools
import math

import jax
import jax.numpy as jnp
from jax import lax
from jax.experimental import pallas as pl
from jax.experimental.pallas import tpu as pltpu
from jax.sharding import PartitionSpec as P

EPSILON = 1e-06
LANES = 128
ROWS = 16
F32 = jnp.float32
BF16 = jnp.bfloat16
VMEM_LIMIT = 24 * 1024 * 1024
NN = (((1,), (0,)), ((), ()))
NT = (((1,), (1,)), ((), ()))
TN = (((0,), (0,)), ((), ()))


def dot(a, b, dims=NN):
    return lax.dot_general(a, b, dims, preferred_element_type=F32)


def split_parts(values):
    high = values.astype(BF16)
    low = (values - high.astype(F32)).astype(BF16)
    return high, low


class Sizes:
    def __init__(self, latents, position, text, q_gain, seq):
        self.frames, self.channels, self.tokens = latents.shape
        self.width = position.shape[1]
        self.head = q_gain.shape[0]
        self.heads = self.width // self.head
        self.seq = seq
        self.share = seq // self.frames
        self.queries = self.frames * self.tokens
        _, self.part, self.text_len = text.shape
        self.half = self.tokens // 2
        self.pieces = self.half // ROWS
        self.text_pieces = -(-self.part // ROWS)
        self.latents_at = self.pieces * self.width
        self.text_at = self.latents_at + 2 * self.frames * self.tokens
        self.payload = self.text_at + self.text_pieces * self.text_len


def prep_kernel(sizes, position_ref, latents_ref, text_ref, payload_ref):
    core = lax.rem(lax.axis_index("queue"), 2)
    width, tokens = sizes.width, sizes.tokens
    for piece in range(sizes.pieces):
        start = pl.multiple_of(core * sizes.half + piece * ROWS, ROWS)
        payload_ref[:, piece * width : (piece + 1) * width] = position_ref[pl.ds(start, ROWS), :]
    for frame in range(sizes.frames):
        high, low = split_parts(latents_ref[frame])
        at = sizes.latents_at + 2 * frame * tokens
        payload_ref[:, at : at + tokens] = high
        payload_ref[:, at + tokens : at + 2 * tokens] = low
    for piece in range(sizes.text_pieces):
        first, last = piece * ROWS, min((piece + 1) * ROWS, sizes.part)
        rows = text_ref[core, first:last, :]
        if last - first < ROWS:
            blank = jnp.zeros((ROWS - (last - first), sizes.text_len), BF16)
            rows = jnp.concatenate([rows, blank], axis=0)
        at = sizes.text_at + piece * sizes.text_len
        payload_ref[:, at : at + sizes.text_len] = rows


def unpack(sizes, block, mine_ref, other_ref, position_scr, latents_scr):
    width, tokens = sizes.width, sizes.tokens
    core = lax.rem(lax.axis_index("queue"), 2)
    frame = lax.rem(lax.axis_index("seq"), sizes.frames)
    for ref, place in ((mine_ref, core), (other_ref, 1 - core)):
        for piece in range(sizes.pieces):
            start = pl.multiple_of(block * tokens + place * sizes.half + piece * ROWS, ROWS)
            position_scr[pl.ds(start, ROWS), :] = ref[:, piece * width : (piece + 1) * width]
    at = pl.multiple_of(sizes.latents_at + 2 * frame * tokens, LANES)
    both = mine_ref[:, pl.ds(at, 2 * tokens)]
    latents_scr[block, 0:ROWS, :] = both[:, :tokens]
    latents_scr[block, ROWS : 2 * ROWS, :] = both[:, tokens:]


def unpack_text(sizes, shard, mine_ref, other_ref, text_scr):
    core = lax.rem(lax.axis_index("queue"), 2)
    for ref, place in ((mine_ref, core), (other_ref, 1 - core)):
        for piece in range(sizes.text_pieces):
            first, last = piece * ROWS, min((piece + 1) * ROWS, sizes.part)
            at = sizes.text_at + piece * sizes.text_len
            rows = ref[:, at : at + sizes.text_len].astype(F32)
            start = pl.multiple_of(shard * sizes.part + first, 8)
            text_scr[place, pl.ds(start, last - first), :] = rows[: last - first]


def normalize(values, scale, shift):
    center = values - jnp.mean(values, axis=-1, keepdims=True)
    variance = jnp.mean(center * center, axis=-1, keepdims=True)
    return (center * lax.rsqrt(variance + EPSILON) * scale + shift).astype(BF16)


def embed_blocks(sizes, blocks, position_scr, latents_scr, embed_ref, rows_ref, normed_scr, hidden):
    tokens = sizes.tokens
    embed = jnp.concatenate([embed_ref[...], embed_ref[...]], axis=0)
    for block in range(blocks):
        rows = slice(block * tokens, (block + 1) * tokens)
        values = dot(latents_scr[block], embed, TN) + position_scr[rows, :].astype(F32)
        if hidden is not None:
            hidden[rows, :] = values
        normed_scr[rows, :] = normalize(values, rows_ref[1:2, :], rows_ref[0:1, :])


def head_sums(sizes):
    column = lax.broadcasted_iota(jnp.int32, (sizes.width, LANES), 0)
    first = lax.broadcasted_iota(jnp.int32, (sizes.width, LANES), 1) * sizes.head
    inside = (column >= first) & (column < first + sizes.head)
    return jnp.where(inside, 1.0, 0.0).astype(BF16)


def head_spread(sizes):
    column = lax.broadcasted_iota(jnp.int32, (LANES, sizes.width), 1)
    first = lax.broadcasted_iota(jnp.int32, (LANES, sizes.width), 0) * sizes.head
    inside = (column >= first) & (column < first + sizes.head)
    one = jnp.where(inside, 1.0, 0.0).astype(BF16)
    return jnp.concatenate([one, one], axis=0)


def spread(values, spread_matrix):
    high, low = split_parts(values)
    return dot(jnp.concatenate([high, low], axis=1), spread_matrix)


def norm_rows(sizes, source, target, gain, sums_matrix, spread_matrix, step=128):
    for start in range(0, source.shape[0], step):
        wide = source[start : start + step, :].astype(F32)
        squares = dot((wide * wide).astype(BF16), sums_matrix) * (1.0 / sizes.head)
        factor = spread(lax.rsqrt(squares + EPSILON), spread_matrix)
        target[start : start + step, :] = (wide * factor * gain).astype(BF16)


def project(normed_scr, weight_ref, first, last, out_ref, chunk=256):
    for start in range(first, last, chunk):
        end = min(start + chunk, last)
        out_ref[:, start - first : end - first] = dot(
            normed_scr[...], weight_ref[:, start:end]
        ).astype(BF16)


def window(first, last, width):
    start = first // LANES * LANES
    end = min(-(-last // LANES) * LANES, width)
    return start, end


def lane_mask(shape, first, last, axis=1):
    lane = lax.broadcasted_iota(jnp.int32, shape, axis)
    return (lane >= first) & (lane < last)


def keep(values, first, last, axis=1):
    inside = lane_mask(values.shape, first, last, axis)
    return jnp.where(inside, values, jnp.zeros_like(values))


def attend_self(sizes, q_ref, k_ref, v_ref, num_ref, sum_ref, fresh, q_step=256):
    queries, width = q_ref.shape
    keys = k_ref.shape[0]
    for q_start in range(0, queries, q_step):
        rows = slice(q_start, q_start + q_step)
        sums = jnp.zeros((q_step, LANES), F32)
        pending = jnp.zeros((q_step, LANES), F32)
        for h in range(sizes.heads):
            first, last = h * sizes.head, (h + 1) * sizes.head
            start, end = window(first, last, width)
            span = (first - start, last - start)
            scores = dot(keep(q_ref[rows, start:end], *span), k_ref[:, start:end], NT)
            weights = jnp.exp2(scores).astype(BF16)
            v = keep(v_ref[:, start:end], *span)
            mark = lane_mask((keys, LANES), h, h + 1)
            if end - start == LANES:
                ones = jnp.where(mark, 1.0, 0.0).astype(BF16)
                both = dot(weights, jnp.concatenate([v, ones], axis=1))
                sums = sums + both[:, LANES:]
                pending = pending + both[:, :LANES]
            else:
                lead = jnp.where(mark, jnp.ones((), BF16), v[:, :LANES])
                both = dot(weights, jnp.concatenate([lead, v[:, LANES:]], axis=1))
                tops = lane_mask((q_step, LANES), 0, sizes.heads)
                left = both[:, :LANES]
                sums = sums + jnp.where(tops, left, 0.0)
                pending = pending + jnp.where(tops, 0.0, left)
            if last >= start + LANES:
                if fresh:
                    num_ref[rows, start : start + LANES] = pending
                else:
                    num_ref[rows, start : start + LANES] += pending
                wide = end - start > LANES
                pending = both[:, LANES:] if wide else jnp.zeros((q_step, LANES), F32)
        if fresh:
            sum_ref[rows, :] = sums
        else:
            sum_ref[rows, :] += sums


def attend_text(sizes, q_ref, k_scr, v_scr, num_ref, sum_ref, q_step=256):
    queries, width = q_ref.shape
    keys = k_scr.shape[1]
    for q_start in range(0, queries, q_step):
        rows = slice(q_start, q_start + q_step)
        sums = jnp.zeros((q_step, LANES), F32)
        for pair in range(0, sizes.heads, 2):
            edges = [(pair + i) * sizes.head for i in range(3)]
            start, end = window(edges[0], edges[2], width)
            spans = [(edges[i] - start, edges[i + 1] - start) for i in range(2)]
            k = jnp.concatenate([keep(k_scr[start:end, :], *span, 0) for span in spans], axis=1)
            v = jnp.concatenate([keep(v_scr[start:end, :], *span, 0) for span in spans], axis=1)
            ones = [
                jnp.where(lane_mask((keys, LANES), h, h + 1), 1.0, 0.0).astype(BF16)
                for h in (pair, pair + 1)
            ]
            weights = jnp.exp2(dot(q_ref[rows, start:end], k)).astype(BF16)
            num_ref[rows, start:end] += dot(weights, v, NT)
            sums = sums + dot(weights, jnp.concatenate(ones, axis=0))
        sum_ref[rows, :] = sums


def first_kernel(
    sizes, step_ref, modulation_ref, q_gain_ref, k_gain_ref, mine, other, embed_ref, weight_ref,
    rows_ref, q_ref, k_ref, v_ref, hidden_ref, position_scr, latents_scr, normed_scr, proj_scr,
):
    width = sizes.width
    frame = lax.rem(lax.axis_index("seq"), sizes.frames)
    index = step_ref[frame]
    for i in range(5):
        row = modulation_ref[i, pl.ds(index, 1), :]
        rows_ref[i : i + 1, :] = row + 1.0 if i in (1, 4) else row
    factor = math.log2(math.e) / math.sqrt(sizes.head)
    for h in range(sizes.heads):
        rows_ref[5:6, h * sizes.head : (h + 1) * sizes.head] = q_gain_ref[...] * factor
        rows_ref[6:7, h * sizes.head : (h + 1) * sizes.head] = k_gain_ref[...]
    rows_ref[7:8, :] = jnp.zeros((1, width), F32)
    unpack(sizes, 0, mine, other, position_scr, latents_scr)
    embed_blocks(
        sizes, 1, position_scr, latents_scr, embed_ref, rows_ref, normed_scr, hidden_ref
    )
    project(normed_scr, weight_ref, 0, 2 * width, proj_scr)
    project(normed_scr, weight_ref, 2 * width, 3 * width, v_ref)
    matrices = head_sums(sizes), head_spread(sizes)
    norm_rows(sizes, proj_scr.at[:, :width], q_ref, rows_ref[5:6, :], *matrices)
    norm_rows(sizes, proj_scr.at[:, width:], k_ref, rows_ref[6:7, :], *matrices)


def own_kernel(sizes, *refs):
    count = sizes.frames - 1
    mine, other = refs[:count], refs[count : 2 * count]
    (
        embed_ref, rows_ref, weight_ref, q_one, k_one, v_one, hidden_one,
        q_ref, k_ref, v_ref, hidden_ref, position_scr, latents_scr, normed_scr, proj_scr,
    ) = refs[2 * count :]
    width, tokens = sizes.width, sizes.tokens
    for block in range(count):
        unpack(sizes, block, mine[block], other[block], position_scr, latents_scr)
    q_ref[:tokens, :] = q_one[...]
    k_ref[:tokens, :] = k_one[...]
    v_ref[:tokens, :] = v_one[...]
    hidden_ref[:tokens, :] = hidden_one[...]
    embed_blocks(
        sizes, count, position_scr, latents_scr, embed_ref, rows_ref, normed_scr,
        hidden_ref.at[tokens:, :],
    )
    project(normed_scr, weight_ref, 0, 2 * width, proj_scr)
    project(normed_scr, weight_ref, 2 * width, 3 * width, v_ref.at[tokens:, :])
    matrices = head_sums(sizes), head_spread(sizes)
    norm_rows(
        sizes, proj_scr.at[:, :width], q_ref.at[tokens:, :], rows_ref[5:6, :], *matrices
    )
    norm_rows(
        sizes, proj_scr.at[:, width:], k_ref.at[tokens:, :], rows_ref[6:7, :], *matrices
    )


def attend_kernel(sizes, q_ref, k_ref, v_ref, num_ref, sum_ref):
    attend_self(sizes, q_ref, k_ref, v_ref, num_ref, sum_ref, True)


def rest_kernel(sizes, *refs):
    frames, share, width, tokens = sizes.frames, sizes.share, sizes.width, sizes.tokens
    count = frames * share
    mine, other = refs[:count], refs[count : 2 * count]
    (
        embed_ref, rows_ref, weight_ref, q_ref, hidden_ref, num_in_ref, sum_in_ref,
        out_weight_ref, final_weight_ref,
    ) = refs[2 * count : 2 * count + 9]
    velocity_refs = refs[2 * count + 9 : 2 * count + 9 + frames]
    (
        position_scr, latents_scr, normed_scr, proj_scr, k_scr, v_scr, num_ref, sum_ref,
        text_scr, tk_scr, tv_scr, tnum_scr, tsum_scr, attention_scr,
    ) = refs[2 * count + 9 + frames :]
    sums_matrix, spread_matrix = head_sums(sizes), head_spread(sizes)
    num_ref[...] = num_in_ref[...]
    sum_ref[...] = sum_in_ref[...]
    for group in range(1, share):
        for block in range(frames):
            at = group * frames + block
            unpack(sizes, block, mine[at], other[at], position_scr, latents_scr)
        embed_blocks(
            sizes, frames, position_scr, latents_scr, embed_ref, rows_ref, normed_scr, None
        )
        project(normed_scr, weight_ref, width, 2 * width, proj_scr)
        project(normed_scr, weight_ref, 2 * width, 3 * width, v_scr)
        norm_rows(sizes, proj_scr, k_scr, rows_ref[6:7, :], sums_matrix, spread_matrix)
        attend_self(sizes, q_ref, k_scr, v_scr, num_ref, sum_ref, False)

    place = lax.axis_index("seq")
    for at in range(count):
        unpack_text(sizes, jnp.bitwise_xor(place, at), mine[at], other[at], text_scr)
    gain_column = jnp.transpose(jnp.broadcast_to(rows_ref[6:7, :], (LANES, width)))[:, 0:1]
    for h in range(sizes.heads):
        rows = slice(h * sizes.head, (h + 1) * sizes.head)
        values = text_scr[0, rows, :]
        mean = jnp.mean(values * values, axis=0, keepdims=True)
        text_scr[0, rows, :] = values * lax.rsqrt(mean + EPSILON) * gain_column[rows]
    tk_scr[...] = text_scr[0].astype(BF16)
    tv_scr[...] = text_scr[1].astype(BF16)
    tnum_scr[...] = jnp.zeros_like(tnum_scr)
    attend_text(sizes, q_ref, tk_scr, tv_scr, tnum_scr, tsum_scr)

    for start in range(0, sizes.queries, LANES):
        rows = slice(start, start + LANES)
        used = lane_mask((LANES, LANES), 0, sizes.heads)
        own = spread(jnp.where(used, 1.0 / sum_ref[rows, :], 0.0), spread_matrix)
        text = spread(jnp.where(used, 1.0 / tsum_scr[rows, :], 0.0), spread_matrix)
        attention_scr[rows, :] = (num_ref[rows, :] * own + tnum_scr[rows, :] * text).astype(BF16)
    num_ref[...] = dot(attention_scr[...], out_weight_ref[...])
    for block in range(frames):
        rows = slice(block * tokens, (block + 1) * tokens)
        hidden = hidden_ref[rows, :] + rows_ref[2:3, :] * num_ref[rows, :]
        normed = normalize(hidden, rows_ref[4:5, :], rows_ref[3:4, :])
        velocity_refs[block][...] = dot(final_weight_ref[...], normed, NT)


def finish_kernel(sizes, step_ref, levels_ref, latents_ref, *refs):
    frames = sizes.frames
    arrived = refs[:frames]
    velocity_ref, moved_ref, first_ref = refs[frames:]
    own_frame = lax.rem(lax.axis_index("seq"), frames)
    for d in range(frames):
        velocity_ref[jnp.bitwise_xor(own_frame, d)] = arrived[d][...]
    for frame in range(frames):
        index = step_ref[frame]
        size = levels_ref[index + 1] - levels_ref[index]
        updated = latents_ref[frame] + size * velocity_ref[frame]
        if frame == 0:
            first_ref[...] = updated
        else:
            moved_ref[frame - 1] = updated
    moved_ref[frames - 1] = jnp.zeros_like(first_ref)


def kernel(function, sizes, name, ins, outs, scratch, us, smem=0):
    spec = pl.BlockSpec(memory_space=pltpu.VMEM)
    scalars = pl.BlockSpec(memory_space=pltpu.SMEM)
    return pl.pallas_call(
        functools.partial(function, sizes),
        out_shape=outs,
        in_specs=[scalars] * smem + [spec] * (ins - smem),
        out_specs=jax.tree.map(lambda _: spec, outs),
        scratch_shapes=scratch,
        compiler_params=pltpu.CompilerParams(vmem_limit_bytes=VMEM_LIMIT),
        cost_estimate=pl.CostEstimate(
            flops=int(us * 1e9), bytes_accessed=int(us * 1e6), transcendentals=0
        ),
        name=name,
    )


def body(
    latents,
    step_index,
    levels,
    modulation,
    embed_weight,
    position,
    qkv_weight,
    q_gain,
    k_gain,
    text_kv,
    out_weight,
    final_weight,
    new_noise,
):
    text = jnp.swapaxes(text_kv, 1, 2)
    modulation = jnp.swapaxes(modulation, 0, 1)
    sizes = Sizes(latents, position, text, q_gain, lax.axis_size("seq"))
    frames, width, tokens, queries = sizes.frames, sizes.width, sizes.tokens, sizes.queries
    queue = lax.axis_size("queue")

    def swapped(value, d):
        return lax.ppermute(value, "seq", [(i, i ^ d) for i in range(sizes.seq)])

    def over_cores(value):
        return lax.ppermute(value, "queue", [(i, i ^ 1) for i in range(queue)])

    near = functools.partial(pltpu.with_memory_space_constraint, memory_space=pltpu.VMEM)
    qkv_weight, out_weight = near(qkv_weight), near(out_weight)

    payload = kernel(
        prep_kernel, sizes, "prep", 3, pltpu.VMEM((ROWS, sizes.payload), BF16), [], 1.5
    )(position, latents, text)
    mine = [payload] + [swapped(payload, d) for d in range(1, frames)]
    for group in range(1, sizes.share):
        far = swapped(payload, group * frames)
        mine += [far] + [swapped(far, d) for d in range(1, frames)]
    other = [over_cores(value) for value in mine]

    def blocks(count):
        return [
            pltpu.VMEM((count * tokens, width), BF16),
            pltpu.VMEM((count, 2 * ROWS, tokens), BF16),
            pltpu.VMEM((count * tokens, width), BF16),
        ]

    def token_arrays(count):
        rows = count * tokens
        return [pltpu.VMEM((rows, width), BF16)] * 3 + [pltpu.VMEM((rows, width), F32)]

    rows, *one = kernel(
        first_kernel,
        sizes,
        "first",
        8,
        [pltpu.VMEM((8, width), F32)] + token_arrays(1),
        blocks(1) + [pltpu.VMEM((tokens, 2 * width), BF16)],
        4,
        smem=1,
    )(
        step_index,
        modulation,
        q_gain[None],
        k_gain[None],
        mine[0],
        other[0],
        embed_weight,
        qkv_weight,
    )
    q_hat, k_hat, value, hidden = kernel(
        own_kernel,
        sizes,
        "own",
        2 * (frames - 1) + 7,
        token_arrays(frames),
        blocks(frames - 1) + [pltpu.VMEM(((frames - 1) * tokens, 2 * width), BF16)],
        8,
    )(*mine[1:frames], *other[1:frames], embed_weight, rows, qkv_weight, *one)
    sums_shape = pltpu.VMEM((queries, LANES), F32)
    num, sums = kernel(
        attend_kernel,
        sizes,
        "attend",
        3,
        [pltpu.VMEM((queries, width), F32), sums_shape],
        [],
        5,
    )(q_hat, k_hat, value)
    velocities = kernel(
        rest_kernel,
        sizes,
        "rest",
        2 * sizes.seq + 9,
        [pltpu.VMEM((sizes.channels, tokens), F32)] * frames,
        blocks(frames)
        + [pltpu.VMEM((queries, width), BF16)] * 3
        + [
            pltpu.VMEM((queries, width), F32),
            sums_shape,
            pltpu.VMEM((2, width, sizes.text_len), F32),
            pltpu.VMEM((width, sizes.text_len), BF16),
            pltpu.VMEM((width, sizes.text_len), BF16),
            pltpu.VMEM((queries, width), F32),
            sums_shape,
            pltpu.VMEM((queries, width), BF16),
        ],
        18,
    )(
        *mine,
        *other,
        embed_weight,
        rows,
        qkv_weight,
        q_hat,
        hidden,
        num,
        sums,
        out_weight,
        final_weight.T,
    )

    arrived = [velocities[0]] + [swapped(velocities[d], d) for d in range(1, frames)]
    whole = jax.ShapeDtypeStruct(latents.shape, F32)
    velocity, moved, first = kernel(
        finish_kernel,
        sizes,
        "finish",
        3 + frames,
        [whole, whole, pltpu.VMEM(latents.shape[1:], F32)],
        [],
        1,
        smem=2,
    )(step_index, levels, latents, *arrived)
    came = lax.ppermute(first, "queue", [(i, i - 1) for i in range(1, queue)])
    at_end = lax.axis_index("queue") == queue - 1
    came = jnp.where(at_end, new_noise, came)
    advanced = lax.dynamic_update_slice_in_dim(moved, came[None], frames - 1, 0)
    return (advanced, velocity)


def solution(mesh):
    in_specs = (
        P("queue", None, "seq"),
        P("queue"),
        P(),
        P(),
        P(),
        P("seq", None),
        P(),
        P(),
        P(),
        P(None, None, "seq"),
        P(),
        P(),
        P(None, "seq"),
    )
    out_specs = (P("queue", None, "seq"), P("queue", None, "seq"))
    return jax.shard_map(body, mesh=mesh, in_specs=in_specs, out_specs=out_specs, check_vma=False)
```

time: 238 us -> 75 us (0.32)
  waiting for transfers between devices: 74.7 us -> 10.9 us
  matrix products: 62.3 us -> 0 us
  local copies, waits for them, and re-layouts: 54.7 us -> 5.9 us
  Pallas kernels: 0 us -> 33.6 us
  other arithmetic: 17.3 us -> 0.6 us
  starting transfers between devices: 26.4 us -> 22.8 us
    all_to_all x4 -> x0, waiting for transfers between devices: 72.3 us -> none  [the longest x1 26.5 us: body(): lax.all_to_all(mixture, 'seq', split_axis=0, concat_axis=2, tiled=True)]
    dot_general x15 -> x0, matrix products: 62.3 us -> none  [the longest x2 20.7 us: one_block(): jnp.einsum('fqhe,fkhe->fhqk', query_block, keys_all, preferred_element_ty...]
    pallas_call x0 -> x6, Pallas kernels: none -> 33.6 us  [the longest x1 17.7 us: body(): kernel(rest_kernel, sizes, 'rest', 2 * sizes.seq + 9, [pltpu.VMEM((sizes....]
    all_to_all x4 -> x0, starting transfers between devices: 21.6 us -> none  [the longest x1 6.36 us: body(): lax.all_to_all(keys_raw, 'seq', split_axis=2, concat_axis=1, tiled=True)]
    convert_element_type x6 -> x0, local copies, waits for them, and re-layouts: 18.8 us -> none  [the longest x4 11.4 us: head_norm(): widened = values.astype(jnp.float32)]
    ppermute x1 -> x19, starting transfers between devices: 4.88 us -> 22.8 us  [the longest x10 11.5 us: swapped(): return lax.ppermute(value, 'seq', [(i, i ^ d) for i in range(sizes.seq)])]
    ppermute x1 -> x19, waiting for transfers between devices: 2.43 us -> 10.9 us  [the longest x10 8.41 us: swapped(): return lax.ppermute(value, 'seq', [(i, i ^ d) for i in range(sizes.seq)])]
    mul x2 -> x0, local copies, waits for them, and re-layouts: 7.16 us -> none  [head_norm(): widened * widened]
  transfers between devices with their start and end apart: 5 -> 19, of which waited for: 4 -> 4; matrix products, arithmetic and copies ran while one was open for 17% -> 0% of each run, Pallas kernels for 0% -> 20%
where the time goes in v3:
time: 75 us; the launch traced here: 74.7 us
  Pallas kernels  33.6 us (45%)
  starting transfers between devices  22.8 us (30%)
  waiting for transfers between devices  10.9 us (15%)
  local copies, waits for them, and re-layouts  5.9 us (8%)
  between operations  0.82 us (1%)
    pallas_call x1, Pallas kernels, body(): kernel(rest_kernel, sizes, 'rest', 2 * sizes.seq + 9, [pltpu.VMEM((sizes....  17.7 us
    ppermute x10, starting transfers between devices, swapped(): return lax.ppermute(value, 'seq', [(i, i ^ d) for i in range(sizes.seq)])  11.5 us
    ppermute x10, waiting for transfers between devices, swapped(): return lax.ppermute(value, 'seq', [(i, i ^ d) for i in range(sizes.seq)])  8.41 us
    ppermute x8, starting transfers between devices, over_cores(): return lax.ppermute(value, 'queue', [(i, i ^ 1) for i in range(queue)])  7.74 us
    pallas_call x1, Pallas kernels, body(): kernel(own_kernel, sizes, 'own', 2 * (frames - 1) + 7, token_arrays(frame...  6.6 us
    unnamed x30, local copies, waits for them, and re-layouts  5.9 us
    pallas_call x1, Pallas kernels, body(): kernel(attend_kernel, sizes, 'attend', 3, [pltpu.VMEM((queries, width), F...  4.92 us
    ppermute x1, starting transfers between devices, body(): came = lax.ppermute(first, 'queue', [(i, i - 1) for i in range(1, queue)])  3.62 us
  transfers between devices with their start and end apart: 19, of which 4 were waited for; matrix products, arithmetic and copies ran while one was open for 0% of the time, Pallas kernels for 20%

profile of v3, /device:TPU:1, one launch (start us, length us, event | category | flops | bytes accessed | tf_op | source)
XLA Modules:
  0.0 74.7 jit_solution(1889123848415914041)
XLA Ops:
  0.6 1.0 %copy-done.4 = bf16[128,1152]{1,0:T(8,128)(2,1)S(1)} copy-done((bf16[128,1152]{1,0:T(8,128)(2,1)S(1)}, bf16[128,1152]{1,0:T(8,128)(2,1)}, u32[]{:S(2)}) %copy-start.4) | copy-done | bytes 294936
  1.6 0.9 %copy-done.5 = bf16[2,128,144]{1,2,0:T(8,128)(2,1)S(1)} copy-done((bf16[2,128,144]{1,2,0:T(8,128)(2,1)S(1)}, bf16[2,128,144]{1,2,0:T(8,128)(2,1)}, u32[]{:S(2)}) %copy-start.5) | copy-done | bytes 73752
  2.5 0.8 %copy-done.8 = f32[4,16,128]{2,1,0:T(8,128)S(1)} copy-done((f32[4,16,128]{2,1,0:T(8,128)S(1)}, f32[4,16,128]{2,1,0:T(8,128)}, u32[]{:S(2)}) %copy-start.8) | copy-done | bytes 32792
  3.3 3.1 %collective-permute-start.2 = (bf16[16,6784]{1,0:T(8,128)(2,1)S(1)}, bf16[16,6784]{1,0:T(8,128)(2,1)S(1)}, u32[]{:S(2)}, u32[]{:S(2)}) collective-permute-start(bf16[16,6784]{1,0:T(8,128)(2,1)S(1)} %prep.1.mine.refs_0_), channel_id=1, source_target_pairs={{0,3},{1,2},{2,1},{3,0},{4,7},{5,6},{6,5},{7,4},{8,11},{9,10},{10,... | collective-permute-start | bytes 651272 | tf_op jit(solution)/shard_map/ppermute | solution.py:399
  6.4 2.3 %collective-permute-start.3 = (bf16[16,6784]{1,0:T(8,128)(2,1)S(1)}, bf16[16,6784]{1,0:T(8,128)(2,1)S(1)}, u32[]{:S(2)}, u32[]{:S(2)}) collective-permute-start(bf16[16,6784]{1,0:T(8,128)(2,1)S(1)} %prep.1.mine.refs_0_), channel_id=1, source_target_pairs={{0,4},{1,5},{2,6},{3,7},{4,0},{5,1},{6,2},{7,3},{8,12},{9,13},{10,... | collective-permute-start | bytes 651272 | tf_op jit(solution)/shard_map/ppermute | solution.py:399
  8.7 1.2 %collective-permute-start.7 = (bf16[16,6784]{1,0:T(8,128)(2,1)S(1)}, bf16[16,6784]{1,0:T(8,128)(2,1)S(1)}, u32[]{:S(2)}, u32[]{:S(2)}) collective-permute-start(bf16[16,6784]{1,0:T(8,128)(2,1)S(1)} %prep.1.mine.refs_0_), channel_id=1, source_target_pairs={{0,8},{8,0},{16,24},{24,16},{1,9},{9,1},{17,25},{25,17},{2,10},{10... | collective-permute-start | bytes 651272 | tf_op jit(solution)/shard_map/ppermute | solution.py:402
  10.4 5.6 %collective-permute-done.2.refs_2_.refs_3_ = bf16[16,6784]{1,0:T(8,128)(2,1)S(1)} collective-permute-done((bf16[16,6784]{1,0:T(8,128)(2,1)S(1)}, bf16[16,6784]{1,0:T(8,128)(2,1)S(1)}, u32[]{:S(2)}, u32[]{:S(2)}) %collective-permute-start.2) | collective-permute-done | bytes 217120 | tf_op jit(solution)/shard_map/ppermute | solution.py:399
  16.0 2.1 %collective-permute-start.10 = (bf16[16,6784]{1,0:T(8,128)(2,1)S(1)}, bf16[16,6784]{1,0:T(8,128)(2,1)S(1)}, u32[]{:S(2)}, u32[]{:S(2)}) collective-permute-start(bf16[16,6784]{1,0:T(8,128)(2,1)S(1)} %collective-permute-done.2.refs_2_.refs_3_), channel_id=1, source_target_pairs={{0,8},{8,0},{16,24},{24,16},{1,9},{9,1},{17,25},{25,17},{2,10},{10... | collective-permute-start | bytes 651272 | tf_op jit(solution)/shard_map/ppermute | solution.py:402
  18.1 1.7 %collective-permute-start.4 = (bf16[16,6784]{1,0:T(8,128)(2,1)S(1)}, bf16[16,6784]{1,0:T(8,128)(2,1)S(1)}, u32[]{:S(2)}, u32[]{:S(2)}) collective-permute-start(bf16[16,6784]{1,0:T(8,128)(2,1)S(1)} %collective-permute-done.3.refs_4_), channel_id=1, source_target_pairs={{0,1},{1,0},{2,3},{3,2},{4,5},{5,4},{6,7},{7,6},{8,9},{9,8},{10,11... | collective-permute-start | bytes 651272 | tf_op jit(solution)/shard_map/ppermute | solution.py:399
  19.8 1.2 %collective-permute-start.6 = (bf16[16,6784]{1,0:T(8,128)(2,1)S(1)}, bf16[16,6784]{1,0:T(8,128)(2,1)S(1)}, u32[]{:S(2)}, u32[]{:S(2)}) collective-permute-start(bf16[16,6784]{1,0:T(8,128)(2,1)S(1)} %collective-permute-done.3.refs_4_), channel_id=1, source_target_pairs={{0,3},{1,2},{2,1},{3,0},{4,7},{5,6},{6,5},{7,4},{8,11},{9,10},{10,... | collective-permute-start | bytes 651272 | tf_op jit(solution)/shard_map/ppermute | solution.py:399
  21.1 1.8 %collective-permute-start.8 = (bf16[16,6784]{1,0:T(8,128)(2,1)S(1)}, bf16[16,6784]{1,0:T(8,128)(2,1)S(1)}, u32[]{:S(2)}, u32[]{:S(2)}) collective-permute-start(bf16[16,6784]{1,0:T(8,128)(2,1)S(1)} %collective-permute-done.refs_0_.refs_1_), channel_id=1, source_target_pairs={{0,8},{8,0},{16,24},{24,16},{1,9},{9,1},{17,25},{25,17},{2,10},{10... | collective-permute-start | bytes 651272 | tf_op jit(solution)/shard_map/ppermute | solution.py:402
  23.0 3.3 %copy-done = bf16[1152,3456]{1,0:T(8,128)(2,1)S(1)} copy-done((bf16[1152,3456]{1,0:T(8,128)(2,1)S(1)}, bf16[1152,3456]{1,0:T(8,128)(2,1)}, u32[]{:S(2)}) %copy-start) | copy-done | bytes 7962648
  26.3 3.2 %first.1 = (f32[8,1152]{1,0:T(8,128)S(1)}, bf16[128,1152]{1,0:T(8,128)(2,1)S(1)}, bf16[128,1152]{1,0:T(8,128)(2,1)S(1)}, bf16[128,1152]{1,0:T(8,128)(2,1)S(1)}, f32[128,1152]{1,0:T(8,128)S(1)}) custom-call(s32[4]{0:T(128)S(1)} %copy-done.12, f32[5,30,1152]{2,1,0:T(8,128)S(1)} %bitcast.7, f32[1,72]{1,0:T(1,128)S(1)} %bitcast.10, f32[1,72]{1,0:T(1,128)S(1)} %bitcast.11, ...), custom_call_target="tpu_custom_call" | custom-call | flops 4000000000 | bytes 4000000 | tf_op jit(solution)/shard_map/first/pallas_call | solution.py:427
  30.5 1.5 %collective-permute-start.14 = (bf16[16,6784]{1,0:T(8,128)(2,1)S(1)}, bf16[16,6784]{1,0:T(8,128)(2,1)S(1)}, u32[]{:S(2)}, u32[]{:S(2)}) collective-permute-start(bf16[16,6784]{1,0:T(8,128)(2,1)S(1)} %collective-permute-done.6.refs_7_), channel_id=1, source_target_pairs={{0,8},{8,0},{16,24},{24,16},{1,9},{9,1},{17,25},{25,17},{2,10},{10... | collective-permute-start | bytes 651272 | tf_op jit(solution)/shard_map/ppermute | solution.py:402
  32.0 6.6 %own.1 = (bf16[512,1152]{1,0:T(8,128)(2,1)S(1)}, bf16[512,1152]{1,0:T(8,128)(2,1)S(1)}, bf16[512,1152]{1,0:T(8,128)(2,1)S(1)}, f32[512,1152]{1,0:T(8,128)S(1)}) custom-call(bf16[16,6784]{1,0:T(8,128)(2,1)S(1)} %collective-permute-done.refs_0_.refs_1_, bf16[16,6784]{1,0:T(8,128)(2,1)S(1)} %collective-permute-done.1.refs_1_.refs_2_, ...), custom_call_target="tpu_custom_call" | custom-call | flops 8000000000 | bytes 8000000 | tf_op jit(solution)/shard_map/own/pallas_call | solution.py:446
  38.6 4.9 %attend.1 = (f32[512,1152]{1,0:T(8,128)S(1)}, f32[512,128]{1,0:T(8,128)S(1)}) custom-call(bf16[512,1152]{1,0:T(8,128)(2,1)S(1)} %get-tuple-element.25.q_ref.refs_19_, bf16[512,1152]{1,0:T(8,128)(2,1)S(1)} %get-tuple-element.27.k_ref, bf16[512,1152]{1,0:T(8,128)(2,1)S(1)} %get-tuple-element.28.v_ref), custom_call_target="tpu_custom_call" | custom-call | flops 5000000000 | bytes 5000000 | tf_op jit(solution)/shard_map/attend/pallas_call | solution.py:456
  43.6 17.7 %rest.1 = (f32[16,128]{1,0:T(8,128)S(1)}, f32[16,128]{1,0:T(8,128)S(1)}, f32[16,128]{1,0:T(8,128)S(1)}, f32[16,128]{1,0:T(8,128)S(1)}) custom-call(bf16[16,6784]{1,0:T(8,128)(2,1)S(1)} %prep.1.mine.refs_0_, bf16[16,6784]{1,0:T(8,128)(2,1)S(1)} %collective-permute-done.refs_0_.refs_1_, bf16[16,6784]{1,0:T(8,128)(2,1)S(1)} %collective-permute-done.1.refs_1_.refs_2_, ...), custom_call_target="tpu_custom_call" | custom-call | flops 17999998976 | bytes 18000000 | tf_op jit(solution)/shard_map/rest/pallas_call | solution.py:465
  61.4 1.4 %collective-permute-start.15 = (f32[16,128]{1,0:T(8,128)S(1)}, f32[16,128]{1,0:T(8,128)S(1)}, u32[]{:S(2)}, u32[]{:S(2)}) collective-permute-start(f32[16,128]{1,0:T(8,128)S(1)} %get-tuple-element.32), channel_id=1, source_target_pairs={{0,1},{1,0},{2,3},{3,2},{4,5},{5,4},{6,7},{7,6},{8,9},{9,8},{10,11... | collective-permute-start | bytes 24584 | tf_op jit(solution)/shard_map/ppermute | solution.py:399
  63.4 0.6 collective-permute-start.17
  64.1 1.2 %collective-permute-done.16.refs_2_ = f32[16,128]{1,0:T(8,128)S(1)} collective-permute-done((f32[16,128]{1,0:T(8,128)S(1)}, f32[16,128]{1,0:T(8,128)S(1)}, u32[]{:S(2)}, u32[]{:S(2)}) %collective-permute-start.16) | collective-permute-done | bytes 8224 | tf_op jit(solution)/shard_map/ppermute | solution.py:399
  65.3 1.5 %collective-permute-done.17.refs_3_ = f32[16,128]{1,0:T(8,128)S(1)} collective-permute-done((f32[16,128]{1,0:T(8,128)S(1)}, f32[16,128]{1,0:T(8,128)S(1)}, u32[]{:S(2)}, u32[]{:S(2)}) %collective-permute-start.17) | collective-permute-done | bytes 8224 | tf_op jit(solution)/shard_map/ppermute | solution.py:399
  66.8 1.2 %finish.1 = (f32[4,16,128]{2,1,0:T(8,128)}, f32[4,16,128]{2,1,0:T(8,128)}, f32[16,128]{1,0:T(8,128)S(1)}) custom-call(s32[4]{0:T(128)S(1)} %copy-done.12, f32[31]{0:T(128)S(1)} %copy-done.13, f32[4,16,128]{2,1,0:T(8,128)S(1)} %copy-done.9, f32[16,128]{1,0:T(8,128)S(1)} %get-tuple-element.31.refs_0_, f32[16,128]{1,0:T(8,128)S(1)} %collective-permute-done.15.refs_1_, ...), custom_call_target="tpu_custom_call" | custom-call | flops 1000000000 | bytes 1000000 | tf_op jit(solution)/shard_map/finish/pallas_call | solution.py:500
  68.0 3.6 %collective-permute-start.18 = (f32[16,128]{1,0:T(8,128)S(1)}, f32[16,128]{1,0:T(8,128)S(1)}, u32[]{:S(2)}, u32[]{:S(2)}) collective-permute-start(f32[16,128]{1,0:T(8,128)S(1)} %get-tuple-element.36), channel_id=1, source_target_pairs={{8,0},{16,8},{24,16},{9,1},{17,9},{25,17},{10,2},{18,10},{26,18},{... | collective-permute-start | bytes 24584 | tf_op jit(solution)/shard_map/ppermute | solution.py:510
  71.6 2.4 %collective-permute-done.18 = f32[16,128]{1,0:T(8,128)S(1)} collective-permute-done((f32[16,128]{1,0:T(8,128)S(1)}, f32[16,128]{1,0:T(8,128)S(1)}, u32[]{:S(2)}, u32[]{:S(2)}) %collective-permute-start.18) | collective-permute-done | bytes 8224 | tf_op jit(solution)/shard_map/ppermute | solution.py:510
  (51 shorter events, 2.9 us)
Async XLA Ops:
  3.2 19.7 %copy-start.10 = (f32[72]{0:T(128)S(1)}, f32[72]{0:T(128)}, u32[]{:S(2)}) copy-start(f32[72]{0:T(128)} %param.20) | copy-start | bytes 868
  3.2 19.7 %copy-start.11 = (f32[72]{0:T(128)S(1)}, f32[72]{0:T(128)}, u32[]{:S(2)}) copy-start(f32[72]{0:T(128)} %param.21) | copy-start | bytes 868
  3.2 19.7 %copy-start.12 = (s32[4]{0:T(128)S(1)}, s32[4]{0:T(128)}, u32[]{:S(2)}) copy-start(s32[4]{0:T(128)} %step_ref.3) | copy-start | bytes 52
  3.3 12.7 %collective-permute-start.2 = (bf16[16,6784]{1,0:T(8,128)(2,1)S(1)}, bf16[16,6784]{1,0:T(8,128)(2,1)S(1)}, u32[]{:S(2)}, u32[]{:S(2)}) collective-permute-start(bf16[16,6784]{1,0:T(8,128)(2,1)S(1)} %prep.1.mine.refs_0_), channel_id=1, source_target_pairs={{0,3},{1,2},{2,1},{3,0},{4,7},{5,6},{6,5},{7,4},{8,11},{9,10},{10,... | collective-permute-start | bytes 651272 | tf_op jit(solution)/shard_map/ppermute | solution.py:399
  6.4 11.7 %collective-permute-start.3 = (bf16[16,6784]{1,0:T(8,128)(2,1)S(1)}, bf16[16,6784]{1,0:T(8,128)(2,1)S(1)}, u32[]{:S(2)}, u32[]{:S(2)}) collective-permute-start(bf16[16,6784]{1,0:T(8,128)(2,1)S(1)} %prep.1.mine.refs_0_), channel_id=1, source_target_pairs={{0,4},{1,5},{2,6},{3,7},{4,0},{5,1},{6,2},{7,3},{8,12},{9,13},{10,... | collective-permute-start | bytes 651272 | tf_op jit(solution)/shard_map/ppermute | solution.py:399
  8.7 11.1 %collective-permute-start.7 = (bf16[16,6784]{1,0:T(8,128)(2,1)S(1)}, bf16[16,6784]{1,0:T(8,128)(2,1)S(1)}, u32[]{:S(2)}, u32[]{:S(2)}) collective-permute-start(bf16[16,6784]{1,0:T(8,128)(2,1)S(1)} %prep.1.mine.refs_0_), channel_id=1, source_target_pairs={{0,8},{8,0},{16,24},{24,16},{1,9},{9,1},{17,25},{25,17},{2,10},{10... | collective-permute-start | bytes 651272 | tf_op jit(solution)/shard_map/ppermute | solution.py:402
  10.0 9.8 %collective-permute-start = (bf16[16,6784]{1,0:T(8,128)(2,1)S(1)}, bf16[16,6784]{1,0:T(8,128)(2,1)S(1)}, u32[]{:S(2)}, u32[]{:S(2)}) collective-permute-start(bf16[16,6784]{1,0:T(8,128)(2,1)S(1)} %prep.1.mine.refs_0_), channel_id=1, source_target_pairs={{0,1},{1,0},{2,3},{3,2},{4,5},{5,4},{6,7},{7,6},{8,9},{9,8},{10,11... | collective-permute-start | bytes 651272 | tf_op jit(solution)/shard_map/ppermute | solution.py:399
  10.2 10.8 %collective-permute-start.1 = (bf16[16,6784]{1,0:T(8,128)(2,1)S(1)}, bf16[16,6784]{1,0:T(8,128)(2,1)S(1)}, u32[]{:S(2)}, u32[]{:S(2)}) collective-permute-start(bf16[16,6784]{1,0:T(8,128)(2,1)S(1)} %prep.1.mine.refs_0_), channel_id=1, source_target_pairs={{0,2},{1,3},{2,0},{3,1},{4,6},{5,7},{6,4},{7,5},{8,10},{9,11},{10,... | collective-permute-start | bytes 651272 | tf_op jit(solution)/shard_map/ppermute | solution.py:399
  16.0 6.9 %collective-permute-start.10 = (bf16[16,6784]{1,0:T(8,128)(2,1)S(1)}, bf16[16,6784]{1,0:T(8,128)(2,1)S(1)}, u32[]{:S(2)}, u32[]{:S(2)}) collective-permute-start(bf16[16,6784]{1,0:T(8,128)(2,1)S(1)} %collective-permute-done.2.refs_2_.refs_3_), channel_id=1, source_target_pairs={{0,8},{8,0},{16,24},{24,16},{1,9},{9,1},{17,25},{25,17},{2,10},{10... | collective-permute-start | bytes 651272 | tf_op jit(solution)/shard_map/ppermute | solution.py:402
  18.1 11.9 %collective-permute-start.4 = (bf16[16,6784]{1,0:T(8,128)(2,1)S(1)}, bf16[16,6784]{1,0:T(8,128)(2,1)S(1)}, u32[]{:S(2)}, u32[]{:S(2)}) collective-permute-start(bf16[16,6784]{1,0:T(8,128)(2,1)S(1)} %collective-permute-done.3.refs_4_), channel_id=1, source_target_pairs={{0,1},{1,0},{2,3},{3,2},{4,5},{5,4},{6,7},{7,6},{8,9},{9,8},{10,11... | collective-permute-start | bytes 651272 | tf_op jit(solution)/shard_map/ppermute | solution.py:399
  19.8 10.2 %collective-permute-start.5 = (bf16[16,6784]{1,0:T(8,128)(2,1)S(1)}, bf16[16,6784]{1,0:T(8,128)(2,1)S(1)}, u32[]{:S(2)}, u32[]{:S(2)}) collective-permute-start(bf16[16,6784]{1,0:T(8,128)(2,1)S(1)} %collective-permute-done.3.refs_4_), channel_id=1, source_target_pairs={{0,2},{1,3},{2,0},{3,1},{4,6},{5,7},{6,4},{7,5},{8,10},{9,11},{10,... | collective-permute-start | bytes 651272 | tf_op jit(solution)/shard_map/ppermute | solution.py:399
  19.8 10.7 %collective-permute-start.6 = (bf16[16,6784]{1,0:T(8,128)(2,1)S(1)}, bf16[16,6784]{1,0:T(8,128)(2,1)S(1)}, u32[]{:S(2)}, u32[]{:S(2)}) collective-permute-start(bf16[16,6784]{1,0:T(8,128)(2,1)S(1)} %collective-permute-done.3.refs_4_), channel_id=1, source_target_pairs={{0,3},{1,2},{2,1},{3,0},{4,7},{5,6},{6,5},{7,4},{8,11},{9,10},{10,... | collective-permute-start | bytes 651272 | tf_op jit(solution)/shard_map/ppermute | solution.py:399
  21.1 8.4 %collective-permute-start.8 = (bf16[16,6784]{1,0:T(8,128)(2,1)S(1)}, bf16[16,6784]{1,0:T(8,128)(2,1)S(1)}, u32[]{:S(2)}, u32[]{:S(2)}) collective-permute-start(bf16[16,6784]{1,0:T(8,128)(2,1)S(1)} %collective-permute-done.refs_0_.refs_1_), channel_id=1, source_target_pairs={{0,8},{8,0},{16,24},{24,16},{1,9},{9,1},{17,25},{25,17},{2,10},{10... | collective-permute-start | bytes 651272 | tf_op jit(solution)/shard_map/ppermute | solution.py:402
  22.9 9.1 %collective-permute-start.9 = (bf16[16,6784]{1,0:T(8,128)(2,1)S(1)}, bf16[16,6784]{1,0:T(8,128)(2,1)S(1)}, u32[]{:S(2)}, u32[]{:S(2)}) collective-permute-start(bf16[16,6784]{1,0:T(8,128)(2,1)S(1)} %collective-permute-done.1.refs_1_.refs_2_), channel_id=1, source_target_pairs={{0,8},{8,0},{16,24},{24,16},{1,9},{9,1},{17,25},{25,17},{2,10},{10... | collective-permute-start | bytes 651272 | tf_op jit(solution)/shard_map/ppermute | solution.py:402
  29.4 14.1 %collective-permute-start.11 = (bf16[16,6784]{1,0:T(8,128)(2,1)S(1)}, bf16[16,6784]{1,0:T(8,128)(2,1)S(1)}, u32[]{:S(2)}, u32[]{:S(2)}) collective-permute-start(bf16[16,6784]{1,0:T(8,128)(2,1)S(1)} %collective-permute-done.3.refs_4_), channel_id=1, source_target_pairs={{0,8},{8,0},{16,24},{24,16},{1,9},{9,1},{17,25},{25,17},{2,10},{10... | collective-permute-start | bytes 651272 | tf_op jit(solution)/shard_map/ppermute | solution.py:402
  29.9 13.6 %collective-permute-start.12 = (bf16[16,6784]{1,0:T(8,128)(2,1)S(1)}, bf16[16,6784]{1,0:T(8,128)(2,1)S(1)}, u32[]{:S(2)}, u32[]{:S(2)}) collective-permute-start(bf16[16,6784]{1,0:T(8,128)(2,1)S(1)} %collective-permute-done.4.refs_5_), channel_id=1, source_target_pairs={{0,8},{8,0},{16,24},{24,16},{1,9},{9,1},{17,25},{25,17},{2,10},{10... | collective-permute-start | bytes 651272 | tf_op jit(solution)/shard_map/ppermute | solution.py:402
  30.0 13.5 %collective-permute-start.13 = (bf16[16,6784]{1,0:T(8,128)(2,1)S(1)}, bf16[16,6784]{1,0:T(8,128)(2,1)S(1)}, u32[]{:S(2)}, u32[]{:S(2)}) collective-permute-start(bf16[16,6784]{1,0:T(8,128)(2,1)S(1)} %collective-permute-done.5.refs_6_), channel_id=1, source_target_pairs={{0,8},{8,0},{16,24},{24,16},{1,9},{9,1},{17,25},{25,17},{2,10},{10... | collective-permute-start | bytes 651272 | tf_op jit(solution)/shard_map/ppermute | solution.py:402
  30.5 13.1 %collective-permute-start.14 = (bf16[16,6784]{1,0:T(8,128)(2,1)S(1)}, bf16[16,6784]{1,0:T(8,128)(2,1)S(1)}, u32[]{:S(2)}, u32[]{:S(2)}) collective-permute-start(bf16[16,6784]{1,0:T(8,128)(2,1)S(1)} %collective-permute-done.6.refs_7_), channel_id=1, source_target_pairs={{0,8},{8,0},{16,24},{24,16},{1,9},{9,1},{17,25},{25,17},{2,10},{10... | collective-permute-start | bytes 651272 | tf_op jit(solution)/shard_map/ppermute | solution.py:402
  43.6 23.2 %copy-start.9 = (f32[4,16,128]{2,1,0:T(8,128)S(1)}, f32[4,16,128]{2,1,0:T(8,128)}, u32[]{:S(2)}) copy-start(f32[4,16,128]{2,1,0:T(8,128)} %latents_ref.3) | copy-start | bytes 98308
  43.6 23.2 %copy-start.13 = (f32[31]{0:T(128)S(1)}, f32[31]{0:T(128)}, u32[]{:S(2)}) copy-start(f32[31]{0:T(128)} %levels_ref.1) | copy-start | bytes 376
  61.4 2.7 %collective-permute-start.15 = (f32[16,128]{1,0:T(8,128)S(1)}, f32[16,128]{1,0:T(8,128)S(1)}, u32[]{:S(2)}, u32[]{:S(2)}) collective-permute-start(f32[16,128]{1,0:T(8,128)S(1)} %get-tuple-element.32), channel_id=1, source_target_pairs={{0,1},{1,0},{2,3},{3,2},{4,5},{5,4},{6,7},{7,6},{8,9},{9,8},{10,11... | collective-permute-start | bytes 24584 | tf_op jit(solution)/shard_map/ppermute | solution.py:399
  62.8 2.5 %collective-permute-start.16 = (f32[16,128]{1,0:T(8,128)S(1)}, f32[16,128]{1,0:T(8,128)S(1)}, u32[]{:S(2)}, u32[]{:S(2)}) collective-permute-start(f32[16,128]{1,0:T(8,128)S(1)} %get-tuple-element.33), channel_id=1, source_target_pairs={{0,2},{1,3},{2,0},{3,1},{4,6},{5,7},{6,4},{7,5},{8,10},{9,11},{10,... | collective-permute-start | bytes 24584 | tf_op jit(solution)/shard_map/ppermute | solution.py:399
  63.4 3.4 %collective-permute-start.17 = (f32[16,128]{1,0:T(8,128)S(1)}, f32[16,128]{1,0:T(8,128)S(1)}, u32[]{:S(2)}, u32[]{:S(2)}) collective-permute-start(f32[16,128]{1,0:T(8,128)S(1)} %get-tuple-element.34), channel_id=1, source_target_pairs={{0,3},{1,2},{2,1},{3,0},{4,7},{5,6},{6,5},{7,4},{8,11},{9,10},{10,... | collective-permute-start | bytes 24584 | tf_op jit(solution)/shard_map/ppermute | solution.py:399
  68.0 6.1 %collective-permute-start.18 = (f32[16,128]{1,0:T(8,128)S(1)}, f32[16,128]{1,0:T(8,128)S(1)}, u32[]{:S(2)}, u32[]{:S(2)}) collective-permute-start(f32[16,128]{1,0:T(8,128)S(1)} %get-tuple-element.36), channel_id=1, source_target_pairs={{8,0},{16,8},{24,16},{9,1},{17,9},{25,17},{10,2},{18,10},{26,18},{... | collective-permute-start | bytes 24584 | tf_op jit(solution)/shard_map/ppermute | solution.py:510
  (10 other events, 73.8 us)

commit v4 on v3

--- a/solution.py
+++ b/solution.py
@@ -47,25 +47,43 @@
         self.payload = self.text_at + self.text_pieces * self.text_len
 
 
-def prep_kernel(sizes, position_ref, latents_ref, text_ref, payload_ref):
+def prep_kernel(
+    sizes, position_ref, latents_ref, text_ref, payload_ref, latents_scr, text_scr, sems
+):
     core = lax.rem(lax.axis_index("queue"), 2)
     width, tokens = sizes.width, sizes.tokens
+    copies = [
+        pltpu.make_async_copy(latents_ref, latents_scr, sems.at[0]),
+        pltpu.make_async_copy(text_ref.at[core], text_scr, sems.at[1]),
+    ]
     for piece in range(sizes.pieces):
         start = pl.multiple_of(core * sizes.half + piece * ROWS, ROWS)
-        payload_ref[:, piece * width : (piece + 1) * width] = position_ref[pl.ds(start, ROWS), :]
+        copies.append(
+            pltpu.make_async_copy(
+                position_ref.at[pl.ds(start, ROWS), :],
+                payload_ref.at[:, piece * width : (piece + 1) * width],
+                sems.at[2 + piece],
+            )
+        )
+    for copy in copies:
+        copy.start()
+    copies[0].wait()
     for frame in range(sizes.frames):
-        high, low = split_parts(latents_ref[frame])
+        high, low = split_parts(latents_scr[frame])
         at = sizes.latents_at + 2 * frame * tokens
         payload_ref[:, at : at + tokens] = high
         payload_ref[:, at + tokens : at + 2 * tokens] = low
+    copies[1].wait()
     for piece in range(sizes.text_pieces):
         first, last = piece * ROWS, min((piece + 1) * ROWS, sizes.part)
-        rows = text_ref[core, first:last, :]
+        rows = text_scr[first:last, :]
         if last - first < ROWS:
             blank = jnp.zeros((ROWS - (last - first), sizes.text_len), BF16)
             rows = jnp.concatenate([rows, blank], axis=0)
         at = sizes.text_at + piece * sizes.text_len
         payload_ref[:, at : at + sizes.text_len] = rows
+    for copy in copies[2:]:
+        copy.wait()
 
 
 def unpack(sizes, block, mine_ref, other_ref, position_scr, latents_scr):
@@ -78,8 +96,16 @@
             position_scr[pl.ds(start, ROWS), :] = ref[:, piece * width : (piece + 1) * width]
     at = pl.multiple_of(sizes.latents_at + 2 * frame * tokens, LANES)
     both = mine_ref[:, pl.ds(at, 2 * tokens)]
-    latents_scr[block, 0:ROWS, :] = both[:, :tokens]
-    latents_scr[block, ROWS : 2 * ROWS, :] = both[:, tokens:]
+    lanes = slice(block * tokens, (block + 1) * tokens)
+    latents_scr[0:ROWS, lanes] = both[:, :tokens]
+    latents_scr[ROWS : 2 * ROWS, lanes] = both[:, tokens:]
+
+
+def own_latents(sizes, mine_ref):
+    frame = lax.rem(lax.axis_index("seq"), sizes.frames)
+    at = pl.multiple_of(sizes.latents_at + 2 * frame * sizes.tokens, LANES)
+    both = mine_ref[:, pl.ds(at, 2 * sizes.tokens)].astype(F32)
+    return both[:, : sizes.tokens] + both[:, sizes.tokens :]
 
 
 def unpack_text(sizes, shard, mine_ref, other_ref, text_scr):
@@ -102,9 +128,10 @@
 def embed_blocks(sizes, blocks, position_scr, latents_scr, embed_ref, rows_ref, normed_scr, hidden):
     tokens = sizes.tokens
     embed = jnp.concatenate([embed_ref[...], embed_ref[...]], axis=0)
+    embedded = dot(latents_scr[...], embed, TN)
     for block in range(blocks):
         rows = slice(block * tokens, (block + 1) * tokens)
-        values = dot(latents_scr[block], embed, TN) + position_scr[rows, :].astype(F32)
+        values = embedded[rows] + position_scr[rows, :].astype(F32)
         if hidden is not None:
             hidden[rows, :] = values
         normed_scr[rows, :] = normalize(values, rows_ref[1:2, :], rows_ref[0:1, :])
@@ -130,7 +157,7 @@
     return dot(jnp.concatenate([high, low], axis=1), spread_matrix)
 
 
-def norm_rows(sizes, source, target, gain, sums_matrix, spread_matrix, step=128):
+def norm_rows(sizes, source, target, gain, sums_matrix, spread_matrix, step=256):
     for start in range(0, source.shape[0], step):
         wide = source[start : start + step, :].astype(F32)
         squares = dot((wide * wide).astype(BF16), sums_matrix) * (1.0 / sizes.head)
@@ -162,7 +189,7 @@
     return jnp.where(inside, values, jnp.zeros_like(values))
 
 
-def attend_self(sizes, q_ref, k_ref, v_ref, num_ref, sum_ref, fresh, q_step=256):
+def attend_self(sizes, q_ref, k_ref, v_ref, num_ref, sum_ref, fresh, q_step=512):
     queries, width = q_ref.shape
     keys = k_ref.shape[0]
     for q_start in range(0, queries, q_step):
@@ -202,12 +229,13 @@
             sum_ref[rows, :] += sums
 
 
-def attend_text(sizes, q_ref, k_scr, v_scr, num_ref, sum_ref, q_step=256):
+def attend_text(sizes, q_ref, k_scr, v_scr, num_ref, sum_ref, q_step=512):
     queries, width = q_ref.shape
     keys = k_scr.shape[1]
     for q_start in range(0, queries, q_step):
         rows = slice(q_start, q_start + q_step)
         sums = jnp.zeros((q_step, LANES), F32)
+        pending, pending_at = None, None
         for pair in range(0, sizes.heads, 2):
             edges = [(pair + i) * sizes.head for i in range(3)]
             start, end = window(edges[0], edges[2], width)
@@ -219,16 +247,34 @@
                 for h in (pair, pair + 1)
             ]
             weights = jnp.exp2(dot(q_ref[rows, start:end], k)).astype(BF16)
-            num_ref[rows, start:end] += dot(weights, v, NT)
+            both = dot(weights, v, NT)
             sums = sums + dot(weights, jnp.concatenate(ones, axis=0))
+            for at in range(start, end, LANES):
+                part = both[:, at - start : at - start + LANES]
+                if pending_at == at:
+                    part = pending + part
+                elif pending_at is not None and pending_at < at:
+                    num_ref[rows, pending_at : pending_at + LANES] = pending
+                pending, pending_at = part, at
+        num_ref[rows, pending_at : pending_at + LANES] = pending
         sum_ref[rows, :] = sums
 
 
 def first_kernel(
-    sizes, step_ref, modulation_ref, q_gain_ref, k_gain_ref, mine, other, embed_ref, weight_ref,
-    rows_ref, q_ref, k_ref, v_ref, hidden_ref, position_scr, latents_scr, normed_scr, proj_scr,
+    sizes, step_ref, levels_ref, modulation_ref, q_gain_ref, k_gain_ref, mine, other, embed_ref, weight_ref,
+    rows_ref, near_ref, q_ref, k_ref, v_ref, hidden_ref,
+    position_scr, latents_scr, normed_scr, proj_scr, sems,
 ):
     width = sizes.width
+    copies = []
+    for i in range(3):
+        columns = slice(i * width, (i + 1) * width)
+        copies.append(
+            pltpu.make_async_copy(
+                weight_ref.at[:, columns], near_ref.at[:, columns], sems.at[i]
+            )
+        )
+        copies[i].start()
     frame = lax.rem(lax.axis_index("seq"), sizes.frames)
     index = step_ref[frame]
     for i in range(5):
@@ -238,16 +284,20 @@
     for h in range(sizes.heads):
         rows_ref[5:6, h * sizes.head : (h + 1) * sizes.head] = q_gain_ref[...] * factor
         rows_ref[6:7, h * sizes.head : (h + 1) * sizes.head] = k_gain_ref[...]
-    rows_ref[7:8, :] = jnp.zeros((1, width), F32)
+    rows_ref[7:8, :] = jnp.full((1, width), levels_ref[index + 1] - levels_ref[index])
     unpack(sizes, 0, mine, other, position_scr, latents_scr)
     embed_blocks(
         sizes, 1, position_scr, latents_scr, embed_ref, rows_ref, normed_scr, hidden_ref
     )
-    project(normed_scr, weight_ref, 0, 2 * width, proj_scr)
-    project(normed_scr, weight_ref, 2 * width, 3 * width, v_ref)
     matrices = head_sums(sizes), head_spread(sizes)
-    norm_rows(sizes, proj_scr.at[:, :width], q_ref, rows_ref[5:6, :], *matrices)
-    norm_rows(sizes, proj_scr.at[:, width:], k_ref, rows_ref[6:7, :], *matrices)
+    copies[0].wait()
+    project(normed_scr, near_ref, 0, width, proj_scr)
+    norm_rows(sizes, proj_scr, q_ref, rows_ref[5:6, :], *matrices)
+    copies[1].wait()
+    project(normed_scr, near_ref, width, 2 * width, proj_scr)
+    norm_rows(sizes, proj_scr, k_ref, rows_ref[6:7, :], *matrices)
+    copies[2].wait()
+    project(normed_scr, near_ref, 2 * width, 3 * width, v_ref)
 
 
 def own_kernel(sizes, *refs):
@@ -279,8 +329,13 @@
     )
 
 
-def attend_kernel(sizes, q_ref, k_ref, v_ref, num_ref, sum_ref):
+def attend_kernel(
+    sizes, q_ref, k_ref, v_ref, out_weight_ref, num_ref, sum_ref, near_ref, sem
+):
+    copy = pltpu.make_async_copy(out_weight_ref, near_ref, sem)
+    copy.start()
     attend_self(sizes, q_ref, k_ref, v_ref, num_ref, sum_ref, True)
+    copy.wait()
 
 
 def rest_kernel(sizes, *refs):
@@ -292,10 +347,11 @@
         out_weight_ref, final_weight_ref,
     ) = refs[2 * count : 2 * count + 9]
     velocity_refs = refs[2 * count + 9 : 2 * count + 9 + frames]
+    updated_refs = refs[2 * count + 9 + frames : 2 * count + 9 + 2 * frames]
     (
-        position_scr, latents_scr, normed_scr, proj_scr, k_scr, v_scr, num_ref, sum_ref,
+        position_scr, latents_scr, normed_scr, proj_scr, k_scr, num_ref, sum_ref,
         text_scr, tk_scr, tv_scr, tnum_scr, tsum_scr, attention_scr,
-    ) = refs[2 * count + 9 + frames :]
+    ) = refs[2 * count + 9 + 2 * frames :]
     sums_matrix, spread_matrix = head_sums(sizes), head_spread(sizes)
     num_ref[...] = num_in_ref[...]
     sum_ref[...] = sum_in_ref[...]
@@ -306,10 +362,10 @@
         embed_blocks(
             sizes, frames, position_scr, latents_scr, embed_ref, rows_ref, normed_scr, None
         )
-        project(normed_scr, weight_ref, width, 2 * width, proj_scr)
-        project(normed_scr, weight_ref, 2 * width, 3 * width, v_scr)
-        norm_rows(sizes, proj_scr, k_scr, rows_ref[6:7, :], sums_matrix, spread_matrix)
-        attend_self(sizes, q_ref, k_scr, v_scr, num_ref, sum_ref, False)
+        project(normed_scr, weight_ref, width, 3 * width, proj_scr)
+        keys, values = proj_scr.at[:, :width], proj_scr.at[:, width:]
+        norm_rows(sizes, keys, k_scr, rows_ref[6:7, :], sums_matrix, spread_matrix)
+        attend_self(sizes, q_ref, k_scr, values, num_ref, sum_ref, False)
 
     place = lax.axis_index("seq")
     for at in range(count):
@@ -322,7 +378,6 @@
         text_scr[0, rows, :] = values * lax.rsqrt(mean + EPSILON) * gain_column[rows]
     tk_scr[...] = text_scr[0].astype(BF16)
     tv_scr[...] = text_scr[1].astype(BF16)
-    tnum_scr[...] = jnp.zeros_like(tnum_scr)
     attend_text(sizes, q_ref, tk_scr, tv_scr, tnum_scr, tsum_scr)
 
     for start in range(0, sizes.queries, LANES):
@@ -336,35 +391,36 @@
         rows = slice(block * tokens, (block + 1) * tokens)
         hidden = hidden_ref[rows, :] + rows_ref[2:3, :] * num_ref[rows, :]
         normed = normalize(hidden, rows_ref[4:5, :], rows_ref[3:4, :])
-        velocity_refs[block][...] = dot(final_weight_ref[...], normed, NT)
-
-
-def finish_kernel(sizes, step_ref, levels_ref, latents_ref, *refs):
+        velocity = dot(final_weight_ref[...], normed, NT)
+        velocity_refs[block][...] = velocity
+        updated_refs[block][...] = own_latents(sizes, mine[block]) + rows_ref[7:8, :tokens] * velocity
+
+
+def finish_kernel(sizes, step_ref, levels_ref, latents_ref, noise_ref, *refs):
     frames = sizes.frames
-    arrived = refs[:frames]
-    velocity_ref, moved_ref, first_ref = refs[frames:]
+    arrived, next_ones = refs[:frames], refs[frames : 2 * frames]
+    advanced_ref, velocity_ref = refs[2 * frames :]
     own_frame = lax.rem(lax.axis_index("seq"), frames)
     for d in range(frames):
         velocity_ref[jnp.bitwise_xor(own_frame, d)] = arrived[d][...]
-    for frame in range(frames):
+    for frame in range(1, frames):
         index = step_ref[frame]
         size = levels_ref[index + 1] - levels_ref[index]
-        updated = latents_ref[frame] + size * velocity_ref[frame]
-        if frame == 0:
-            first_ref[...] = updated
-        else:
-            moved_ref[frame - 1] = updated
-    moved_ref[frames - 1] = jnp.zeros_like(first_ref)
-
-
-def kernel(function, sizes, name, ins, outs, scratch, us, smem=0):
-    spec = pl.BlockSpec(memory_space=pltpu.VMEM)
-    scalars = pl.BlockSpec(memory_space=pltpu.SMEM)
+        advanced_ref[frame - 1] = latents_ref[frame] + size * velocity_ref[frame]
+    after = next_ones[0][...]
+    for d in range(1, frames):
+        after = jnp.where(own_frame == d, next_ones[d][...], after)
+    at_end = lax.axis_index("queue") == lax.axis_size("queue") - 1
+    advanced_ref[frames - 1] = jnp.where(at_end, noise_ref[...], after)
+
+
+def kernel(function, sizes, name, places, outs, scratch, us):
+    spaces = {"v": pltpu.VMEM, "h": pltpu.HBM, "s": pltpu.SMEM}
     return pl.pallas_call(
         functools.partial(function, sizes),
         out_shape=outs,
-        in_specs=[scalars] * smem + [spec] * (ins - smem),
-        out_specs=jax.tree.map(lambda _: spec, outs),
+        in_specs=[pl.BlockSpec(memory_space=spaces[place]) for place in places],
+        out_specs=jax.tree.map(lambda _: pl.BlockSpec(memory_space=pltpu.VMEM), outs),
         scratch_shapes=scratch,
         compiler_params=pltpu.CompilerParams(vmem_limit_bytes=VMEM_LIMIT),
         cost_estimate=pl.CostEstimate(
@@ -401,22 +457,30 @@
     def over_cores(value):
         return lax.ppermute(value, "queue", [(i, i ^ 1) for i in range(queue)])
 
-    near = functools.partial(pltpu.with_memory_space_constraint, memory_space=pltpu.VMEM)
-    qkv_weight, out_weight = near(qkv_weight), near(out_weight)
+    far = functools.partial(pltpu.with_memory_space_constraint, memory_space=pltpu.HBM)
 
     payload = kernel(
-        prep_kernel, sizes, "prep", 3, pltpu.VMEM((ROWS, sizes.payload), BF16), [], 1.5
-    )(position, latents, text)
-    mine = [payload] + [swapped(payload, d) for d in range(1, frames)]
-    for group in range(1, sizes.share):
-        far = swapped(payload, group * frames)
-        mine += [far] + [swapped(far, d) for d in range(1, frames)]
-    other = [over_cores(value) for value in mine]
+        prep_kernel,
+        sizes,
+        "prep",
+        "hhh",
+        pltpu.VMEM((ROWS, sizes.payload), BF16),
+        [
+            pltpu.VMEM(latents.shape, F32),
+            pltpu.VMEM(text.shape[1:], BF16),
+            pltpu.SemaphoreType.DMA((2 + sizes.pieces,)),
+        ],
+        1.5,
+    )(far(position), far(latents), far(text))
+
+    direct = [swapped(payload, d) for d in range(1, frames)]
+    direct += [swapped(payload, group * frames) for group in range(1, sizes.share)]
+    payload_other = over_cores(payload)
 
     def blocks(count):
         return [
             pltpu.VMEM((count * tokens, width), BF16),
-            pltpu.VMEM((count, 2 * ROWS, tokens), BF16),
+            pltpu.VMEM((2 * ROWS, count * tokens), BF16),
             pltpu.VMEM((count * tokens, width), BF16),
         ]
 
@@ -424,52 +488,60 @@
         rows = count * tokens
         return [pltpu.VMEM((rows, width), BF16)] * 3 + [pltpu.VMEM((rows, width), F32)]
 
-    rows, *one = kernel(
+    rows, near_qkv, *one = kernel(
         first_kernel,
         sizes,
         "first",
-        8,
-        [pltpu.VMEM((8, width), F32)] + token_arrays(1),
-        blocks(1) + [pltpu.VMEM((tokens, 2 * width), BF16)],
+        "ssvvvvvvh",
+        [pltpu.VMEM((8, width), F32), pltpu.VMEM(qkv_weight.shape, BF16)] + token_arrays(1),
+        blocks(1) + [pltpu.VMEM((tokens, width), BF16), pltpu.SemaphoreType.DMA((3,))],
         4,
-        smem=1,
     )(
         step_index,
+        levels,
         modulation,
         q_gain[None],
         k_gain[None],
-        mine[0],
-        other[0],
+        payload,
+        payload_other,
         embed_weight,
-        qkv_weight,
-    )
+        far(qkv_weight),
+    )
+    rows, *direct = lax.optimization_barrier((rows, *direct))
+    square, far_blocks = direct[: frames - 1], direct[frames - 1 :]
+    square_other = [over_cores(value) for value in square]
+    beyond = [far_blocks] + [[swapped(v, d) for v in far_blocks] for d in range(1, frames)]
+    beyond = [beyond[d][group] for group in range(sizes.share - 1) for d in range(frames)]
     q_hat, k_hat, value, hidden = kernel(
         own_kernel,
         sizes,
         "own",
-        2 * (frames - 1) + 7,
+        "v" * (2 * (frames - 1) + 7),
         token_arrays(frames),
         blocks(frames - 1) + [pltpu.VMEM(((frames - 1) * tokens, 2 * width), BF16)],
         8,
-    )(*mine[1:frames], *other[1:frames], embed_weight, rows, qkv_weight, *one)
+    )(*square, *square_other, embed_weight, rows, near_qkv, *one)
     sums_shape = pltpu.VMEM((queries, LANES), F32)
-    num, sums = kernel(
+    num, sums, near_out = kernel(
         attend_kernel,
         sizes,
         "attend",
-        3,
-        [pltpu.VMEM((queries, width), F32), sums_shape],
-        [],
+        "vvvh",
+        [pltpu.VMEM((queries, width), F32), sums_shape, pltpu.VMEM(out_weight.shape, BF16)],
+        [pltpu.SemaphoreType.DMA],
         5,
-    )(q_hat, k_hat, value)
-    velocities = kernel(
+    )(q_hat, k_hat, value, far(out_weight))
+    num, *beyond = lax.optimization_barrier((num, *beyond))
+    mine = [payload, *square, *beyond]
+    other = [payload_other, *square_other] + [over_cores(value) for value in beyond]
+    results = kernel(
         rest_kernel,
         sizes,
         "rest",
-        2 * sizes.seq + 9,
-        [pltpu.VMEM((sizes.channels, tokens), F32)] * frames,
+        "v" * (2 * sizes.seq + 9),
+        [pltpu.VMEM((sizes.channels, tokens), F32)] * (2 * frames),
         blocks(frames)
-        + [pltpu.VMEM((queries, width), BF16)] * 3
+        + [pltpu.VMEM((queries, 2 * width), BF16), pltpu.VMEM((queries, width), BF16)]
         + [
             pltpu.VMEM((queries, width), F32),
             sums_shape,
@@ -486,32 +558,33 @@
         *other,
         embed_weight,
         rows,
-        qkv_weight,
+        near_qkv,
         q_hat,
         hidden,
         num,
         sums,
-        out_weight,
+        near_out,
         final_weight.T,
     )
 
+    velocities, updated = results[:frames], results[frames:]
+
+    def to_previous(value, d):
+        route = [
+            (q * sizes.seq + i, (q - 1) * sizes.seq + (i ^ d))
+            for q in range(1, queue)
+            for i in range(0, sizes.seq, frames)
+        ]
+        return lax.ppermute(value, ("queue", "seq"), route)
+
     arrived = [velocities[0]] + [swapped(velocities[d], d) for d in range(1, frames)]
+    next_ones = [to_previous(updated[d], d) for d in range(frames)]
     whole = jax.ShapeDtypeStruct(latents.shape, F32)
-    velocity, moved, first = kernel(
-        finish_kernel,
-        sizes,
-        "finish",
-        3 + frames,
-        [whole, whole, pltpu.VMEM(latents.shape[1:], F32)],
-        [],
-        1,
-        smem=2,
-    )(step_index, levels, latents, *arrived)
-    came = lax.ppermute(first, "queue", [(i, i - 1) for i in range(1, queue)])
-    at_end = lax.axis_index("queue") == queue - 1
-    came = jnp.where(at_end, new_noise, came)
-    advanced = lax.dynamic_update_slice_in_dim(moved, came[None], frames - 1, 0)
-    return (advanced, velocity)
+    return tuple(
+        kernel(finish_kernel, sizes, "finish", "ss" + "v" * (2 + 2 * frames), [whole, whole], [], 1)(
+            step_index, levels, latents, new_noise, *arrived, *next_ones
+        )
+    )
 
 
 def solution(mesh):

time: 75 us -> 67.6 us (0.901)
  local copies, waits for them, and re-layouts: 5.9 us -> 0.04 us
  waiting for transfers between devices: 10.9 us -> 8.93 us
  Pallas kernels: 33.6 us -> 34.5 us
    unnamed x30 -> x18, local copies, waits for them, and re-layouts: 5.9 us -> 0.04 us
    ppermute x8, starting transfers between devices: 7.74 us -> 2.7 us  [over_cores(): return lax.ppermute(value, 'queue', [(i, i ^ 1) for i in range(queue)])]
    ppermute x1 -> x4, starting transfers between devices: 3.62 us -> 7.01 us  [to_previous(): return lax.ppermute(value, ('queue', 'seq'), route)]
    ppermute x10, waiting for transfers between devices: 8.41 us -> 6.68 us  [swapped(): return lax.ppermute(value, 'seq', [(i, i ^ d) for i in range(sizes.seq)])]
    ppermute x1 -> x4, waiting for transfers between devices: 2.44 us -> 0.74 us  [to_previous(): return lax.ppermute(value, ('queue', 'seq'), route)]
    ppermute x10, starting transfers between devices: 11.5 us -> 13 us  [swapped(): return lax.ppermute(value, 'seq', [(i, i ^ d) for i in range(sizes.seq)])]
    ppermute x8, waiting for transfers between devices: 0.02 us -> 1.51 us  [over_cores(): return lax.ppermute(value, 'queue', [(i, i ^ 1) for i in range(queue)])]
    pallas_call x6, Pallas kernels: 33.6 us -> 34.5 us  [the longest x1 15.6 us: body(): kernel(rest_kernel, sizes, 'rest', 'v' * (2 * sizes.seq + 9), [pltpu.VMEM...]
  transfers between devices with their start and end apart: 19 -> 22, of which waited for: 4 -> 7; matrix products, arithmetic and copies ran while one was open for 0% -> 0% of each run, Pallas kernels for 20% -> 25%
where the time goes in v4:
time: 67.6 us; the launch traced here: 67.1 us
  Pallas kernels  34.5 us (51%)
  starting transfers between devices  22.7 us (34%)
  waiting for transfers between devices  8.93 us (13%)
  between operations  0.89 us (1%)
    pallas_call x1, Pallas kernels, body(): kernel(rest_kernel, sizes, 'rest', 'v' * (2 * sizes.seq + 9), [pltpu.VMEM...  15.6 us
    ppermute x10, starting transfers between devices, swapped(): return lax.ppermute(value, 'seq', [(i, i ^ d) for i in range(sizes.seq)])  13 us
    ppermute x4, starting transfers between devices, to_previous(): return lax.ppermute(value, ('queue', 'seq'), route)  7.01 us
    ppermute x10, waiting for transfers between devices, swapped(): return lax.ppermute(value, 'seq', [(i, i ^ d) for i in range(sizes.seq)])  6.68 us
    pallas_call x1, Pallas kernels, body(): kernel(own_kernel, sizes, 'own', 'v' * (2 * (frames - 1) + 7), token_arra...  6.26 us
    pallas_call x1, Pallas kernels, body(): kernel(first_kernel, sizes, 'first', 'ssvvvvvvh', [pltpu.VMEM((8, width),...  5.54 us
    pallas_call x1, Pallas kernels, body(): kernel(attend_kernel, sizes, 'attend', 'vvvh', [pltpu.VMEM((queries, widt...  4.87 us
    ppermute x8, starting transfers between devices, over_cores(): return lax.ppermute(value, 'queue', [(i, i ^ 1) for i in range(queue)])  2.7 us
  transfers between devices with their start and end apart: 22, of which 7 were waited for; matrix products, arithmetic and copies ran while one was open for 0% of the time, Pallas kernels for 25%

profile of v4, /device:TPU:1, one launch (start us, length us, event | category | flops | bytes accessed | tf_op | source)
XLA Modules:
  0.0 67.1 jit_solution(1874653968470584206)
XLA Ops:
  0.7 1.0 %prep.1.mine.refs_0_ = bf16[16,6784]{1,0:T(8,128)(2,1)S(1)} custom-call(bf16[128,1152]{1,0:T(8,128)(2,1)} %position_ref.1, f32[4,16,128]{2,1,0:T(8,128)} %latents_ref.3, bf16[2,144,128]{2,1,0:T(8,128)(2,1)} %bitcast.9), custom_call_target="tpu_custom_call" | custom-call | flops 1500000000 | bytes 1500000 | tf_op jit(solution)/shard_map/prep/pallas_call | solution.py:462
  1.8 2.7 %collective-permute-start.1 = (bf16[16,6784]{1,0:T(8,128)(2,1)S(1)}, bf16[16,6784]{1,0:T(8,128)(2,1)S(1)}, u32[]{:S(2)}, u32[]{:S(2)}) collective-permute-start(bf16[16,6784]{1,0:T(8,128)(2,1)S(1)} %prep.1.mine.refs_0_), channel_id=1, source_target_pairs={{0,1},{1,0},{2,3},{3,2},{4,5},{5,4},{6,7},{7,6},{8,9},{9,8},{10,11... | collective-permute-start | bytes 651272 | tf_op jit(solution)/shard_map/ppermute | solution.py:455
  4.5 1.3 %collective-permute-start.2 = (bf16[16,6784]{1,0:T(8,128)(2,1)S(1)}, bf16[16,6784]{1,0:T(8,128)(2,1)S(1)}, u32[]{:S(2)}, u32[]{:S(2)}) collective-permute-start(bf16[16,6784]{1,0:T(8,128)(2,1)S(1)} %prep.1.mine.refs_0_), channel_id=1, source_target_pairs={{0,2},{1,3},{2,0},{3,1},{4,6},{5,7},{6,4},{7,5},{8,10},{9,11},{10,... | collective-permute-start | bytes 651272 | tf_op jit(solution)/shard_map/ppermute | solution.py:455
  5.8 2.4 %collective-permute-start.4 = (bf16[16,6784]{1,0:T(8,128)(2,1)S(1)}, bf16[16,6784]{1,0:T(8,128)(2,1)S(1)}, u32[]{:S(2)}, u32[]{:S(2)}) collective-permute-start(bf16[16,6784]{1,0:T(8,128)(2,1)S(1)} %prep.1.mine.refs_0_), channel_id=1, source_target_pairs={{0,4},{1,5},{2,6},{3,7},{4,0},{5,1},{6,2},{7,3},{8,12},{9,13},{10,... | collective-permute-start | bytes 651272 | tf_op jit(solution)/shard_map/ppermute | solution.py:455
  8.3 5.5 %first.1 = (f32[8,1152]{1,0:T(8,128)S(1)}, bf16[1152,3456]{1,0:T(8,128)(2,1)S(1)}, bf16[128,1152]{1,0:T(8,128)(2,1)S(1)}, bf16[128,1152]{1,0:T(8,128)(2,1)S(1)},...) custom-call(s32[4]{0:T(128)S(1)} %copy-done.7, f32[31]{0:T(128)S(1)} %copy-done.8, f32[5,30,1152]{2,1,0:T(8,128)S(1)} %bitcast.5, ...), custom_call_target="tpu_custom_call" | custom-call | flops 4000000000 | bytes 4000000 | tf_op jit(solution)/shard_map/first/pallas_call | solution.py:491
  13.8 1.9 %collective-permute-done.2.refs_1_.refs_2_ = bf16[16,6784]{1,0:T(8,128)(2,1)S(1)} collective-permute-done((bf16[16,6784]{1,0:T(8,128)(2,1)S(1)}, bf16[16,6784]{1,0:T(8,128)(2,1)S(1)}, u32[]{:S(2)}, u32[]{:S(2)}) %collective-permute-start.2) | collective-permute-done | bytes 217120 | tf_op jit(solution)/shard_map/ppermute | solution.py:455
  15.7 4.8 %collective-permute-done.3.refs_2_.refs_3_ = bf16[16,6784]{1,0:T(8,128)(2,1)S(1)} collective-permute-done((bf16[16,6784]{1,0:T(8,128)(2,1)S(1)}, bf16[16,6784]{1,0:T(8,128)(2,1)S(1)}, u32[]{:S(2)}, u32[]{:S(2)}) %collective-permute-start.3) | collective-permute-done | bytes 217120 | tf_op jit(solution)/shard_map/ppermute | solution.py:455
  20.5 0.9 %collective-permute-start.5 = (bf16[16,6784]{1,0:T(8,128)(2,1)S(1)}, bf16[16,6784]{1,0:T(8,128)(2,1)S(1)}, u32[]{:S(2)}, u32[]{:S(2)}) collective-permute-start(bf16[16,6784]{1,0:T(8,128)(2,1)S(1)} %collective-permute-done.1.refs_0_.refs_1_), channel_id=1, source_target_pairs={{0,8},{8,0},{16,24},{24,16},{1,9},{9,1},{17,25},{25,17},{2,10},{10... | collective-permute-start | bytes 651272 | tf_op jit(solution)/shard_map/ppermute | solution.py:458
  21.8 2.5 %collective-permute-start.10 = (bf16[16,6784]{1,0:T(8,128)(2,1)S(1)}, bf16[16,6784]{1,0:T(8,128)(2,1)S(1)}, u32[]{:S(2)}, u32[]{:S(2)}) collective-permute-start(bf16[16,6784]{1,0:T(8,128)(2,1)S(1)} %collective-permute-done.4.refs_4_), channel_id=1, source_target_pairs={{0,3},{1,2},{2,1},{3,0},{4,7},{5,6},{6,5},{7,4},{8,11},{9,10},{10,... | collective-permute-start | bytes 651272 | tf_op jit(solution)/shard_map/ppermute | solution.py:455
  24.3 1.2 %collective-permute-start.8 = (bf16[16,6784]{1,0:T(8,128)(2,1)S(1)}, bf16[16,6784]{1,0:T(8,128)(2,1)S(1)}, u32[]{:S(2)}, u32[]{:S(2)}) collective-permute-start(bf16[16,6784]{1,0:T(8,128)(2,1)S(1)} %collective-permute-done.4.refs_4_), channel_id=1, source_target_pairs={{0,1},{1,0},{2,3},{3,2},{4,5},{5,4},{6,7},{7,6},{8,9},{9,8},{10,11... | collective-permute-start | bytes 651272 | tf_op jit(solution)/shard_map/ppermute | solution.py:455
  25.6 6.3 %own.1 = (bf16[512,1152]{1,0:T(8,128)(2,1)S(1)}, bf16[512,1152]{1,0:T(8,128)(2,1)S(1)}, bf16[512,1152]{1,0:T(8,128)(2,1)S(1)}, f32[512,1152]{1,0:T(8,128)S(1)}) custom-call(bf16[16,6784]{1,0:T(8,128)(2,1)S(1)} %collective-permute-done.1.refs_0_.refs_1_, bf16[16,6784]{1,0:T(8,128)(2,1)S(1)} %collective-permute-done.2.refs_1_.refs_2_, ...), custom_call_target="tpu_custom_call" | custom-call | flops 8000000000 | bytes 8000000 | tf_op jit(solution)/shard_map/own/pallas_call | solution.py:515
  31.8 4.9 %attend.1 = (f32[512,1152]{1,0:T(8,128)S(1)}, f32[512,128]{1,0:T(8,128)S(1)}, bf16[1152,1152]{1,0:T(8,128)(2,1)S(1)}) custom-call(bf16[512,1152]{1,0:T(8,128)(2,1)S(1)} %get-tuple-element.43.q_ref.refs_19_, bf16[512,1152]{1,0:T(8,128)(2,1)S(1)} %get-tuple-element.44.k_ref, bf16[512,1152]{1,0:T(8,128)(2,1)S(1)} %get-tuple-element.45.v_ref, ...), custom_call_target="tpu_custom_call" | custom-call | flops 5000000000 | bytes 5000000 | tf_op jit(solution)/shard_map/attend/pallas_call | solution.py:525
  36.7 0.6 collective-permute-start.11
  38.0 0.5 collective-permute-done.11.refs_12_
  39.5 15.6 %rest.1 = (f32[16,128]{1,0:T(8,128)S(1)}, f32[16,128]{1,0:T(8,128)S(1)}, f32[16,128]{1,0:T(8,128)S(1)}, f32[16,128]{1,0:T(8,128)S(1)}, f32[16,128]{1,0:T(8,128)S...) custom-call(bf16[16,6784]{1,0:T(8,128)(2,1)S(1)} %prep.1.mine.refs_0_, ...), custom_call_target="tpu_custom_call" | custom-call | flops 17999998976 | bytes 18000000 | tf_op jit(solution)/shard_map/rest/pallas_call | solution.py:537
  55.1 0.6 collective-permute-start.15
  55.7 1.4 %collective-permute-start.16 = (f32[16,128]{1,0:T(8,128)S(1)}, f32[16,128]{1,0:T(8,128)S(1)}, u32[]{:S(2)}, u32[]{:S(2)}) collective-permute-start(f32[16,128]{1,0:T(8,128)S(1)} %get-tuple-element.58), channel_id=1, source_target_pairs={{0,2},{1,3},{2,0},{3,1},{4,6},{5,7},{6,4},{7,5},{8,10},{9,11},{10,... | collective-permute-start | bytes 24584 | tf_op jit(solution)/shard_map/ppermute | solution.py:455
  57.1 0.9 %collective-permute-start.17 = (f32[16,128]{1,0:T(8,128)S(1)}, f32[16,128]{1,0:T(8,128)S(1)}, u32[]{:S(2)}, u32[]{:S(2)}) collective-permute-start(f32[16,128]{1,0:T(8,128)S(1)} %get-tuple-element.59), channel_id=1, source_target_pairs={{0,3},{1,2},{2,1},{3,0},{4,7},{5,6},{6,5},{7,4},{8,11},{9,10},{10,... | collective-permute-start | bytes 24584 | tf_op jit(solution)/shard_map/ppermute | solution.py:455
  58.0 2.8 %collective-permute-start.18 = (f32[16,128]{1,0:T(8,128)S(1)}, f32[16,128]{1,0:T(8,128)S(1)}, u32[]{:S(2)}, u32[]{:S(2)}) collective-permute-start(f32[16,128]{1,0:T(8,128)S(1)} %get-tuple-element.60), channel_id=1, source_target_pairs={{8,0},{12,4},{16,8},{20,12},{24,16},{28,20}} | collective-permute-start | bytes 24584 | tf_op jit(solution)/shard_map/ppermute | solution.py:578
  60.8 1.3 %collective-permute-start.19 = (f32[16,128]{1,0:T(8,128)S(1)}, f32[16,128]{1,0:T(8,128)S(1)}, u32[]{:S(2)}, u32[]{:S(2)}) collective-permute-start(f32[16,128]{1,0:T(8,128)S(1)} %get-tuple-element.61), channel_id=1, source_target_pairs={{8,1},{12,5},{16,9},{20,13},{24,17},{28,21}} | collective-permute-start | bytes 24584 | tf_op jit(solution)/shard_map/ppermute | solution.py:578
  62.1 1.6 %collective-permute-start.20 = (f32[16,128]{1,0:T(8,128)S(1)}, f32[16,128]{1,0:T(8,128)S(1)}, u32[]{:S(2)}, u32[]{:S(2)}) collective-permute-start(f32[16,128]{1,0:T(8,128)S(1)} %get-tuple-element.62), channel_id=1, source_target_pairs={{8,2},{12,6},{16,10},{20,14},{24,18},{28,22}} | collective-permute-start | bytes 24584 | tf_op jit(solution)/shard_map/ppermute | solution.py:578
  63.8 1.3 %collective-permute-start.21 = (f32[16,128]{1,0:T(8,128)S(1)}, f32[16,128]{1,0:T(8,128)S(1)}, u32[]{:S(2)}, u32[]{:S(2)}) collective-permute-start(f32[16,128]{1,0:T(8,128)S(1)} %get-tuple-element.63), channel_id=1, source_target_pairs={{8,3},{12,7},{16,11},{20,15},{24,19},{28,23}} | collective-permute-start | bytes 24584 | tf_op jit(solution)/shard_map/ppermute | solution.py:578
  65.1 0.7 %collective-permute-done.21.refs_7_ = f32[16,128]{1,0:T(8,128)S(1)} collective-permute-done((f32[16,128]{1,0:T(8,128)S(1)}, f32[16,128]{1,0:T(8,128)S(1)}, u32[]{:S(2)}, u32[]{:S(2)}) %collective-permute-start.21) | collective-permute-done | bytes 8224 | tf_op jit(solution)/shard_map/ppermute | solution.py:578
  65.9 1.2 %finish.1 = (f32[4,16,128]{2,1,0:T(8,128)}, f32[4,16,128]{2,1,0:T(8,128)}) custom-call(s32[4]{0:T(128)S(1)} %copy-done.7, f32[31]{0:T(128)S(1)} %copy-done.8, f32[4,16,128]{2,1,0:T(8,128)S(1)} %copy-done.3, f32[16,128]{1,0:T(8,128)S(1)} %copy-done.4, f32[16,128]{1,0:T(8,128)S(1)} %get-tuple-element.56.refs_0_, ...), custom_call_target="tpu_custom_call" | custom-call | flops 1000000000 | bytes 1000000 | tf_op jit(solution)/shard_map/finish/pallas_call | solution.py:584
  (44 shorter events, 2.3 us)
Async XLA Ops:
  1.7 6.5 %collective-permute-start = (bf16[16,6784]{1,0:T(8,128)(2,1)S(1)}, bf16[16,6784]{1,0:T(8,128)(2,1)S(1)}, u32[]{:S(2)}, u32[]{:S(2)}) collective-permute-start(bf16[16,6784]{1,0:T(8,128)(2,1)S(1)} %prep.1.mine.refs_0_), channel_id=1, source_target_pairs={{0,8},{8,0},{16,24},{24,16},{1,9},{9,1},{17,25},{25,17},{2,10},{10... | collective-permute-start | bytes 651272 | tf_op jit(solution)/shard_map/ppermute | solution.py:458
  1.8 12.0 %collective-permute-start.1 = (bf16[16,6784]{1,0:T(8,128)(2,1)S(1)}, bf16[16,6784]{1,0:T(8,128)(2,1)S(1)}, u32[]{:S(2)}, u32[]{:S(2)}) collective-permute-start(bf16[16,6784]{1,0:T(8,128)(2,1)S(1)} %prep.1.mine.refs_0_), channel_id=1, source_target_pairs={{0,1},{1,0},{2,3},{3,2},{4,5},{5,4},{6,7},{7,6},{8,9},{9,8},{10,11... | collective-permute-start | bytes 651272 | tf_op jit(solution)/shard_map/ppermute | solution.py:455
  4.5 11.2 %collective-permute-start.2 = (bf16[16,6784]{1,0:T(8,128)(2,1)S(1)}, bf16[16,6784]{1,0:T(8,128)(2,1)S(1)}, u32[]{:S(2)}, u32[]{:S(2)}) collective-permute-start(bf16[16,6784]{1,0:T(8,128)(2,1)S(1)} %prep.1.mine.refs_0_), channel_id=1, source_target_pairs={{0,2},{1,3},{2,0},{3,1},{4,6},{5,7},{6,4},{7,5},{8,10},{9,11},{10,... | collective-permute-start | bytes 651272 | tf_op jit(solution)/shard_map/ppermute | solution.py:455
  5.8 14.7 %collective-permute-start.3 = (bf16[16,6784]{1,0:T(8,128)(2,1)S(1)}, bf16[16,6784]{1,0:T(8,128)(2,1)S(1)}, u32[]{:S(2)}, u32[]{:S(2)}) collective-permute-start(bf16[16,6784]{1,0:T(8,128)(2,1)S(1)} %prep.1.mine.refs_0_), channel_id=1, source_target_pairs={{0,3},{1,2},{2,1},{3,0},{4,7},{5,6},{6,5},{7,4},{8,11},{9,10},{10,... | collective-permute-start | bytes 651272 | tf_op jit(solution)/shard_map/ppermute | solution.py:455
  5.8 14.7 %collective-permute-start.4 = (bf16[16,6784]{1,0:T(8,128)(2,1)S(1)}, bf16[16,6784]{1,0:T(8,128)(2,1)S(1)}, u32[]{:S(2)}, u32[]{:S(2)}) collective-permute-start(bf16[16,6784]{1,0:T(8,128)(2,1)S(1)} %prep.1.mine.refs_0_), channel_id=1, source_target_pairs={{0,4},{1,5},{2,6},{3,7},{4,0},{5,1},{6,2},{7,3},{8,12},{9,13},{10,... | collective-permute-start | bytes 651272 | tf_op jit(solution)/shard_map/ppermute | solution.py:455
  20.5 5.0 %collective-permute-start.5 = (bf16[16,6784]{1,0:T(8,128)(2,1)S(1)}, bf16[16,6784]{1,0:T(8,128)(2,1)S(1)}, u32[]{:S(2)}, u32[]{:S(2)}) collective-permute-start(bf16[16,6784]{1,0:T(8,128)(2,1)S(1)} %collective-permute-done.1.refs_0_.refs_1_), channel_id=1, source_target_pairs={{0,8},{8,0},{16,24},{24,16},{1,9},{9,1},{17,25},{25,17},{2,10},{10... | collective-permute-start | bytes 651272 | tf_op jit(solution)/shard_map/ppermute | solution.py:458
  21.3 4.2 %collective-permute-start.6 = (bf16[16,6784]{1,0:T(8,128)(2,1)S(1)}, bf16[16,6784]{1,0:T(8,128)(2,1)S(1)}, u32[]{:S(2)}, u32[]{:S(2)}) collective-permute-start(bf16[16,6784]{1,0:T(8,128)(2,1)S(1)} %collective-permute-done.2.refs_1_.refs_2_), channel_id=1, source_target_pairs={{0,8},{8,0},{16,24},{24,16},{1,9},{9,1},{17,25},{25,17},{2,10},{10... | collective-permute-start | bytes 651272 | tf_op jit(solution)/shard_map/ppermute | solution.py:458
  21.3 4.2 %collective-permute-start.7 = (bf16[16,6784]{1,0:T(8,128)(2,1)S(1)}, bf16[16,6784]{1,0:T(8,128)(2,1)S(1)}, u32[]{:S(2)}, u32[]{:S(2)}) collective-permute-start(bf16[16,6784]{1,0:T(8,128)(2,1)S(1)} %collective-permute-done.3.refs_2_.refs_3_), channel_id=1, source_target_pairs={{0,8},{8,0},{16,24},{24,16},{1,9},{9,1},{17,25},{25,17},{2,10},{10... | collective-permute-start | bytes 651272 | tf_op jit(solution)/shard_map/ppermute | solution.py:458
  21.8 14.9 %collective-permute-start.10 = (bf16[16,6784]{1,0:T(8,128)(2,1)S(1)}, bf16[16,6784]{1,0:T(8,128)(2,1)S(1)}, u32[]{:S(2)}, u32[]{:S(2)}) collective-permute-start(bf16[16,6784]{1,0:T(8,128)(2,1)S(1)} %collective-permute-done.4.refs_4_), channel_id=1, source_target_pairs={{0,3},{1,2},{2,1},{3,0},{4,7},{5,6},{6,5},{7,4},{8,11},{9,10},{10,... | collective-permute-start | bytes 651272 | tf_op jit(solution)/shard_map/ppermute | solution.py:455
  24.3 12.4 %collective-permute-start.8 = (bf16[16,6784]{1,0:T(8,128)(2,1)S(1)}, bf16[16,6784]{1,0:T(8,128)(2,1)S(1)}, u32[]{:S(2)}, u32[]{:S(2)}) collective-permute-start(bf16[16,6784]{1,0:T(8,128)(2,1)S(1)} %collective-permute-done.4.refs_4_), channel_id=1, source_target_pairs={{0,1},{1,0},{2,3},{3,2},{4,5},{5,4},{6,7},{7,6},{8,9},{9,8},{10,11... | collective-permute-start | bytes 651272 | tf_op jit(solution)/shard_map/ppermute | solution.py:455
  25.5 11.2 %collective-permute-start.9 = (bf16[16,6784]{1,0:T(8,128)(2,1)S(1)}, bf16[16,6784]{1,0:T(8,128)(2,1)S(1)}, u32[]{:S(2)}, u32[]{:S(2)}) collective-permute-start(bf16[16,6784]{1,0:T(8,128)(2,1)S(1)} %collective-permute-done.4.refs_4_), channel_id=1, source_target_pairs={{0,2},{1,3},{2,0},{3,1},{4,6},{5,7},{6,4},{7,5},{8,10},{9,11},{10,... | collective-permute-start | bytes 651272 | tf_op jit(solution)/shard_map/ppermute | solution.py:455
  36.7 1.7 %collective-permute-start.11 = (bf16[16,6784]{1,0:T(8,128)(2,1)S(1)}, bf16[16,6784]{1,0:T(8,128)(2,1)S(1)}, u32[]{:S(2)}, u32[]{:S(2)}) collective-permute-start(bf16[16,6784]{1,0:T(8,128)(2,1)S(1)} %collective-permute-done.4.refs_4_), channel_id=1, source_target_pairs={{0,8},{8,0},{16,24},{24,16},{1,9},{9,1},{17,25},{25,17},{2,10},{10... | collective-permute-start | bytes 651272 | tf_op jit(solution)/shard_map/ppermute | solution.py:458
  37.4 1.5 %collective-permute-start.12 = (bf16[16,6784]{1,0:T(8,128)(2,1)S(1)}, bf16[16,6784]{1,0:T(8,128)(2,1)S(1)}, u32[]{:S(2)}, u32[]{:S(2)}) collective-permute-start(bf16[16,6784]{1,0:T(8,128)(2,1)S(1)} %collective-permute-done.8.refs_5_), channel_id=1, source_target_pairs={{0,8},{8,0},{16,24},{24,16},{1,9},{9,1},{17,25},{25,17},{2,10},{10... | collective-permute-start | bytes 651272 | tf_op jit(solution)/shard_map/ppermute | solution.py:458
  37.5 1.7 %collective-permute-start.13 = (bf16[16,6784]{1,0:T(8,128)(2,1)S(1)}, bf16[16,6784]{1,0:T(8,128)(2,1)S(1)}, u32[]{:S(2)}, u32[]{:S(2)}) collective-permute-start(bf16[16,6784]{1,0:T(8,128)(2,1)S(1)} %collective-permute-done.9.refs_6_), channel_id=1, source_target_pairs={{0,8},{8,0},{16,24},{24,16},{1,9},{9,1},{17,25},{25,17},{2,10},{10... | collective-permute-start | bytes 651272 | tf_op jit(solution)/shard_map/ppermute | solution.py:458
  37.9 1.6 %collective-permute-start.14 = (bf16[16,6784]{1,0:T(8,128)(2,1)S(1)}, bf16[16,6784]{1,0:T(8,128)(2,1)S(1)}, u32[]{:S(2)}, u32[]{:S(2)}) collective-permute-start(bf16[16,6784]{1,0:T(8,128)(2,1)S(1)} %collective-permute-done.10.refs_7_), channel_id=1, source_target_pairs={{0,8},{8,0},{16,24},{24,16},{1,9},{9,1},{17,25},{25,17},{2,10},{10... | collective-permute-start | bytes 651272 | tf_op jit(solution)/shard_map/ppermute | solution.py:458
  39.5 26.4 %copy-start.3 = (f32[4,16,128]{2,1,0:T(8,128)S(1)}, f32[4,16,128]{2,1,0:T(8,128)}, u32[]{:S(2)}) copy-start(f32[4,16,128]{2,1,0:T(8,128)} %latents_ref.3) | copy-start | bytes 98308
  39.5 26.4 %copy-start.4 = (f32[16,128]{1,0:T(8,128)S(1)}, f32[16,128]{1,0:T(8,128)}, u32[]{:S(2)}) copy-start(f32[16,128]{1,0:T(8,128)} %noise_ref.1) | copy-start | bytes 24580
  55.1 7.0 %collective-permute-start.15 = (f32[16,128]{1,0:T(8,128)S(1)}, f32[16,128]{1,0:T(8,128)S(1)}, u32[]{:S(2)}, u32[]{:S(2)}) collective-permute-start(f32[16,128]{1,0:T(8,128)S(1)} %get-tuple-element.57), channel_id=1, source_target_pairs={{0,1},{1,0},{2,3},{3,2},{4,5},{5,4},{6,7},{7,6},{8,9},{9,8},{10,11... | collective-permute-start | bytes 24584 | tf_op jit(solution)/shard_map/ppermute | solution.py:455
  55.7 8.1 %collective-permute-start.16 = (f32[16,128]{1,0:T(8,128)S(1)}, f32[16,128]{1,0:T(8,128)S(1)}, u32[]{:S(2)}, u32[]{:S(2)}) collective-permute-start(f32[16,128]{1,0:T(8,128)S(1)} %get-tuple-element.58), channel_id=1, source_target_pairs={{0,2},{1,3},{2,0},{3,1},{4,6},{5,7},{6,4},{7,5},{8,10},{9,11},{10,... | collective-permute-start | bytes 24584 | tf_op jit(solution)/shard_map/ppermute | solution.py:455
  57.1 8.0 %collective-permute-start.17 = (f32[16,128]{1,0:T(8,128)S(1)}, f32[16,128]{1,0:T(8,128)S(1)}, u32[]{:S(2)}, u32[]{:S(2)}) collective-permute-start(f32[16,128]{1,0:T(8,128)S(1)} %get-tuple-element.59), channel_id=1, source_target_pairs={{0,3},{1,2},{2,1},{3,0},{4,7},{5,6},{6,5},{7,4},{8,11},{9,10},{10,... | collective-permute-start | bytes 24584 | tf_op jit(solution)/shard_map/ppermute | solution.py:455
  58.0 7.1 %collective-permute-start.18 = (f32[16,128]{1,0:T(8,128)S(1)}, f32[16,128]{1,0:T(8,128)S(1)}, u32[]{:S(2)}, u32[]{:S(2)}) collective-permute-start(f32[16,128]{1,0:T(8,128)S(1)} %get-tuple-element.60), channel_id=1, source_target_pairs={{8,0},{12,4},{16,8},{20,12},{24,16},{28,20}} | collective-permute-start | bytes 24584 | tf_op jit(solution)/shard_map/ppermute | solution.py:578
  60.8 4.3 %collective-permute-start.19 = (f32[16,128]{1,0:T(8,128)S(1)}, f32[16,128]{1,0:T(8,128)S(1)}, u32[]{:S(2)}, u32[]{:S(2)}) collective-permute-start(f32[16,128]{1,0:T(8,128)S(1)} %get-tuple-element.61), channel_id=1, source_target_pairs={{8,1},{12,5},{16,9},{20,13},{24,17},{28,21}} | collective-permute-start | bytes 24584 | tf_op jit(solution)/shard_map/ppermute | solution.py:578
  62.1 3.0 %collective-permute-start.20 = (f32[16,128]{1,0:T(8,128)S(1)}, f32[16,128]{1,0:T(8,128)S(1)}, u32[]{:S(2)}, u32[]{:S(2)}) collective-permute-start(f32[16,128]{1,0:T(8,128)S(1)} %get-tuple-element.62), channel_id=1, source_target_pairs={{8,2},{12,6},{16,10},{20,14},{24,18},{28,22}} | collective-permute-start | bytes 24584 | tf_op jit(solution)/shard_map/ppermute | solution.py:578
  63.8 2.1 %collective-permute-start.21 = (f32[16,128]{1,0:T(8,128)S(1)}, f32[16,128]{1,0:T(8,128)S(1)}, u32[]{:S(2)}, u32[]{:S(2)}) collective-permute-start(f32[16,128]{1,0:T(8,128)S(1)} %get-tuple-element.63), channel_id=1, source_target_pairs={{8,3},{12,7},{16,11},{20,15},{24,19},{28,23}} | collective-permute-start | bytes 24584 | tf_op jit(solution)/shard_map/ppermute | solution.py:578
  (7 other events, 53.1 us)

commit v5 on v4

--- a/solution.py
+++ b/solution.py
@@ -45,11 +45,11 @@
         self.latents_at = self.pieces * self.width
         self.text_at = self.latents_at + 2 * self.frames * self.tokens
         self.payload = self.text_at + self.text_pieces * self.text_len
-
-
-def prep_kernel(
-    sizes, position_ref, latents_ref, text_ref, payload_ref, latents_scr, text_scr, sems
-):
+        self.near = self.latents_at + 2 * self.tokens
+
+
+def prep_kernel(sizes, position_ref, latents_ref, text_ref, payload_ref, tail_ref, *refs):
+    near_refs, (latents_scr, text_scr, sems) = refs[:-3], refs[-3:]
     core = lax.rem(lax.axis_index("queue"), 2)
     width, tokens = sizes.width, sizes.tokens
     copies = [
@@ -82,38 +82,49 @@
             rows = jnp.concatenate([rows, blank], axis=0)
         at = sizes.text_at + piece * sizes.text_len
         payload_ref[:, at : at + sizes.text_len] = rows
+        tail_ref[:, piece * sizes.text_len : (piece + 1) * sizes.text_len] = rows
     for copy in copies[2:]:
         copy.wait()
+    own_frame = lax.rem(lax.axis_index("seq"), sizes.frames)
+    base = sizes.latents_at
+    for d, near_ref in enumerate(near_refs, 1):
+        near_ref[:, :base] = payload_ref[:, :base]
+        at = base + 2 * tokens * jnp.bitwise_xor(own_frame, d)
+        near_ref[:, base:] = payload_ref[:, pl.ds(pl.multiple_of(at, LANES), 2 * tokens)]
+
+
+def join_kernel(sizes, far_ref, tail_ref, joined_ref):
+    joined_ref[:, : sizes.payload] = far_ref[...]
+    joined_ref[:, sizes.payload :] = tail_ref[...]
+
+
+def frame_latents(sizes, mine_ref):
+    if mine_ref.shape[1] == sizes.near:
+        return mine_ref[:, sizes.latents_at :]
+    frame = lax.rem(lax.axis_index("seq"), sizes.frames)
+    at = pl.multiple_of(sizes.latents_at + 2 * frame * sizes.tokens, LANES)
+    return mine_ref[:, pl.ds(at, 2 * sizes.tokens)]
 
 
 def unpack(sizes, block, mine_ref, other_ref, position_scr, latents_scr):
     width, tokens = sizes.width, sizes.tokens
     core = lax.rem(lax.axis_index("queue"), 2)
-    frame = lax.rem(lax.axis_index("seq"), sizes.frames)
     for ref, place in ((mine_ref, core), (other_ref, 1 - core)):
         for piece in range(sizes.pieces):
             start = pl.multiple_of(block * tokens + place * sizes.half + piece * ROWS, ROWS)
             position_scr[pl.ds(start, ROWS), :] = ref[:, piece * width : (piece + 1) * width]
-    at = pl.multiple_of(sizes.latents_at + 2 * frame * tokens, LANES)
-    both = mine_ref[:, pl.ds(at, 2 * tokens)]
+    both = frame_latents(sizes, mine_ref)
     lanes = slice(block * tokens, (block + 1) * tokens)
     latents_scr[0:ROWS, lanes] = both[:, :tokens]
     latents_scr[ROWS : 2 * ROWS, lanes] = both[:, tokens:]
 
 
-def own_latents(sizes, mine_ref):
-    frame = lax.rem(lax.axis_index("seq"), sizes.frames)
-    at = pl.multiple_of(sizes.latents_at + 2 * frame * sizes.tokens, LANES)
-    both = mine_ref[:, pl.ds(at, 2 * sizes.tokens)].astype(F32)
-    return both[:, : sizes.tokens] + both[:, sizes.tokens :]
-
-
-def unpack_text(sizes, shard, mine_ref, other_ref, text_scr):
+def unpack_text(sizes, shard, mine_ref, other_ref, base, text_scr):
     core = lax.rem(lax.axis_index("queue"), 2)
     for ref, place in ((mine_ref, core), (other_ref, 1 - core)):
         for piece in range(sizes.text_pieces):
             first, last = piece * ROWS, min((piece + 1) * ROWS, sizes.part)
-            at = sizes.text_at + piece * sizes.text_len
+            at = base + piece * sizes.text_len
             rows = ref[:, at : at + sizes.text_len].astype(F32)
             start = pl.multiple_of(shard * sizes.part + first, 8)
             text_scr[place, pl.ds(start, last - first), :] = rows[: last - first]
@@ -192,6 +203,7 @@
 def attend_self(sizes, q_ref, k_ref, v_ref, num_ref, sum_ref, fresh, q_step=512):
     queries, width = q_ref.shape
     keys = k_ref.shape[0]
+    q_step = min(q_step, queries)
     for q_start in range(0, queries, q_step):
         rows = slice(q_start, q_start + q_step)
         sums = jnp.zeros((q_step, LANES), F32)
@@ -329,47 +341,75 @@
     )
 
 
-def attend_kernel(
-    sizes, q_ref, k_ref, v_ref, out_weight_ref, num_ref, sum_ref, near_ref, sem
-):
+def attend_kernel(sizes, q_ref, k_ref, v_ref, out_weight_ref, num_ref, sum_ref, near_ref, sem):
     copy = pltpu.make_async_copy(out_weight_ref, near_ref, sem)
     copy.start()
     attend_self(sizes, q_ref, k_ref, v_ref, num_ref, sum_ref, True)
     copy.wait()
 
 
+def far_kernel(sizes, *refs):
+    count, width = sizes.share - 1, sizes.width
+    mine, other = refs[:count], refs[count : 2 * count]
+    (
+        embed_ref, rows_ref, weight_ref, k_ref, v_ref,
+        position_scr, latents_scr, normed_scr, proj_scr,
+    ) = refs[2 * count :]
+    for block in range(count):
+        unpack(sizes, block, mine[block], other[block], position_scr, latents_scr)
+    embed_blocks(
+        sizes, count, position_scr, latents_scr, embed_ref, rows_ref, normed_scr, None
+    )
+    project(normed_scr, weight_ref, width, 2 * width, proj_scr)
+    norm_rows(sizes, proj_scr, k_ref, rows_ref[6:7, :], head_sums(sizes), head_spread(sizes))
+    project(normed_scr, weight_ref, 2 * width, 3 * width, v_ref)
+
+
 def rest_kernel(sizes, *refs):
     frames, share, width, tokens = sizes.frames, sizes.share, sizes.width, sizes.tokens
-    count = frames * share
+    count = frames * (share - 1)
     mine, other = refs[:count], refs[count : 2 * count]
+    refs = refs[2 * count :]
+    payload_ref, payload_other_ref = refs[:2]
+    square = refs[2 : 1 + frames]
     (
         embed_ref, rows_ref, weight_ref, q_ref, hidden_ref, num_in_ref, sum_in_ref,
-        out_weight_ref, final_weight_ref,
-    ) = refs[2 * count : 2 * count + 9]
-    velocity_refs = refs[2 * count + 9 : 2 * count + 9 + frames]
-    updated_refs = refs[2 * count + 9 + frames : 2 * count + 9 + 2 * frames]
+        out_weight_ref, final_weight_ref, far_k_ref, far_v_ref,
+    ) = refs[1 + frames : 12 + frames]
+    refs = refs[12 + frames :]
+    velocity_refs = refs[:frames]
+    updated_refs = refs[frames : 2 * frames]
     (
-        position_scr, latents_scr, normed_scr, proj_scr, k_scr, num_ref, sum_ref,
+        position_scr, latents_scr, normed_scr, proj_scr, k_scr, v_scr, num_ref, sum_ref,
         text_scr, tk_scr, tv_scr, tnum_scr, tsum_scr, attention_scr,
-    ) = refs[2 * count + 9 + 2 * frames :]
+    ) = refs[2 * frames :]
     sums_matrix, spread_matrix = head_sums(sizes), head_spread(sizes)
     num_ref[...] = num_in_ref[...]
     sum_ref[...] = sum_in_ref[...]
-    for group in range(1, share):
-        for block in range(frames):
+    for group in range(share - 1):
+        first = slice(group * tokens, (group + 1) * tokens)
+        k_scr[:tokens, :] = far_k_ref[first, :]
+        v_scr[:tokens, :] = far_v_ref[first, :]
+        for block in range(1, frames):
             at = group * frames + block
-            unpack(sizes, block, mine[at], other[at], position_scr, latents_scr)
+            unpack(sizes, block - 1, mine[at], other[at], position_scr, latents_scr)
         embed_blocks(
-            sizes, frames, position_scr, latents_scr, embed_ref, rows_ref, normed_scr, None
+            sizes, frames - 1, position_scr, latents_scr, embed_ref, rows_ref, normed_scr, None
         )
-        project(normed_scr, weight_ref, width, 3 * width, proj_scr)
-        keys, values = proj_scr.at[:, :width], proj_scr.at[:, width:]
-        norm_rows(sizes, keys, k_scr, rows_ref[6:7, :], sums_matrix, spread_matrix)
-        attend_self(sizes, q_ref, k_scr, values, num_ref, sum_ref, False)
+        project(normed_scr, weight_ref, width, 2 * width, proj_scr)
+        project(normed_scr, weight_ref, 2 * width, 3 * width, v_scr.at[tokens:, :])
+        keys = k_scr.at[tokens:, :]
+        norm_rows(sizes, proj_scr, keys, rows_ref[6:7, :], sums_matrix, spread_matrix)
+        attend_self(sizes, q_ref, k_scr, v_scr, num_ref, sum_ref, False)
 
     place = lax.axis_index("seq")
+    unpack_text(sizes, place, payload_ref, payload_other_ref, sizes.text_at, text_scr)
+    for d in range(1, frames):
+        shard = jnp.bitwise_xor(place, d)
+        unpack_text(sizes, shard, mine[d], other[d], sizes.payload, text_scr)
     for at in range(count):
-        unpack_text(sizes, jnp.bitwise_xor(place, at), mine[at], other[at], text_scr)
+        shard = jnp.bitwise_xor(place, frames + at)
+        unpack_text(sizes, shard, mine[at], other[at], sizes.text_at, text_scr)
     gain_column = jnp.transpose(jnp.broadcast_to(rows_ref[6:7, :], (LANES, width)))[:, 0:1]
     for h in range(sizes.heads):
         rows = slice(h * sizes.head, (h + 1) * sizes.head)
@@ -393,7 +433,9 @@
         normed = normalize(hidden, rows_ref[4:5, :], rows_ref[3:4, :])
         velocity = dot(final_weight_ref[...], normed, NT)
         velocity_refs[block][...] = velocity
-        updated_refs[block][...] = own_latents(sizes, mine[block]) + rows_ref[7:8, :tokens] * velocity
+        both = frame_latents(sizes, square[block - 1] if block else payload_ref).astype(F32)
+        before = both[:, :tokens] + both[:, tokens:]
+        updated_refs[block][...] = before + rows_ref[7:8, :tokens] * velocity
 
 
 def finish_kernel(sizes, step_ref, levels_ref, latents_ref, noise_ref, *refs):
@@ -459,12 +501,16 @@
 
     far = functools.partial(pltpu.with_memory_space_constraint, memory_space=pltpu.HBM)
 
-    payload = kernel(
+    payload, tail, *near = kernel(
         prep_kernel,
         sizes,
         "prep",
         "hhh",
-        pltpu.VMEM((ROWS, sizes.payload), BF16),
+        [
+            pltpu.VMEM((ROWS, sizes.payload), BF16),
+            pltpu.VMEM((ROWS, sizes.payload - sizes.text_at), BF16),
+        ]
+        + [pltpu.VMEM((ROWS, sizes.near), BF16)] * (frames - 1),
         [
             pltpu.VMEM(latents.shape, F32),
             pltpu.VMEM(text.shape[1:], BF16),
@@ -473,9 +519,12 @@
         1.5,
     )(far(position), far(latents), far(text))
 
-    direct = [swapped(payload, d) for d in range(1, frames)]
-    direct += [swapped(payload, group * frames) for group in range(1, sizes.share)]
+    order = sorted(range(1, frames), key=lambda d: (d.bit_count() - 2 * (d >= frames // 2), d))
+    sent = {d: swapped(near[d - 1], d) for d in order}
+    direct = [sent[d] for d in range(1, frames)]
     payload_other = over_cores(payload)
+    late, payload_other = lax.optimization_barrier((payload, payload_other))
+    direct += [swapped(late, group * frames) for group in range(1, sizes.share)]
 
     def blocks(count):
         return [
@@ -510,8 +559,21 @@
     rows, *direct = lax.optimization_barrier((rows, *direct))
     square, far_blocks = direct[: frames - 1], direct[frames - 1 :]
     square_other = [over_cores(value) for value in square]
-    beyond = [far_blocks] + [[swapped(v, d) for v in far_blocks] for d in range(1, frames)]
-    beyond = [beyond[d][group] for group in range(sizes.share - 1) for d in range(frames)]
+    far_other = [over_cores(value) for value in far_blocks]
+    joined = [
+        kernel(
+            join_kernel,
+            sizes,
+            "join",
+            "vv",
+            pltpu.VMEM((ROWS, 2 * sizes.payload - sizes.text_at), BF16),
+            [],
+            0.3,
+        )(value, tail)
+        for value in far_blocks
+    ]
+    forwarded = [[swapped(value, d) for d in range(1, frames)] for value in joined]
+    forwarded = sum(forwarded, [])
     q_hat, k_hat, value, hidden = kernel(
         own_kernel,
         sizes,
@@ -521,41 +583,62 @@
         blocks(frames - 1) + [pltpu.VMEM(((frames - 1) * tokens, 2 * width), BF16)],
         8,
     )(*square, *square_other, embed_weight, rows, near_qkv, *one)
-    sums_shape = pltpu.VMEM((queries, LANES), F32)
     num, sums, near_out = kernel(
         attend_kernel,
         sizes,
         "attend",
         "vvvh",
-        [pltpu.VMEM((queries, width), F32), sums_shape, pltpu.VMEM(out_weight.shape, BF16)],
+        [
+            pltpu.VMEM((queries, width), F32),
+            pltpu.VMEM((queries, LANES), F32),
+            pltpu.VMEM(out_weight.shape, BF16),
+        ],
         [pltpu.SemaphoreType.DMA],
         5,
     )(q_hat, k_hat, value, far(out_weight))
-    num, *beyond = lax.optimization_barrier((num, *beyond))
-    mine = [payload, *square, *beyond]
-    other = [payload_other, *square_other] + [over_cores(value) for value in beyond]
+    num, rows_late, *forwarded = lax.optimization_barrier((num, rows, *forwarded))
+    forwarded_other = [over_cores(value) for value in forwarded]
+    far_rows = (sizes.share - 1) * tokens
+    far_k, far_v = kernel(
+        far_kernel,
+        sizes,
+        "far",
+        "v" * (2 * len(far_blocks) + 3),
+        [pltpu.VMEM((far_rows, width), BF16)] * 2,
+        blocks(sizes.share - 1) + [pltpu.VMEM((far_rows, width), BF16)],
+        2.5,
+    )(*far_blocks, *far_other, embed_weight, rows_late, near_qkv)
+    mine, other = [], []
+    for group in range(sizes.share - 1):
+        here = slice(group * (frames - 1), (group + 1) * (frames - 1))
+        mine += [far_blocks[group], *forwarded[here]]
+        other += [far_other[group], *forwarded_other[here]]
     results = kernel(
         rest_kernel,
         sizes,
         "rest",
-        "v" * (2 * sizes.seq + 9),
+        "v" * (2 * len(mine) + 12 + frames),
         [pltpu.VMEM((sizes.channels, tokens), F32)] * (2 * frames),
-        blocks(frames)
-        + [pltpu.VMEM((queries, 2 * width), BF16), pltpu.VMEM((queries, width), BF16)]
+        blocks(frames - 1)
+        + [pltpu.VMEM(((frames - 1) * tokens, width), BF16)]
+        + [pltpu.VMEM((queries, width), BF16)] * 2
         + [
             pltpu.VMEM((queries, width), F32),
-            sums_shape,
+            pltpu.VMEM((queries, LANES), F32),
             pltpu.VMEM((2, width, sizes.text_len), F32),
             pltpu.VMEM((width, sizes.text_len), BF16),
             pltpu.VMEM((width, sizes.text_len), BF16),
             pltpu.VMEM((queries, width), F32),
-            sums_shape,
+            pltpu.VMEM((queries, LANES), F32),
             pltpu.VMEM((queries, width), BF16),
         ],
         18,
     )(
         *mine,
         *other,
+        payload,
+        payload_other,
+        *square,
         embed_weight,
         rows,
         near_qkv,
@@ -565,6 +648,8 @@
         sums,
         near_out,
         final_weight.T,
+        far_k,
+        far_v,
     )
 
     velocities, updated = results[:frames], results[frames:]

time: 67.6 us -> 65.2 us (0.964)
  waiting for transfers between devices: 8.93 us -> 4.84 us
  Pallas kernels: 34.5 us -> 35.6 us
    ppermute x10, waiting for transfers between devices: 6.68 us -> 4.08 us  [swapped(): return lax.ppermute(value, 'seq', [(i, i ^ d) for i in range(sizes.seq)])]
    ppermute x8, waiting for transfers between devices: 1.51 us -> 0.02 us  [over_cores(): return lax.ppermute(value, 'queue', [(i, i ^ 1) for i in range(queue)])]
    pallas_call x2 -> x4, Pallas kernels: 16.6 us -> 17.8 us  [the longest x1 14.7 us: body(): kernel(rest_kernel, sizes, 'rest', 'v' * (2 * len(mine) + 12 + frames), [...]
  transfers between devices with their start and end apart: 22 -> 22, of which waited for: 7 -> 3; matrix products, arithmetic and copies ran while one was open for 0% -> 0% of each run, Pallas kernels for 25% -> 29%
where the time goes in v5:
time: 65.2 us; the launch traced here: 64.4 us
  Pallas kernels  35.6 us (55%)
  starting transfers between devices  22.9 us (35%)
  waiting for transfers between devices  4.84 us (7%)
  between operations  0.92 us (1%)
    pallas_call x1, Pallas kernels, body(): kernel(rest_kernel, sizes, 'rest', 'v' * (2 * len(mine) + 12 + frames), [...  14.7 us
    ppermute x10, starting transfers between devices, swapped(): return lax.ppermute(value, 'seq', [(i, i ^ d) for i in range(sizes.seq)])  12.9 us
    ppermute x4, starting transfers between devices, to_previous(): return lax.ppermute(value, ('queue', 'seq'), route)  6.77 us
    pallas_call x1, Pallas kernels, body(): kernel(own_kernel, sizes, 'own', 'v' * (2 * (frames - 1) + 7), token_arra...  6.29 us
    pallas_call x1, Pallas kernels, body(): kernel(first_kernel, sizes, 'first', 'ssvvvvvvh', [pltpu.VMEM((8, width),...  5.52 us
    pallas_call x1, Pallas kernels, body(): kernel(attend_kernel, sizes, 'attend', 'vvvh', [pltpu.VMEM((queries, widt...  4.86 us
    ppermute x10, waiting for transfers between devices, swapped(): return lax.ppermute(value, 'seq', [(i, i ^ d) for i in range(sizes.seq)])  4.08 us
    ppermute x8, starting transfers between devices, over_cores(): return lax.ppermute(value, 'queue', [(i, i ^ 1) for i in range(queue)])  3.3 us
  transfers between devices with their start and end apart: 22, of which 3 were waited for; matrix products, arithmetic and copies ran while one was open for 0% of the time, Pallas kernels for 29%

profile of v5, /device:TPU:1, one launch (start us, length us, event | category | flops | bytes accessed | tf_op | source)
XLA Modules:
  0.0 64.4 jit_solution(5410012318734314275)
XLA Ops:
  0.7 1.0 %prep.1 = (bf16[16,6784]{1,0:T(8,128)(2,1)S(1)}, bf16[16,1152]{1,0:T(8,128)(2,1)S(1)}, bf16[16,4864]{1,0:T(8,128)(2,1)S(1)}, bf16[16,4864]{1,0:T(8,128)(2,1)S(1)}, bf16[16,4864]{1,0:T(8,128)(2,1)S(1)}) custom-call(bf16[128,1152]{1,0:T(8,128)(2,1)} %position_ref.1, f32[4,16,128]{2,1,0:T(8,128)} %latents_ref.3, bf16[2,144,128]{2,1,0:T(8,128)(2,1)} %bitcast.9), custom_call_target="tpu_custom_call" | custom-call | flops 1500000000 | bytes 1500000 | tf_op jit(solution)/shard_map/prep/pallas_call | solution.py:504
  1.8 2.7 %collective-permute-start.1 = (bf16[16,4864]{1,0:T(8,128)(2,1)S(1)}, bf16[16,4864]{1,0:T(8,128)(2,1)S(1)}, u32[]{:S(2)}, u32[]{:S(2)}) collective-permute-start(bf16[16,4864]{1,0:T(8,128)(2,1)S(1)} %get-tuple-element.45), channel_id=1, source_target_pairs={{0,1},{1,0},{2,3},{3,2},{4,5},{5,4},{6,7},{7,6},{8,9},{9,8},{10,11... | collective-permute-start | bytes 466952 | tf_op jit(solution)/shard_map/ppermute | solution.py:497
  4.5 1.3 %collective-permute-start.2 = (bf16[16,4864]{1,0:T(8,128)(2,1)S(1)}, bf16[16,4864]{1,0:T(8,128)(2,1)S(1)}, u32[]{:S(2)}, u32[]{:S(2)}) collective-permute-start(bf16[16,4864]{1,0:T(8,128)(2,1)S(1)} %get-tuple-element.46), channel_id=1, source_target_pairs={{0,2},{1,3},{2,0},{3,1},{4,6},{5,7},{6,4},{7,5},{8,10},{9,11},{10,... | collective-permute-start | bytes 466952 | tf_op jit(solution)/shard_map/ppermute | solution.py:497
  5.8 2.4 %collective-permute-start.4 = (bf16[16,6784]{1,0:T(8,128)(2,1)S(1)}, bf16[16,6784]{1,0:T(8,128)(2,1)S(1)}, u32[]{:S(2)}, u32[]{:S(2)}) collective-permute-start(bf16[16,6784]{1,0:T(8,128)(2,1)S(1)} %get-tuple-element.48.mine.refs_8_), channel_id=1, source_target_pairs={{0,4},{1,5},{2,6},{3,7},{4,0},{5,1},{6,2},{7,3},{8,12},{9,13},{10,... | collective-permute-start | bytes 651272 | tf_op jit(solution)/shard_map/ppermute | solution.py:497
  8.3 5.5 %first.1 = (f32[8,1152]{1,0:T(8,128)S(1)}, bf16[1152,3456]{1,0:T(8,128)(2,1)S(1)}, bf16[128,1152]{1,0:T(8,128)(2,1)S(1)}, bf16[128,1152]{1,0:T(8,128)(2,1)S(1)},...) custom-call(s32[4]{0:T(128)S(1)} %copy-done.7, f32[31]{0:T(128)S(1)} %copy-done.8, f32[5,30,1152]{2,1,0:T(8,128)S(1)} %bitcast.5, ...), custom_call_target="tpu_custom_call" | custom-call | flops 4000000000 | bytes 4000000 | tf_op jit(solution)/shard_map/first/pallas_call | solution.py:540
  13.8 0.6 collective-permute-done.2.refs_1_.refs_11_
  14.4 3.5 %collective-permute-done.3.refs_2_.refs_12_ = bf16[16,4864]{1,0:T(8,128)(2,1)S(1)} collective-permute-done((bf16[16,4864]{1,0:T(8,128)(2,1)S(1)}, bf16[16,4864]{1,0:T(8,128)(2,1)S(1)}, u32[]{:S(2)}, u32[]{:S(2)}) %collective-permute-start.3) | collective-permute-done | bytes 155680 | tf_op jit(solution)/shard_map/ppermute | solution.py:497
  17.9 0.9 %collective-permute-start.5 = (bf16[16,4864]{1,0:T(8,128)(2,1)S(1)}, bf16[16,4864]{1,0:T(8,128)(2,1)S(1)}, u32[]{:S(2)}, u32[]{:S(2)}) collective-permute-start(bf16[16,4864]{1,0:T(8,128)(2,1)S(1)} %collective-permute-done.1.refs_0_.refs_10_), channel_id=1, source_target_pairs={{0,8},{8,0},{16,24},{24,16},{1,9},{9,1},{17,25},{25,17},{2,10},{10... | collective-permute-start | bytes 466952 | tf_op jit(solution)/shard_map/ppermute | solution.py:500
  19.3 1.4 %collective-permute-start.8 = (bf16[16,7936]{1,0:T(8,128)(2,1)S(1)}, bf16[16,7936]{1,0:T(8,128)(2,1)S(1)}, u32[]{:S(2)}, u32[]{:S(2)}) collective-permute-start(bf16[16,7936]{1,0:T(8,128)(2,1)S(1)} %join.1), channel_id=1, source_target_pairs={{0,1},{1,0},{2,3},{3,2},{4,5},{5,4},{6,7},{7,6},{8,9},{9,8},{10,11... | collective-permute-start | bytes 761864 | tf_op jit(solution)/shard_map/ppermute | solution.py:497
  20.7 1.4 %collective-permute-start.9 = (bf16[16,7936]{1,0:T(8,128)(2,1)S(1)}, bf16[16,7936]{1,0:T(8,128)(2,1)S(1)}, u32[]{:S(2)}, u32[]{:S(2)}) collective-permute-start(bf16[16,7936]{1,0:T(8,128)(2,1)S(1)} %join.1), channel_id=1, source_target_pairs={{0,2},{1,3},{2,0},{3,1},{4,6},{5,7},{6,4},{7,5},{8,10},{9,11},{10,... | collective-permute-start | bytes 761864 | tf_op jit(solution)/shard_map/ppermute | solution.py:497
  22.1 0.9 %collective-permute-start.10 = (bf16[16,7936]{1,0:T(8,128)(2,1)S(1)}, bf16[16,7936]{1,0:T(8,128)(2,1)S(1)}, u32[]{:S(2)}, u32[]{:S(2)}) collective-permute-start(bf16[16,7936]{1,0:T(8,128)(2,1)S(1)} %join.1), channel_id=1, source_target_pairs={{0,3},{1,2},{2,1},{3,0},{4,7},{5,6},{6,5},{7,4},{8,11},{9,10},{10,... | collective-permute-start | bytes 761864 | tf_op jit(solution)/shard_map/ppermute | solution.py:497
  23.6 6.3 %own.1 = (bf16[512,1152]{1,0:T(8,128)(2,1)S(1)}, bf16[512,1152]{1,0:T(8,128)(2,1)S(1)}, bf16[512,1152]{1,0:T(8,128)(2,1)S(1)}, f32[512,1152]{1,0:T(8,128)S(1)}) custom-call(bf16[16,4864]{1,0:T(8,128)(2,1)S(1)} %collective-permute-done.1.refs_0_.refs_10_, bf16[16,4864]{1,0:T(8,128)(2,1)S(1)} %collective-permute-done.2.refs_1_.refs_11_, ...), custom_call_target="tpu_custom_call" | custom-call | flops 8000000000 | bytes 8000000 | tf_op jit(solution)/shard_map/own/pallas_call | solution.py:577
  29.9 4.9 %attend.1 = (f32[512,1152]{1,0:T(8,128)S(1)}, f32[512,128]{1,0:T(8,128)S(1)}, bf16[1152,1152]{1,0:T(8,128)(2,1)S(1)}) custom-call(bf16[512,1152]{1,0:T(8,128)(2,1)S(1)} %get-tuple-element.59.q_ref.refs_16_, bf16[512,1152]{1,0:T(8,128)(2,1)S(1)} %get-tuple-element.60.k_ref, bf16[512,1152]{1,0:T(8,128)(2,1)S(1)} %get-tuple-element.61.v_ref, ...), custom_call_target="tpu_custom_call" | custom-call | flops 5000000000 | bytes 5000000 | tf_op jit(solution)/shard_map/attend/pallas_call | solution.py:586
  34.8 0.7 %collective-permute-start.12 = (bf16[16,7936]{1,0:T(8,128)(2,1)S(1)}, bf16[16,7936]{1,0:T(8,128)(2,1)S(1)}, u32[]{:S(2)}, u32[]{:S(2)}) collective-permute-start(bf16[16,7936]{1,0:T(8,128)(2,1)S(1)} %collective-permute-done.8.refs_1_), channel_id=1, source_target_pairs={{0,8},{8,0},{16,24},{24,16},{1,9},{9,1},{17,25},{25,17},{2,10},{10... | collective-permute-start | bytes 761864 | tf_op jit(solution)/shard_map/ppermute | solution.py:500
  36.1 2.0 %far.1 = (bf16[128,1152]{1,0:T(8,128)(2,1)S(1)}, bf16[128,1152]{1,0:T(8,128)(2,1)S(1)}) custom-call(bf16[16,6784]{1,0:T(8,128)(2,1)S(1)} %collective-permute-done.4.far_ref.refs_0_, bf16[16,6784]{1,0:T(8,128)(2,1)S(1)} %collective-permute-done.11.refs_1_.refs_4_, bf16[16,1152]{1,0:T(8,128)(2,1)S(1)} %copy-done.1, ...), custom_call_target="tpu_custom_call" | custom-call | flops 2500000000 | bytes 2500000 | tf_op jit(solution)/shard_map/far/pallas_call | solution.py:602
  38.1 14.7 %rest.1 = (f32[16,128]{1,0:T(8,128)S(1)}, f32[16,128]{1,0:T(8,128)S(1)}, f32[16,128]{1,0:T(8,128)S(1)}, f32[16,128]{1,0:T(8,128)S(1)}, f32[16,128]{1,0:T(8,128)S...) custom-call(bf16[16,6784]{1,0:T(8,128)(2,1)S(1)} %collective-permute-done.4.far_ref.refs_0_, ...), custom_call_target="tpu_custom_call" | custom-call | flops 17999998976 | bytes 18000000 | tf_op jit(solution)/shard_map/rest/pallas_call | solution.py:616
  53.3 1.4 %collective-permute-start.16 = (f32[16,128]{1,0:T(8,128)S(1)}, f32[16,128]{1,0:T(8,128)S(1)}, u32[]{:S(2)}, u32[]{:S(2)}) collective-permute-start(f32[16,128]{1,0:T(8,128)S(1)} %get-tuple-element.76), channel_id=1, source_target_pairs={{0,2},{1,3},{2,0},{3,1},{4,6},{5,7},{6,4},{7,5},{8,10},{9,11},{10,... | collective-permute-start | bytes 24584 | tf_op jit(solution)/shard_map/ppermute | solution.py:497
  54.7 0.9 %collective-permute-start.17 = (f32[16,128]{1,0:T(8,128)S(1)}, f32[16,128]{1,0:T(8,128)S(1)}, u32[]{:S(2)}, u32[]{:S(2)}) collective-permute-start(f32[16,128]{1,0:T(8,128)S(1)} %get-tuple-element.77), channel_id=1, source_target_pairs={{0,3},{1,2},{2,1},{3,0},{4,7},{5,6},{6,5},{7,4},{8,11},{9,10},{10,... | collective-permute-start | bytes 24584 | tf_op jit(solution)/shard_map/ppermute | solution.py:497
  55.6 2.7 %collective-permute-start.18 = (f32[16,128]{1,0:T(8,128)S(1)}, f32[16,128]{1,0:T(8,128)S(1)}, u32[]{:S(2)}, u32[]{:S(2)}) collective-permute-start(f32[16,128]{1,0:T(8,128)S(1)} %get-tuple-element.78), channel_id=1, source_target_pairs={{8,0},{12,4},{16,8},{20,12},{24,16},{28,20}} | collective-permute-start | bytes 24584 | tf_op jit(solution)/shard_map/ppermute | solution.py:663
  58.3 1.3 %collective-permute-start.19 = (f32[16,128]{1,0:T(8,128)S(1)}, f32[16,128]{1,0:T(8,128)S(1)}, u32[]{:S(2)}, u32[]{:S(2)}) collective-permute-start(f32[16,128]{1,0:T(8,128)S(1)} %get-tuple-element.79), channel_id=1, source_target_pairs={{8,1},{12,5},{16,9},{20,13},{24,17},{28,21}} | collective-permute-start | bytes 24584 | tf_op jit(solution)/shard_map/ppermute | solution.py:663
  59.6 1.5 %collective-permute-start.20 = (f32[16,128]{1,0:T(8,128)S(1)}, f32[16,128]{1,0:T(8,128)S(1)}, u32[]{:S(2)}, u32[]{:S(2)}) collective-permute-start(f32[16,128]{1,0:T(8,128)S(1)} %get-tuple-element.80), channel_id=1, source_target_pairs={{8,2},{12,6},{16,10},{20,14},{24,18},{28,22}} | collective-permute-start | bytes 24584 | tf_op jit(solution)/shard_map/ppermute | solution.py:663
  61.1 1.3 %collective-permute-start.21 = (f32[16,128]{1,0:T(8,128)S(1)}, f32[16,128]{1,0:T(8,128)S(1)}, u32[]{:S(2)}, u32[]{:S(2)}) collective-permute-start(f32[16,128]{1,0:T(8,128)S(1)} %get-tuple-element.81), channel_id=1, source_target_pairs={{8,3},{12,7},{16,11},{20,15},{24,19},{28,23}} | collective-permute-start | bytes 24584 | tf_op jit(solution)/shard_map/ppermute | solution.py:663
  62.5 0.7 %collective-permute-done.21.refs_7_ = f32[16,128]{1,0:T(8,128)S(1)} collective-permute-done((f32[16,128]{1,0:T(8,128)S(1)}, f32[16,128]{1,0:T(8,128)S(1)}, u32[]{:S(2)}, u32[]{:S(2)}) %collective-permute-start.21) | collective-permute-done | bytes 8224 | tf_op jit(solution)/shard_map/ppermute | solution.py:663
  63.2 1.2 %finish.1 = (f32[4,16,128]{2,1,0:T(8,128)}, f32[4,16,128]{2,1,0:T(8,128)}) custom-call(s32[4]{0:T(128)S(1)} %copy-done.7, f32[31]{0:T(128)S(1)} %copy-done.8, f32[4,16,128]{2,1,0:T(8,128)S(1)} %copy-done.3, f32[16,128]{1,0:T(8,128)S(1)} %copy-done.4, f32[16,128]{1,0:T(8,128)S(1)} %get-tuple-element.74.refs_0_, ...), custom_call_target="tpu_custom_call" | custom-call | flops 1000000000 | bytes 1000000 | tf_op jit(solution)/shard_map/finish/pallas_call | solution.py:669
  (46 shorter events, 2.2 us)
Async XLA Ops:
  1.7 4.1 %collective-permute-start = (bf16[16,6784]{1,0:T(8,128)(2,1)S(1)}, bf16[16,6784]{1,0:T(8,128)(2,1)S(1)}, u32[]{:S(2)}, u32[]{:S(2)}) collective-permute-start(bf16[16,6784]{1,0:T(8,128)(2,1)S(1)} %get-tuple-element.48.mine.refs_8_), channel_id=1, source_target_pairs={{0,8},{8,0},{16,24},{24,16},{1,9},{9,1},{17,25},{25,17},{2,10},{10... | collective-permute-start | bytes 651272 | tf_op jit(solution)/shard_map/ppermute | solution.py:500
  1.8 12.0 %collective-permute-start.1 = (bf16[16,4864]{1,0:T(8,128)(2,1)S(1)}, bf16[16,4864]{1,0:T(8,128)(2,1)S(1)}, u32[]{:S(2)}, u32[]{:S(2)}) collective-permute-start(bf16[16,4864]{1,0:T(8,128)(2,1)S(1)} %get-tuple-element.45), channel_id=1, source_target_pairs={{0,1},{1,0},{2,3},{3,2},{4,5},{5,4},{6,7},{7,6},{8,9},{9,8},{10,11... | collective-permute-start | bytes 466952 | tf_op jit(solution)/shard_map/ppermute | solution.py:497
  4.5 9.9 %collective-permute-start.2 = (bf16[16,4864]{1,0:T(8,128)(2,1)S(1)}, bf16[16,4864]{1,0:T(8,128)(2,1)S(1)}, u32[]{:S(2)}, u32[]{:S(2)}) collective-permute-start(bf16[16,4864]{1,0:T(8,128)(2,1)S(1)} %get-tuple-element.46), channel_id=1, source_target_pairs={{0,2},{1,3},{2,0},{3,1},{4,6},{5,7},{6,4},{7,5},{8,10},{9,11},{10,... | collective-permute-start | bytes 466952 | tf_op jit(solution)/shard_map/ppermute | solution.py:497
  5.8 12.1 %collective-permute-start.3 = (bf16[16,4864]{1,0:T(8,128)(2,1)S(1)}, bf16[16,4864]{1,0:T(8,128)(2,1)S(1)}, u32[]{:S(2)}, u32[]{:S(2)}) collective-permute-start(bf16[16,4864]{1,0:T(8,128)(2,1)S(1)} %get-tuple-element.47), channel_id=1, source_target_pairs={{0,3},{1,2},{2,1},{3,0},{4,7},{5,6},{6,5},{7,4},{8,11},{9,10},{10,... | collective-permute-start | bytes 466952 | tf_op jit(solution)/shard_map/ppermute | solution.py:497
  5.8 12.1 %collective-permute-start.4 = (bf16[16,6784]{1,0:T(8,128)(2,1)S(1)}, bf16[16,6784]{1,0:T(8,128)(2,1)S(1)}, u32[]{:S(2)}, u32[]{:S(2)}) collective-permute-start(bf16[16,6784]{1,0:T(8,128)(2,1)S(1)} %get-tuple-element.48.mine.refs_8_), channel_id=1, source_target_pairs={{0,4},{1,5},{2,6},{3,7},{4,0},{5,1},{6,2},{7,3},{8,12},{9,13},{10,... | collective-permute-start | bytes 651272 | tf_op jit(solution)/shard_map/ppermute | solution.py:497
  17.9 4.2 %collective-permute-start.5 = (bf16[16,4864]{1,0:T(8,128)(2,1)S(1)}, bf16[16,4864]{1,0:T(8,128)(2,1)S(1)}, u32[]{:S(2)}, u32[]{:S(2)}) collective-permute-start(bf16[16,4864]{1,0:T(8,128)(2,1)S(1)} %collective-permute-done.1.refs_0_.refs_10_), channel_id=1, source_target_pairs={{0,8},{8,0},{16,24},{24,16},{1,9},{9,1},{17,25},{25,17},{2,10},{10... | collective-permute-start | bytes 466952 | tf_op jit(solution)/shard_map/ppermute | solution.py:500
  18.7 4.3 %collective-permute-start.6 = (bf16[16,4864]{1,0:T(8,128)(2,1)S(1)}, bf16[16,4864]{1,0:T(8,128)(2,1)S(1)}, u32[]{:S(2)}, u32[]{:S(2)}) collective-permute-start(bf16[16,4864]{1,0:T(8,128)(2,1)S(1)} %collective-permute-done.2.refs_1_.refs_11_), channel_id=1, source_target_pairs={{0,8},{8,0},{16,24},{24,16},{1,9},{9,1},{17,25},{25,17},{2,10},{10... | collective-permute-start | bytes 466952 | tf_op jit(solution)/shard_map/ppermute | solution.py:500
  18.7 4.9 %collective-permute-start.7 = (bf16[16,4864]{1,0:T(8,128)(2,1)S(1)}, bf16[16,4864]{1,0:T(8,128)(2,1)S(1)}, u32[]{:S(2)}, u32[]{:S(2)}) collective-permute-start(bf16[16,4864]{1,0:T(8,128)(2,1)S(1)} %collective-permute-done.3.refs_2_.refs_12_), channel_id=1, source_target_pairs={{0,8},{8,0},{16,24},{24,16},{1,9},{9,1},{17,25},{25,17},{2,10},{10... | collective-permute-start | bytes 466952 | tf_op jit(solution)/shard_map/ppermute | solution.py:500
  19.3 15.5 %collective-permute-start.8 = (bf16[16,7936]{1,0:T(8,128)(2,1)S(1)}, bf16[16,7936]{1,0:T(8,128)(2,1)S(1)}, u32[]{:S(2)}, u32[]{:S(2)}) collective-permute-start(bf16[16,7936]{1,0:T(8,128)(2,1)S(1)} %join.1), channel_id=1, source_target_pairs={{0,1},{1,0},{2,3},{3,2},{4,5},{5,4},{6,7},{7,6},{8,9},{9,8},{10,11... | collective-permute-start | bytes 761864 | tf_op jit(solution)/shard_map/ppermute | solution.py:497
  20.7 14.1 %collective-permute-start.9 = (bf16[16,7936]{1,0:T(8,128)(2,1)S(1)}, bf16[16,7936]{1,0:T(8,128)(2,1)S(1)}, u32[]{:S(2)}, u32[]{:S(2)}) collective-permute-start(bf16[16,7936]{1,0:T(8,128)(2,1)S(1)} %join.1), channel_id=1, source_target_pairs={{0,2},{1,3},{2,0},{3,1},{4,6},{5,7},{6,4},{7,5},{8,10},{9,11},{10,... | collective-permute-start | bytes 761864 | tf_op jit(solution)/shard_map/ppermute | solution.py:497
  22.1 12.7 %collective-permute-start.10 = (bf16[16,7936]{1,0:T(8,128)(2,1)S(1)}, bf16[16,7936]{1,0:T(8,128)(2,1)S(1)}, u32[]{:S(2)}, u32[]{:S(2)}) collective-permute-start(bf16[16,7936]{1,0:T(8,128)(2,1)S(1)} %join.1), channel_id=1, source_target_pairs={{0,3},{1,2},{2,1},{3,0},{4,7},{5,6},{6,5},{7,4},{8,11},{9,10},{10,... | collective-permute-start | bytes 761864 | tf_op jit(solution)/shard_map/ppermute | solution.py:497
  23.0 13.0 %collective-permute-start.11 = (bf16[16,6784]{1,0:T(8,128)(2,1)S(1)}, bf16[16,6784]{1,0:T(8,128)(2,1)S(1)}, u32[]{:S(2)}, u32[]{:S(2)}) collective-permute-start(bf16[16,6784]{1,0:T(8,128)(2,1)S(1)} %collective-permute-done.4.far_ref.refs_0_), channel_id=1, source_target_pairs={{0,8},{8,0},{16,24},{24,16},{1,9},{9,1},{17,25},{25,17},{2,10},{10... | collective-permute-start | bytes 651272 | tf_op jit(solution)/shard_map/ppermute | solution.py:500
  34.8 3.3 %collective-permute-start.12 = (bf16[16,7936]{1,0:T(8,128)(2,1)S(1)}, bf16[16,7936]{1,0:T(8,128)(2,1)S(1)}, u32[]{:S(2)}, u32[]{:S(2)}) collective-permute-start(bf16[16,7936]{1,0:T(8,128)(2,1)S(1)} %collective-permute-done.8.refs_1_), channel_id=1, source_target_pairs={{0,8},{8,0},{16,24},{24,16},{1,9},{9,1},{17,25},{25,17},{2,10},{10... | collective-permute-start | bytes 761864 | tf_op jit(solution)/shard_map/ppermute | solution.py:500
  35.5 2.5 %collective-permute-start.13 = (bf16[16,7936]{1,0:T(8,128)(2,1)S(1)}, bf16[16,7936]{1,0:T(8,128)(2,1)S(1)}, u32[]{:S(2)}, u32[]{:S(2)}) collective-permute-start(bf16[16,7936]{1,0:T(8,128)(2,1)S(1)} %collective-permute-done.9.refs_2_), channel_id=1, source_target_pairs={{0,8},{8,0},{16,24},{24,16},{1,9},{9,1},{17,25},{25,17},{2,10},{10... | collective-permute-start | bytes 761864 | tf_op jit(solution)/shard_map/ppermute | solution.py:500
  35.5 2.6 %collective-permute-start.14 = (bf16[16,7936]{1,0:T(8,128)(2,1)S(1)}, bf16[16,7936]{1,0:T(8,128)(2,1)S(1)}, u32[]{:S(2)}, u32[]{:S(2)}) collective-permute-start(bf16[16,7936]{1,0:T(8,128)(2,1)S(1)} %collective-permute-done.10.refs_3_), channel_id=1, source_target_pairs={{0,8},{8,0},{16,24},{24,16},{1,9},{9,1},{17,25},{25,17},{2,10},{10... | collective-permute-start | bytes 761864 | tf_op jit(solution)/shard_map/ppermute | solution.py:500
  38.1 25.1 %copy-start.3 = (f32[4,16,128]{2,1,0:T(8,128)S(1)}, f32[4,16,128]{2,1,0:T(8,128)}, u32[]{:S(2)}) copy-start(f32[4,16,128]{2,1,0:T(8,128)} %latents_ref.3) | copy-start | bytes 98308
  38.1 25.1 %copy-start.4 = (f32[16,128]{1,0:T(8,128)S(1)}, f32[16,128]{1,0:T(8,128)}, u32[]{:S(2)}) copy-start(f32[16,128]{1,0:T(8,128)} %noise_ref.1) | copy-start | bytes 24580
  52.9 6.7 %collective-permute-start.15 = (f32[16,128]{1,0:T(8,128)S(1)}, f32[16,128]{1,0:T(8,128)S(1)}, u32[]{:S(2)}, u32[]{:S(2)}) collective-permute-start(f32[16,128]{1,0:T(8,128)S(1)} %get-tuple-element.75), channel_id=1, source_target_pairs={{0,1},{1,0},{2,3},{3,2},{4,5},{5,4},{6,7},{7,6},{8,9},{9,8},{10,11... | collective-permute-start | bytes 24584 | tf_op jit(solution)/shard_map/ppermute | solution.py:497
  53.3 7.8 %collective-permute-start.16 = (f32[16,128]{1,0:T(8,128)S(1)}, f32[16,128]{1,0:T(8,128)S(1)}, u32[]{:S(2)}, u32[]{:S(2)}) collective-permute-start(f32[16,128]{1,0:T(8,128)S(1)} %get-tuple-element.76), channel_id=1, source_target_pairs={{0,2},{1,3},{2,0},{3,1},{4,6},{5,7},{6,4},{7,5},{8,10},{9,11},{10,... | collective-permute-start | bytes 24584 | tf_op jit(solution)/shard_map/ppermute | solution.py:497
  54.7 7.8 %collective-permute-start.17 = (f32[16,128]{1,0:T(8,128)S(1)}, f32[16,128]{1,0:T(8,128)S(1)}, u32[]{:S(2)}, u32[]{:S(2)}) collective-permute-start(f32[16,128]{1,0:T(8,128)S(1)} %get-tuple-element.77), channel_id=1, source_target_pairs={{0,3},{1,2},{2,1},{3,0},{4,7},{5,6},{6,5},{7,4},{8,11},{9,10},{10,... | collective-permute-start | bytes 24584 | tf_op jit(solution)/shard_map/ppermute | solution.py:497
  55.6 6.8 %collective-permute-start.18 = (f32[16,128]{1,0:T(8,128)S(1)}, f32[16,128]{1,0:T(8,128)S(1)}, u32[]{:S(2)}, u32[]{:S(2)}) collective-permute-start(f32[16,128]{1,0:T(8,128)S(1)} %get-tuple-element.78), channel_id=1, source_target_pairs={{8,0},{12,4},{16,8},{20,12},{24,16},{28,20}} | collective-permute-start | bytes 24584 | tf_op jit(solution)/shard_map/ppermute | solution.py:663
  58.3 4.1 %collective-permute-start.19 = (f32[16,128]{1,0:T(8,128)S(1)}, f32[16,128]{1,0:T(8,128)S(1)}, u32[]{:S(2)}, u32[]{:S(2)}) collective-permute-start(f32[16,128]{1,0:T(8,128)S(1)} %get-tuple-element.79), channel_id=1, source_target_pairs={{8,1},{12,5},{16,9},{20,13},{24,17},{28,21}} | collective-permute-start | bytes 24584 | tf_op jit(solution)/shard_map/ppermute | solution.py:663
  59.6 2.8 %collective-permute-start.20 = (f32[16,128]{1,0:T(8,128)S(1)}, f32[16,128]{1,0:T(8,128)S(1)}, u32[]{:S(2)}, u32[]{:S(2)}) collective-permute-start(f32[16,128]{1,0:T(8,128)S(1)} %get-tuple-element.80), channel_id=1, source_target_pairs={{8,2},{12,6},{16,10},{20,14},{24,18},{28,22}} | collective-permute-start | bytes 24584 | tf_op jit(solution)/shard_map/ppermute | solution.py:663
  61.1 2.1 %collective-permute-start.21 = (f32[16,128]{1,0:T(8,128)S(1)}, f32[16,128]{1,0:T(8,128)S(1)}, u32[]{:S(2)}, u32[]{:S(2)}) collective-permute-start(f32[16,128]{1,0:T(8,128)S(1)} %get-tuple-element.81), channel_id=1, source_target_pairs={{8,3},{12,7},{16,11},{20,15},{24,19},{28,23}} | collective-permute-start | bytes 24584 | tf_op jit(solution)/shard_map/ppermute | solution.py:663
  (7 other events, 48.9 us)

commit v6 on v5

--- a/solution.py
+++ b/solution.py
@@ -48,23 +48,24 @@
         self.near = self.latents_at + 2 * self.tokens
 
 
-def prep_kernel(sizes, position_ref, latents_ref, text_ref, payload_ref, tail_ref, *refs):
+def prep_kernel(sizes, position_ref, latents_ref, text_ref, payload_ref, mate_ref, tail_ref, *refs):
     near_refs, (latents_scr, text_scr, sems) = refs[:-3], refs[-3:]
     core = lax.rem(lax.axis_index("queue"), 2)
     width, tokens = sizes.width, sizes.tokens
     copies = [
         pltpu.make_async_copy(latents_ref, latents_scr, sems.at[0]),
-        pltpu.make_async_copy(text_ref.at[core], text_scr, sems.at[1]),
+        pltpu.make_async_copy(text_ref, text_scr, sems.at[1]),
     ]
-    for piece in range(sizes.pieces):
-        start = pl.multiple_of(core * sizes.half + piece * ROWS, ROWS)
-        copies.append(
-            pltpu.make_async_copy(
-                position_ref.at[pl.ds(start, ROWS), :],
-                payload_ref.at[:, piece * width : (piece + 1) * width],
-                sems.at[2 + piece],
+    for i, (target, place) in enumerate(((payload_ref, core), (mate_ref, 1 - core))):
+        for piece in range(sizes.pieces):
+            start = pl.multiple_of(place * sizes.half + piece * ROWS, ROWS)
+            copies.append(
+                pltpu.make_async_copy(
+                    position_ref.at[pl.ds(start, ROWS), :],
+                    target.at[:, piece * width : (piece + 1) * width],
+                    sems.at[2 + i * sizes.pieces + piece],
+                )
             )
-        )
     for copy in copies:
         copy.start()
     copies[0].wait()
@@ -76,13 +77,14 @@
     copies[1].wait()
     for piece in range(sizes.text_pieces):
         first, last = piece * ROWS, min((piece + 1) * ROWS, sizes.part)
-        rows = text_scr[first:last, :]
-        if last - first < ROWS:
-            blank = jnp.zeros((ROWS - (last - first), sizes.text_len), BF16)
-            rows = jnp.concatenate([rows, blank], axis=0)
         at = sizes.text_at + piece * sizes.text_len
-        payload_ref[:, at : at + sizes.text_len] = rows
-        tail_ref[:, piece * sizes.text_len : (piece + 1) * sizes.text_len] = rows
+        for target, place in ((payload_ref, core), (mate_ref, 1 - core)):
+            rows = text_scr[place, first:last, :]
+            if last - first < ROWS:
+                blank = jnp.zeros((ROWS - (last - first), sizes.text_len), BF16)
+                rows = jnp.concatenate([rows, blank], axis=0)
+            target[:, at : at + sizes.text_len] = rows
+    tail_ref[...] = payload_ref[:, sizes.text_at :]
     for copy in copies[2:]:
         copy.wait()
     own_frame = lax.rem(lax.axis_index("seq"), sizes.frames)
@@ -501,20 +503,21 @@
 
     far = functools.partial(pltpu.with_memory_space_constraint, memory_space=pltpu.HBM)
 
-    payload, tail, *near = kernel(
+    payload, payload_other, tail, *near = kernel(
         prep_kernel,
         sizes,
         "prep",
         "hhh",
         [
             pltpu.VMEM((ROWS, sizes.payload), BF16),
+            pltpu.VMEM((ROWS, sizes.payload), BF16),
             pltpu.VMEM((ROWS, sizes.payload - sizes.text_at), BF16),
         ]
         + [pltpu.VMEM((ROWS, sizes.near), BF16)] * (frames - 1),
         [
             pltpu.VMEM(latents.shape, F32),
-            pltpu.VMEM(text.shape[1:], BF16),
-            pltpu.SemaphoreType.DMA((2 + sizes.pieces,)),
+            pltpu.VMEM(text.shape, BF16),
+            pltpu.SemaphoreType.DMA((2 + 2 * sizes.pieces,)),
         ],
         1.5,
     )(far(position), far(latents), far(text))
@@ -522,9 +525,7 @@
     order = sorted(range(1, frames), key=lambda d: (d.bit_count() - 2 * (d >= frames // 2), d))
     sent = {d: swapped(near[d - 1], d) for d in order}
     direct = [sent[d] for d in range(1, frames)]
-    payload_other = over_cores(payload)
-    late, payload_other = lax.optimization_barrier((payload, payload_other))
-    direct += [swapped(late, group * frames) for group in range(1, sizes.share)]
+    direct += [swapped(payload, group * frames) for group in range(1, sizes.share)]
 
     def blocks(count):
         return [
@@ -556,8 +557,9 @@
         embed_weight,
         far(qkv_weight),
     )
-    rows, *direct = lax.optimization_barrier((rows, *direct))
     square, far_blocks = direct[: frames - 1], direct[frames - 1 :]
+    rows, *square = lax.optimization_barrier((rows, *square))
+    rows, *far_blocks = lax.optimization_barrier((rows, *far_blocks))
     square_other = [over_cores(value) for value in square]
     far_other = [over_cores(value) for value in far_blocks]
     joined = [

time: 65.2 us -> 64 us (0.982)
  starting transfers between devices: 22.9 us -> 22.2 us
    ppermute x10, starting transfers between devices: 12.9 us -> 11.5 us  [swapped(): return lax.ppermute(value, 'seq', [(i, i ^ d) for i in range(sizes.seq)])]
    ppermute x8 -> x7, starting transfers between devices: 3.3 us -> 3.56 us  [over_cores(): return lax.ppermute(value, 'queue', [(i, i ^ 1) for i in range(queue)])]
  transfers between devices with their start and end apart: 22 -> 21, of which waited for: 3 -> 2; matrix products, arithmetic and copies ran while one was open for 0% -> 0% of each run, Pallas kernels for 29% -> 30%
where the time goes in v6:
time: 64 us; the launch traced here: 63.5 us
  Pallas kernels  36 us (56%)
  starting transfers between devices  22.2 us (35%)
  waiting for transfers between devices  4.34 us (7%)
  between operations  0.93 us (1%)
    pallas_call x1, Pallas kernels, body(): kernel(rest_kernel, sizes, 'rest', 'v' * (2 * len(mine) + 12 + frames), [...  14.8 us
    ppermute x10, starting transfers between devices, swapped(): return lax.ppermute(value, 'seq', [(i, i ^ d) for i in range(sizes.seq)])  11.5 us
    ppermute x4, starting transfers between devices, to_previous(): return lax.ppermute(value, ('queue', 'seq'), route)  7.15 us
    pallas_call x1, Pallas kernels, body(): kernel(own_kernel, sizes, 'own', 'v' * (2 * (frames - 1) + 7), token_arra...  6.31 us
    pallas_call x1, Pallas kernels, body(): kernel(first_kernel, sizes, 'first', 'ssvvvvvvh', [pltpu.VMEM((8, width),...  5.55 us
    pallas_call x1, Pallas kernels, body(): kernel(attend_kernel, sizes, 'attend', 'vvvh', [pltpu.VMEM((queries, widt...  4.93 us
    ppermute x10, waiting for transfers between devices, swapped(): return lax.ppermute(value, 'seq', [(i, i ^ d) for i in range(sizes.seq)])  3.58 us
    ppermute x7, starting transfers between devices, over_cores(): return lax.ppermute(value, 'queue', [(i, i ^ 1) for i in range(queue)])  3.56 us
  transfers between devices with their start and end apart: 21, of which 2 were waited for; matrix products, arithmetic and copies ran while one was open for 0% of the time, Pallas kernels for 30%

profile of v6, /device:TPU:1, one launch (start us, length us, event | category | flops | bytes accessed | tf_op | source)
XLA Modules:
  0.0 63.5 jit_solution(5853746930555817378)
XLA Ops:
  0.7 1.1 %prep.1 = (bf16[16,6784]{1,0:T(8,128)(2,1)S(1)}, bf16[16,6784]{1,0:T(8,128)(2,1)S(1)}, bf16[16,1152]{1,0:T(8,128)(2,1)S(1)}, bf16[16,4864]{1,0:T(8,128)(2,1)S(1)...) custom-call(bf16[128,1152]{1,0:T(8,128)(2,1)} %position_ref.1, f32[4,16,128]{2,1,0:T(8,128)} %latents_ref.3, ...), custom_call_target="tpu_custom_call" | custom-call | flops 1500000000 | bytes 1500000 | tf_op jit(solution)/shard_map/prep/pallas_call | solution.py:506
  1.8 2.1 %collective-permute-start = (bf16[16,4864]{1,0:T(8,128)(2,1)S(1)}, bf16[16,4864]{1,0:T(8,128)(2,1)S(1)}, u32[]{:S(2)}, u32[]{:S(2)}) collective-permute-start(bf16[16,4864]{1,0:T(8,128)(2,1)S(1)} %get-tuple-element.45), channel_id=1, source_target_pairs={{0,1},{1,0},{2,3},{3,2},{4,5},{5,4},{6,7},{7,6},{8,9},{9,8},{10,11... | collective-permute-start | bytes 466952 | tf_op jit(solution)/shard_map/ppermute | solution.py:499
  3.9 1.3 %collective-permute-start.1 = (bf16[16,4864]{1,0:T(8,128)(2,1)S(1)}, bf16[16,4864]{1,0:T(8,128)(2,1)S(1)}, u32[]{:S(2)}, u32[]{:S(2)}) collective-permute-start(bf16[16,4864]{1,0:T(8,128)(2,1)S(1)} %get-tuple-element.46), channel_id=1, source_target_pairs={{0,2},{1,3},{2,0},{3,1},{4,6},{5,7},{6,4},{7,5},{8,10},{9,11},{10,... | collective-permute-start | bytes 466952 | tf_op jit(solution)/shard_map/ppermute | solution.py:499
  5.2 2.4 %collective-permute-start.3 = (bf16[16,6784]{1,0:T(8,128)(2,1)S(1)}, bf16[16,6784]{1,0:T(8,128)(2,1)S(1)}, u32[]{:S(2)}, u32[]{:S(2)}) collective-permute-start(bf16[16,6784]{1,0:T(8,128)(2,1)S(1)} %get-tuple-element.42.mine.refs_8_), channel_id=1, source_target_pairs={{0,4},{1,5},{2,6},{3,7},{4,0},{5,1},{6,2},{7,3},{8,12},{9,13},{10,... | collective-permute-start | bytes 651272 | tf_op jit(solution)/shard_map/ppermute | solution.py:499
  7.7 5.6 %first.1 = (f32[8,1152]{1,0:T(8,128)S(1)}, bf16[1152,3456]{1,0:T(8,128)(2,1)S(1)}, bf16[128,1152]{1,0:T(8,128)(2,1)S(1)}, bf16[128,1152]{1,0:T(8,128)(2,1)S(1)},...) custom-call(s32[4]{0:T(128)S(1)} %copy-done.7, f32[31]{0:T(128)S(1)} %copy-done.8, f32[5,30,1152]{2,1,0:T(8,128)S(1)} %bitcast.5, ...), custom_call_target="tpu_custom_call" | custom-call | flops 4000000000 | bytes 4000000 | tf_op jit(solution)/shard_map/first/pallas_call | solution.py:541
  13.3 3.6 %collective-permute-done.2.refs_2_.refs_12_ = bf16[16,4864]{1,0:T(8,128)(2,1)S(1)} collective-permute-done((bf16[16,4864]{1,0:T(8,128)(2,1)S(1)}, bf16[16,4864]{1,0:T(8,128)(2,1)S(1)}, u32[]{:S(2)}, u32[]{:S(2)}) %collective-permute-start.2) | collective-permute-done | bytes 155680 | tf_op jit(solution)/shard_map/ppermute | solution.py:499
  16.9 1.3 %collective-permute-start.4 = (bf16[16,4864]{1,0:T(8,128)(2,1)S(1)}, bf16[16,4864]{1,0:T(8,128)(2,1)S(1)}, u32[]{:S(2)}, u32[]{:S(2)}) collective-permute-start(bf16[16,4864]{1,0:T(8,128)(2,1)S(1)} %collective-permute-done.refs_0_.refs_10_), channel_id=1, source_target_pairs={{0,8},{8,0},{16,24},{24,16},{1,9},{9,1},{17,25},{25,17},{2,10},{10... | collective-permute-start | bytes 466952 | tf_op jit(solution)/shard_map/ppermute | solution.py:502
  18.2 0.5 collective-permute-start.6
  18.7 1.4 %collective-permute-start.7 = (bf16[16,7936]{1,0:T(8,128)(2,1)S(1)}, bf16[16,7936]{1,0:T(8,128)(2,1)S(1)}, u32[]{:S(2)}, u32[]{:S(2)}) collective-permute-start(bf16[16,7936]{1,0:T(8,128)(2,1)S(1)} %join.1), channel_id=1, source_target_pairs={{0,1},{1,0},{2,3},{3,2},{4,5},{5,4},{6,7},{7,6},{8,9},{9,8},{10,11... | collective-permute-start | bytes 761864 | tf_op jit(solution)/shard_map/ppermute | solution.py:499
  20.2 1.3 %collective-permute-start.9 = (bf16[16,7936]{1,0:T(8,128)(2,1)S(1)}, bf16[16,7936]{1,0:T(8,128)(2,1)S(1)}, u32[]{:S(2)}, u32[]{:S(2)}) collective-permute-start(bf16[16,7936]{1,0:T(8,128)(2,1)S(1)} %join.1), channel_id=1, source_target_pairs={{0,3},{1,2},{2,1},{3,0},{4,7},{5,6},{6,5},{7,4},{8,11},{9,10},{10,... | collective-permute-start | bytes 761864 | tf_op jit(solution)/shard_map/ppermute | solution.py:499
  21.4 1.1 %collective-permute-start.10 = (bf16[16,6784]{1,0:T(8,128)(2,1)S(1)}, bf16[16,6784]{1,0:T(8,128)(2,1)S(1)}, u32[]{:S(2)}, u32[]{:S(2)}) collective-permute-start(bf16[16,6784]{1,0:T(8,128)(2,1)S(1)} %collective-permute-done.3.far_ref.refs_0_), channel_id=1, source_target_pairs={{0,8},{8,0},{16,24},{24,16},{1,9},{9,1},{17,25},{25,17},{2,10},{10... | collective-permute-start | bytes 651272 | tf_op jit(solution)/shard_map/ppermute | solution.py:502
  22.5 6.3 %own.1 = (bf16[512,1152]{1,0:T(8,128)(2,1)S(1)}, bf16[512,1152]{1,0:T(8,128)(2,1)S(1)}, bf16[512,1152]{1,0:T(8,128)(2,1)S(1)}, f32[512,1152]{1,0:T(8,128)S(1)}) custom-call(bf16[16,4864]{1,0:T(8,128)(2,1)S(1)} %collective-permute-done.refs_0_.refs_10_, bf16[16,4864]{1,0:T(8,128)(2,1)S(1)} %collective-permute-done.1.refs_1_.refs_11_, ...), custom_call_target="tpu_custom_call" | custom-call | flops 8000000000 | bytes 8000000 | tf_op jit(solution)/shard_map/own/pallas_call | solution.py:579
  28.8 4.9 %attend.1 = (f32[512,1152]{1,0:T(8,128)S(1)}, f32[512,128]{1,0:T(8,128)S(1)}, bf16[1152,1152]{1,0:T(8,128)(2,1)S(1)}) custom-call(bf16[512,1152]{1,0:T(8,128)(2,1)S(1)} %get-tuple-element.59.q_ref.refs_16_, bf16[512,1152]{1,0:T(8,128)(2,1)S(1)} %get-tuple-element.60.k_ref, bf16[512,1152]{1,0:T(8,128)(2,1)S(1)} %get-tuple-element.61.v_ref, ...), custom_call_target="tpu_custom_call" | custom-call | flops 5000000000 | bytes 5000000 | tf_op jit(solution)/shard_map/attend/pallas_call | solution.py:588
  34.5 2.1 %far.1 = (bf16[128,1152]{1,0:T(8,128)(2,1)S(1)}, bf16[128,1152]{1,0:T(8,128)(2,1)S(1)}) custom-call(bf16[16,6784]{1,0:T(8,128)(2,1)S(1)} %collective-permute-done.3.far_ref.refs_0_, bf16[16,6784]{1,0:T(8,128)(2,1)S(1)} %collective-permute-done.10.refs_1_.refs_4_, bf16[16,1152]{1,0:T(8,128)(2,1)S(1)} %copy-done.1, ...), custom_call_target="tpu_custom_call" | custom-call | flops 2500000000 | bytes 2500000 | tf_op jit(solution)/shard_map/far/pallas_call | solution.py:604
  36.6 14.8 %rest.1 = (f32[16,128]{1,0:T(8,128)S(1)}, f32[16,128]{1,0:T(8,128)S(1)}, f32[16,128]{1,0:T(8,128)S(1)}, f32[16,128]{1,0:T(8,128)S(1)}, f32[16,128]{1,0:T(8,128)S...) custom-call(bf16[16,6784]{1,0:T(8,128)(2,1)S(1)} %collective-permute-done.3.far_ref.refs_0_, ...), custom_call_target="tpu_custom_call" | custom-call | flops 17999998976 | bytes 18000000 | tf_op jit(solution)/shard_map/rest/pallas_call | solution.py:618
  51.4 1.4 %collective-permute-start.14 = (f32[16,128]{1,0:T(8,128)S(1)}, f32[16,128]{1,0:T(8,128)S(1)}, u32[]{:S(2)}, u32[]{:S(2)}) collective-permute-start(f32[16,128]{1,0:T(8,128)S(1)} %get-tuple-element.75), channel_id=1, source_target_pairs={{0,1},{1,0},{2,3},{3,2},{4,5},{5,4},{6,7},{7,6},{8,9},{9,8},{10,11... | collective-permute-start | bytes 24584 | tf_op jit(solution)/shard_map/ppermute | solution.py:499
  52.8 0.6 %collective-permute-start.15 = (f32[16,128]{1,0:T(8,128)S(1)}, f32[16,128]{1,0:T(8,128)S(1)}, u32[]{:S(2)}, u32[]{:S(2)}) collective-permute-start(f32[16,128]{1,0:T(8,128)S(1)} %get-tuple-element.76), channel_id=1, source_target_pairs={{0,2},{1,3},{2,0},{3,1},{4,6},{5,7},{6,4},{7,5},{8,10},{9,11},{10,... | collective-permute-start | bytes 24584 | tf_op jit(solution)/shard_map/ppermute | solution.py:499
  53.4 0.9 %collective-permute-start.16 = (f32[16,128]{1,0:T(8,128)S(1)}, f32[16,128]{1,0:T(8,128)S(1)}, u32[]{:S(2)}, u32[]{:S(2)}) collective-permute-start(f32[16,128]{1,0:T(8,128)S(1)} %get-tuple-element.77), channel_id=1, source_target_pairs={{0,3},{1,2},{2,1},{3,0},{4,7},{5,6},{6,5},{7,4},{8,11},{9,10},{10,... | collective-permute-start | bytes 24584 | tf_op jit(solution)/shard_map/ppermute | solution.py:499
  54.4 2.9 %collective-permute-start.17 = (f32[16,128]{1,0:T(8,128)S(1)}, f32[16,128]{1,0:T(8,128)S(1)}, u32[]{:S(2)}, u32[]{:S(2)}) collective-permute-start(f32[16,128]{1,0:T(8,128)S(1)} %get-tuple-element.78), channel_id=1, source_target_pairs={{8,0},{12,4},{16,8},{20,12},{24,16},{28,20}} | collective-permute-start | bytes 24584 | tf_op jit(solution)/shard_map/ppermute | solution.py:665
  57.3 1.7 %collective-permute-start.18 = (f32[16,128]{1,0:T(8,128)S(1)}, f32[16,128]{1,0:T(8,128)S(1)}, u32[]{:S(2)}, u32[]{:S(2)}) collective-permute-start(f32[16,128]{1,0:T(8,128)S(1)} %get-tuple-element.79), channel_id=1, source_target_pairs={{8,1},{12,5},{16,9},{20,13},{24,17},{28,21}} | collective-permute-start | bytes 24584 | tf_op jit(solution)/shard_map/ppermute | solution.py:665
  59.0 1.3 %collective-permute-start.19 = (f32[16,128]{1,0:T(8,128)S(1)}, f32[16,128]{1,0:T(8,128)S(1)}, u32[]{:S(2)}, u32[]{:S(2)}) collective-permute-start(f32[16,128]{1,0:T(8,128)S(1)} %get-tuple-element.80), channel_id=1, source_target_pairs={{8,2},{12,6},{16,10},{20,14},{24,18},{28,22}} | collective-permute-start | bytes 24584 | tf_op jit(solution)/shard_map/ppermute | solution.py:665
  60.3 1.3 %collective-permute-start.20 = (f32[16,128]{1,0:T(8,128)S(1)}, f32[16,128]{1,0:T(8,128)S(1)}, u32[]{:S(2)}, u32[]{:S(2)}) collective-permute-start(f32[16,128]{1,0:T(8,128)S(1)} %get-tuple-element.81), channel_id=1, source_target_pairs={{8,3},{12,7},{16,11},{20,15},{24,19},{28,23}} | collective-permute-start | bytes 24584 | tf_op jit(solution)/shard_map/ppermute | solution.py:665
  61.6 0.7 %collective-permute-done.20.refs_7_ = f32[16,128]{1,0:T(8,128)S(1)} collective-permute-done((f32[16,128]{1,0:T(8,128)S(1)}, f32[16,128]{1,0:T(8,128)S(1)}, u32[]{:S(2)}, u32[]{:S(2)}) %collective-permute-start.20) | collective-permute-done | bytes 8224 | tf_op jit(solution)/shard_map/ppermute | solution.py:665
  62.3 1.2 %finish.1 = (f32[4,16,128]{2,1,0:T(8,128)}, f32[4,16,128]{2,1,0:T(8,128)}) custom-call(s32[4]{0:T(128)S(1)} %copy-done.7, f32[31]{0:T(128)S(1)} %copy-done.8, f32[4,16,128]{2,1,0:T(8,128)S(1)} %copy-done.3, f32[16,128]{1,0:T(8,128)S(1)} %copy-done.4, f32[16,128]{1,0:T(8,128)S(1)} %get-tuple-element.74.refs_0_, ...), custom_call_target="tpu_custom_call" | custom-call | flops 1000000000 | bytes 1000000 | tf_op jit(solution)/shard_map/finish/pallas_call | solution.py:671
  (44 shorter events, 0.8 us)
Async XLA Ops:
  0.6 7.0 %copy-start = (f32[30,5,1152]{2,0,1:T(8,128)S(1)}, f32[30,5,1152]{2,0,1:T(8,128)}, u32[]{:S(2)}) copy-start(f32[30,5,1152]{2,0,1:T(8,128)} %param.16) | copy-start | bytes 2073604
  1.8 11.5 %collective-permute-start = (bf16[16,4864]{1,0:T(8,128)(2,1)S(1)}, bf16[16,4864]{1,0:T(8,128)(2,1)S(1)}, u32[]{:S(2)}, u32[]{:S(2)}) collective-permute-start(bf16[16,4864]{1,0:T(8,128)(2,1)S(1)} %get-tuple-element.45), channel_id=1, source_target_pairs={{0,1},{1,0},{2,3},{3,2},{4,5},{5,4},{6,7},{7,6},{8,9},{9,8},{10,11... | collective-permute-start | bytes 466952 | tf_op jit(solution)/shard_map/ppermute | solution.py:499
  3.9 9.4 %collective-permute-start.1 = (bf16[16,4864]{1,0:T(8,128)(2,1)S(1)}, bf16[16,4864]{1,0:T(8,128)(2,1)S(1)}, u32[]{:S(2)}, u32[]{:S(2)}) collective-permute-start(bf16[16,4864]{1,0:T(8,128)(2,1)S(1)} %get-tuple-element.46), channel_id=1, source_target_pairs={{0,2},{1,3},{2,0},{3,1},{4,6},{5,7},{6,4},{7,5},{8,10},{9,11},{10,... | collective-permute-start | bytes 466952 | tf_op jit(solution)/shard_map/ppermute | solution.py:499
  5.2 11.6 %collective-permute-start.2 = (bf16[16,4864]{1,0:T(8,128)(2,1)S(1)}, bf16[16,4864]{1,0:T(8,128)(2,1)S(1)}, u32[]{:S(2)}, u32[]{:S(2)}) collective-permute-start(bf16[16,4864]{1,0:T(8,128)(2,1)S(1)} %get-tuple-element.47), channel_id=1, source_target_pairs={{0,3},{1,2},{2,1},{3,0},{4,7},{5,6},{6,5},{7,4},{8,11},{9,10},{10,... | collective-permute-start | bytes 466952 | tf_op jit(solution)/shard_map/ppermute | solution.py:499
  5.2 13.4 %collective-permute-start.3 = (bf16[16,6784]{1,0:T(8,128)(2,1)S(1)}, bf16[16,6784]{1,0:T(8,128)(2,1)S(1)}, u32[]{:S(2)}, u32[]{:S(2)}) collective-permute-start(bf16[16,6784]{1,0:T(8,128)(2,1)S(1)} %get-tuple-element.42.mine.refs_8_), channel_id=1, source_target_pairs={{0,4},{1,5},{2,6},{3,7},{4,0},{5,1},{6,2},{7,3},{8,12},{9,13},{10,... | collective-permute-start | bytes 651272 | tf_op jit(solution)/shard_map/ppermute | solution.py:499
  16.9 3.3 %collective-permute-start.4 = (bf16[16,4864]{1,0:T(8,128)(2,1)S(1)}, bf16[16,4864]{1,0:T(8,128)(2,1)S(1)}, u32[]{:S(2)}, u32[]{:S(2)}) collective-permute-start(bf16[16,4864]{1,0:T(8,128)(2,1)S(1)} %collective-permute-done.refs_0_.refs_10_), channel_id=1, source_target_pairs={{0,8},{8,0},{16,24},{24,16},{1,9},{9,1},{17,25},{25,17},{2,10},{10... | collective-permute-start | bytes 466952 | tf_op jit(solution)/shard_map/ppermute | solution.py:502
  18.2 3.3 %collective-permute-start.5 = (bf16[16,4864]{1,0:T(8,128)(2,1)S(1)}, bf16[16,4864]{1,0:T(8,128)(2,1)S(1)}, u32[]{:S(2)}, u32[]{:S(2)}) collective-permute-start(bf16[16,4864]{1,0:T(8,128)(2,1)S(1)} %collective-permute-done.1.refs_1_.refs_11_), channel_id=1, source_target_pairs={{0,8},{8,0},{16,24},{24,16},{1,9},{9,1},{17,25},{25,17},{2,10},{10... | collective-permute-start | bytes 466952 | tf_op jit(solution)/shard_map/ppermute | solution.py:502
  18.2 4.3 %collective-permute-start.6 = (bf16[16,4864]{1,0:T(8,128)(2,1)S(1)}, bf16[16,4864]{1,0:T(8,128)(2,1)S(1)}, u32[]{:S(2)}, u32[]{:S(2)}) collective-permute-start(bf16[16,4864]{1,0:T(8,128)(2,1)S(1)} %collective-permute-done.2.refs_2_.refs_12_), channel_id=1, source_target_pairs={{0,8},{8,0},{16,24},{24,16},{1,9},{9,1},{17,25},{25,17},{2,10},{10... | collective-permute-start | bytes 466952 | tf_op jit(solution)/shard_map/ppermute | solution.py:502
  18.7 15.1 %collective-permute-start.7 = (bf16[16,7936]{1,0:T(8,128)(2,1)S(1)}, bf16[16,7936]{1,0:T(8,128)(2,1)S(1)}, u32[]{:S(2)}, u32[]{:S(2)}) collective-permute-start(bf16[16,7936]{1,0:T(8,128)(2,1)S(1)} %join.1), channel_id=1, source_target_pairs={{0,1},{1,0},{2,3},{3,2},{4,5},{5,4},{6,7},{7,6},{8,9},{9,8},{10,11... | collective-permute-start | bytes 761864 | tf_op jit(solution)/shard_map/ppermute | solution.py:499
  20.1 13.6 %collective-permute-start.8 = (bf16[16,7936]{1,0:T(8,128)(2,1)S(1)}, bf16[16,7936]{1,0:T(8,128)(2,1)S(1)}, u32[]{:S(2)}, u32[]{:S(2)}) collective-permute-start(bf16[16,7936]{1,0:T(8,128)(2,1)S(1)} %join.1), channel_id=1, source_target_pairs={{0,2},{1,3},{2,0},{3,1},{4,6},{5,7},{6,4},{7,5},{8,10},{9,11},{10,... | collective-permute-start | bytes 761864 | tf_op jit(solution)/shard_map/ppermute | solution.py:499
  20.2 13.6 %collective-permute-start.9 = (bf16[16,7936]{1,0:T(8,128)(2,1)S(1)}, bf16[16,7936]{1,0:T(8,128)(2,1)S(1)}, u32[]{:S(2)}, u32[]{:S(2)}) collective-permute-start(bf16[16,7936]{1,0:T(8,128)(2,1)S(1)} %join.1), channel_id=1, source_target_pairs={{0,3},{1,2},{2,1},{3,0},{4,7},{5,6},{6,5},{7,4},{8,11},{9,10},{10,... | collective-permute-start | bytes 761864 | tf_op jit(solution)/shard_map/ppermute | solution.py:499
  21.4 13.1 %collective-permute-start.10 = (bf16[16,6784]{1,0:T(8,128)(2,1)S(1)}, bf16[16,6784]{1,0:T(8,128)(2,1)S(1)}, u32[]{:S(2)}, u32[]{:S(2)}) collective-permute-start(bf16[16,6784]{1,0:T(8,128)(2,1)S(1)} %collective-permute-done.3.far_ref.refs_0_), channel_id=1, source_target_pairs={{0,8},{8,0},{16,24},{24,16},{1,9},{9,1},{17,25},{25,17},{2,10},{10... | collective-permute-start | bytes 651272 | tf_op jit(solution)/shard_map/ppermute | solution.py:502
  33.8 2.7 %collective-permute-start.11 = (bf16[16,7936]{1,0:T(8,128)(2,1)S(1)}, bf16[16,7936]{1,0:T(8,128)(2,1)S(1)}, u32[]{:S(2)}, u32[]{:S(2)}) collective-permute-start(bf16[16,7936]{1,0:T(8,128)(2,1)S(1)} %collective-permute-done.7.refs_1_), channel_id=1, source_target_pairs={{0,8},{8,0},{16,24},{24,16},{1,9},{9,1},{17,25},{25,17},{2,10},{10... | collective-permute-start | bytes 761864 | tf_op jit(solution)/shard_map/ppermute | solution.py:502
  33.9 2.6 %collective-permute-start.12 = (bf16[16,7936]{1,0:T(8,128)(2,1)S(1)}, bf16[16,7936]{1,0:T(8,128)(2,1)S(1)}, u32[]{:S(2)}, u32[]{:S(2)}) collective-permute-start(bf16[16,7936]{1,0:T(8,128)(2,1)S(1)} %collective-permute-done.8.refs_2_), channel_id=1, source_target_pairs={{0,8},{8,0},{16,24},{24,16},{1,9},{9,1},{17,25},{25,17},{2,10},{10... | collective-permute-start | bytes 761864 | tf_op jit(solution)/shard_map/ppermute | solution.py:502
  34.4 2.2 %collective-permute-start.13 = (bf16[16,7936]{1,0:T(8,128)(2,1)S(1)}, bf16[16,7936]{1,0:T(8,128)(2,1)S(1)}, u32[]{:S(2)}, u32[]{:S(2)}) collective-permute-start(bf16[16,7936]{1,0:T(8,128)(2,1)S(1)} %collective-permute-done.9.refs_3_), channel_id=1, source_target_pairs={{0,8},{8,0},{16,24},{24,16},{1,9},{9,1},{17,25},{25,17},{2,10},{10... | collective-permute-start | bytes 761864 | tf_op jit(solution)/shard_map/ppermute | solution.py:502
  36.6 25.8 %copy-start.3 = (f32[4,16,128]{2,1,0:T(8,128)S(1)}, f32[4,16,128]{2,1,0:T(8,128)}, u32[]{:S(2)}) copy-start(f32[4,16,128]{2,1,0:T(8,128)} %latents_ref.3) | copy-start | bytes 98308
  36.6 25.8 %copy-start.4 = (f32[16,128]{1,0:T(8,128)S(1)}, f32[16,128]{1,0:T(8,128)}, u32[]{:S(2)}) copy-start(f32[16,128]{1,0:T(8,128)} %noise_ref.1) | copy-start | bytes 24580
  51.4 7.5 %collective-permute-start.14 = (f32[16,128]{1,0:T(8,128)S(1)}, f32[16,128]{1,0:T(8,128)S(1)}, u32[]{:S(2)}, u32[]{:S(2)}) collective-permute-start(f32[16,128]{1,0:T(8,128)S(1)} %get-tuple-element.75), channel_id=1, source_target_pairs={{0,1},{1,0},{2,3},{3,2},{4,5},{5,4},{6,7},{7,6},{8,9},{9,8},{10,11... | collective-permute-start | bytes 24584 | tf_op jit(solution)/shard_map/ppermute | solution.py:499
  52.8 7.5 %collective-permute-start.15 = (f32[16,128]{1,0:T(8,128)S(1)}, f32[16,128]{1,0:T(8,128)S(1)}, u32[]{:S(2)}, u32[]{:S(2)}) collective-permute-start(f32[16,128]{1,0:T(8,128)S(1)} %get-tuple-element.76), channel_id=1, source_target_pairs={{0,2},{1,3},{2,0},{3,1},{4,6},{5,7},{6,4},{7,5},{8,10},{9,11},{10,... | collective-permute-start | bytes 24584 | tf_op jit(solution)/shard_map/ppermute | solution.py:499
  53.4 8.1 %collective-permute-start.16 = (f32[16,128]{1,0:T(8,128)S(1)}, f32[16,128]{1,0:T(8,128)S(1)}, u32[]{:S(2)}, u32[]{:S(2)}) collective-permute-start(f32[16,128]{1,0:T(8,128)S(1)} %get-tuple-element.77), channel_id=1, source_target_pairs={{0,3},{1,2},{2,1},{3,0},{4,7},{5,6},{6,5},{7,4},{8,11},{9,10},{10,... | collective-permute-start | bytes 24584 | tf_op jit(solution)/shard_map/ppermute | solution.py:499
  54.4 7.2 %collective-permute-start.17 = (f32[16,128]{1,0:T(8,128)S(1)}, f32[16,128]{1,0:T(8,128)S(1)}, u32[]{:S(2)}, u32[]{:S(2)}) collective-permute-start(f32[16,128]{1,0:T(8,128)S(1)} %get-tuple-element.78), channel_id=1, source_target_pairs={{8,0},{12,4},{16,8},{20,12},{24,16},{28,20}} | collective-permute-start | bytes 24584 | tf_op jit(solution)/shard_map/ppermute | solution.py:665
  57.3 4.3 %collective-permute-start.18 = (f32[16,128]{1,0:T(8,128)S(1)}, f32[16,128]{1,0:T(8,128)S(1)}, u32[]{:S(2)}, u32[]{:S(2)}) collective-permute-start(f32[16,128]{1,0:T(8,128)S(1)} %get-tuple-element.79), channel_id=1, source_target_pairs={{8,1},{12,5},{16,9},{20,13},{24,17},{28,21}} | collective-permute-start | bytes 24584 | tf_op jit(solution)/shard_map/ppermute | solution.py:665
  59.0 2.6 %collective-permute-start.19 = (f32[16,128]{1,0:T(8,128)S(1)}, f32[16,128]{1,0:T(8,128)S(1)}, u32[]{:S(2)}, u32[]{:S(2)}) collective-permute-start(f32[16,128]{1,0:T(8,128)S(1)} %get-tuple-element.80), channel_id=1, source_target_pairs={{8,2},{12,6},{16,10},{20,14},{24,18},{28,22}} | collective-permute-start | bytes 24584 | tf_op jit(solution)/shard_map/ppermute | solution.py:665
  60.3 2.1 %collective-permute-start.20 = (f32[16,128]{1,0:T(8,128)S(1)}, f32[16,128]{1,0:T(8,128)S(1)}, u32[]{:S(2)}, u32[]{:S(2)}) collective-permute-start(f32[16,128]{1,0:T(8,128)S(1)} %get-tuple-element.81), channel_id=1, source_target_pairs={{8,3},{12,7},{16,11},{20,15},{24,19},{28,23}} | collective-permute-start | bytes 24584 | tf_op jit(solution)/shard_map/ppermute | solution.py:665
  (6 other events, 37.9 us)

commit v7 on v6

--- a/solution.py
+++ b/solution.py
@@ -202,7 +202,7 @@
     return jnp.where(inside, values, jnp.zeros_like(values))
 
 
-def attend_self(sizes, q_ref, k_ref, v_ref, num_ref, sum_ref, fresh, q_step=512):
+def attend_self(sizes, q_ref, k_ref, v_ref, num_ref, sum_ref, before, q_step=512):
     queries, width = q_ref.shape
     keys = k_ref.shape[0]
     q_step = min(q_step, queries)
@@ -231,16 +231,13 @@
                 sums = sums + jnp.where(tops, left, 0.0)
                 pending = pending + jnp.where(tops, 0.0, left)
             if last >= start + LANES:
-                if fresh:
-                    num_ref[rows, start : start + LANES] = pending
-                else:
-                    num_ref[rows, start : start + LANES] += pending
+                columns = slice(start, start + LANES)
+                if before is not None:
+                    pending = before[0][rows, columns] + pending
+                num_ref[rows, columns] = pending
                 wide = end - start > LANES
                 pending = both[:, LANES:] if wide else jnp.zeros((q_step, LANES), F32)
-        if fresh:
-            sum_ref[rows, :] = sums
-        else:
-            sum_ref[rows, :] += sums
+        sum_ref[rows, :] = sums if before is None else before[1][rows, :] + sums
 
 
 def attend_text(sizes, q_ref, k_scr, v_scr, num_ref, sum_ref, q_step=512):
@@ -346,7 +343,7 @@
 def attend_kernel(sizes, q_ref, k_ref, v_ref, out_weight_ref, num_ref, sum_ref, near_ref, sem):
     copy = pltpu.make_async_copy(out_weight_ref, near_ref, sem)
     copy.start()
-    attend_self(sizes, q_ref, k_ref, v_ref, num_ref, sum_ref, True)
+    attend_self(sizes, q_ref, k_ref, v_ref, num_ref, sum_ref, None)
     copy.wait()
 
 
@@ -386,8 +383,7 @@
         text_scr, tk_scr, tv_scr, tnum_scr, tsum_scr, attention_scr,
     ) = refs[2 * frames :]
     sums_matrix, spread_matrix = head_sums(sizes), head_spread(sizes)
-    num_ref[...] = num_in_ref[...]
-    sum_ref[...] = sum_in_ref[...]
+    before = num_in_ref, sum_in_ref
     for group in range(share - 1):
         first = slice(group * tokens, (group + 1) * tokens)
         k_scr[:tokens, :] = far_k_ref[first, :]
@@ -402,7 +398,8 @@
         project(normed_scr, weight_ref, 2 * width, 3 * width, v_scr.at[tokens:, :])
         keys = k_scr.at[tokens:, :]
         norm_rows(sizes, proj_scr, keys, rows_ref[6:7, :], sums_matrix, spread_matrix)
-        attend_self(sizes, q_ref, k_scr, v_scr, num_ref, sum_ref, False)
+        attend_self(sizes, q_ref, k_scr, v_scr, num_ref, sum_ref, before)
+        before = num_ref, sum_ref
 
     place = lax.axis_index("seq")
     unpack_text(sizes, place, payload_ref, payload_other_ref, sizes.text_at, text_scr)
@@ -422,9 +419,10 @@
     tv_scr[...] = text_scr[1].astype(BF16)
     attend_text(sizes, q_ref, tk_scr, tv_scr, tnum_scr, tsum_scr)
 
-    for start in range(0, sizes.queries, LANES):
-        rows = slice(start, start + LANES)
-        used = lane_mask((LANES, LANES), 0, sizes.heads)
+    step = 2 * LANES
+    for start in range(0, sizes.queries, step):
+        rows = slice(start, start + step)
+        used = lane_mask((step, LANES), 0, sizes.heads)
         own = spread(jnp.where(used, 1.0 / sum_ref[rows, :], 0.0), spread_matrix)
         text = spread(jnp.where(used, 1.0 / tsum_scr[rows, :], 0.0), spread_matrix)
         attention_scr[rows, :] = (num_ref[rows, :] * own + tnum_scr[rows, :] * text).astype(BF16)

time: 64 us -> 63.9 us (level)
  no operation moved by 1% of the time
where the time goes in v7:
time: 63.9 us; the launch traced here: 63.5 us
  Pallas kernels  35.9 us (56%)
  starting transfers between devices  22.2 us (35%)
  waiting for transfers between devices  4.34 us (7%)
  between operations  0.93 us (1%)
    pallas_call x1, Pallas kernels, body(): kernel(rest_kernel, sizes, 'rest', 'v' * (2 * len(mine) + 12 + frames), [...  14.7 us
    ppermute x10, starting transfers between devices, swapped(): return lax.ppermute(value, 'seq', [(i, i ^ d) for i in range(sizes.seq)])  11.5 us
    ppermute x4, starting transfers between devices, to_previous(): return lax.ppermute(value, ('queue', 'seq'), route)  7.15 us
    pallas_call x1, Pallas kernels, body(): kernel(own_kernel, sizes, 'own', 'v' * (2 * (frames - 1) + 7), token_arra...  6.31 us
    pallas_call x1, Pallas kernels, body(): kernel(first_kernel, sizes, 'first', 'ssvvvvvvh', [pltpu.VMEM((8, width),...  5.55 us
    pallas_call x1, Pallas kernels, body(): kernel(attend_kernel, sizes, 'attend', 'vvvh', [pltpu.VMEM((queries, widt...  4.93 us
    ppermute x10, waiting for transfers between devices, swapped(): return lax.ppermute(value, 'seq', [(i, i ^ d) for i in range(sizes.seq)])  3.58 us
    ppermute x7, starting transfers between devices, over_cores(): return lax.ppermute(value, 'queue', [(i, i ^ 1) for i in range(queue)])  3.56 us
  transfers between devices with their start and end apart: 21, of which 2 were waited for; matrix products, arithmetic and copies ran while one was open for 0% of the time, Pallas kernels for 30%

profile of v7, /device:TPU:1, one launch (start us, length us, event | category | flops | bytes accessed | tf_op | source)
XLA Modules:
  0.0 63.5 jit_solution(16740704961993069995)
XLA Ops:
  0.7 1.1 %prep.1 = (bf16[16,6784]{1,0:T(8,128)(2,1)S(1)}, bf16[16,6784]{1,0:T(8,128)(2,1)S(1)}, bf16[16,1152]{1,0:T(8,128)(2,1)S(1)}, bf16[16,4864]{1,0:T(8,128)(2,1)S(1)...) custom-call(bf16[128,1152]{1,0:T(8,128)(2,1)} %position_ref.1, f32[4,16,128]{2,1,0:T(8,128)} %latents_ref.3, ...), custom_call_target="tpu_custom_call" | custom-call | flops 1500000000 | bytes 1500000 | tf_op jit(solution)/shard_map/prep/pallas_call | solution.py:504
  1.8 2.1 %collective-permute-start = (bf16[16,4864]{1,0:T(8,128)(2,1)S(1)}, bf16[16,4864]{1,0:T(8,128)(2,1)S(1)}, u32[]{:S(2)}, u32[]{:S(2)}) collective-permute-start(bf16[16,4864]{1,0:T(8,128)(2,1)S(1)} %get-tuple-element.45), channel_id=1, source_target_pairs={{0,1},{1,0},{2,3},{3,2},{4,5},{5,4},{6,7},{7,6},{8,9},{9,8},{10,11... | collective-permute-start | bytes 466952 | tf_op jit(solution)/shard_map/ppermute | solution.py:497
  3.9 1.3 %collective-permute-start.1 = (bf16[16,4864]{1,0:T(8,128)(2,1)S(1)}, bf16[16,4864]{1,0:T(8,128)(2,1)S(1)}, u32[]{:S(2)}, u32[]{:S(2)}) collective-permute-start(bf16[16,4864]{1,0:T(8,128)(2,1)S(1)} %get-tuple-element.46), channel_id=1, source_target_pairs={{0,2},{1,3},{2,0},{3,1},{4,6},{5,7},{6,4},{7,5},{8,10},{9,11},{10,... | collective-permute-start | bytes 466952 | tf_op jit(solution)/shard_map/ppermute | solution.py:497
  5.2 2.4 %collective-permute-start.3 = (bf16[16,6784]{1,0:T(8,128)(2,1)S(1)}, bf16[16,6784]{1,0:T(8,128)(2,1)S(1)}, u32[]{:S(2)}, u32[]{:S(2)}) collective-permute-start(bf16[16,6784]{1,0:T(8,128)(2,1)S(1)} %get-tuple-element.42.mine.refs_8_), channel_id=1, source_target_pairs={{0,4},{1,5},{2,6},{3,7},{4,0},{5,1},{6,2},{7,3},{8,12},{9,13},{10,... | collective-permute-start | bytes 651272 | tf_op jit(solution)/shard_map/ppermute | solution.py:497
  7.7 5.6 %first.1 = (f32[8,1152]{1,0:T(8,128)S(1)}, bf16[1152,3456]{1,0:T(8,128)(2,1)S(1)}, bf16[128,1152]{1,0:T(8,128)(2,1)S(1)}, bf16[128,1152]{1,0:T(8,128)(2,1)S(1)},...) custom-call(s32[4]{0:T(128)S(1)} %copy-done.7, f32[31]{0:T(128)S(1)} %copy-done.8, f32[5,30,1152]{2,1,0:T(8,128)S(1)} %bitcast.5, ...), custom_call_target="tpu_custom_call" | custom-call | flops 4000000000 | bytes 4000000 | tf_op jit(solution)/shard_map/first/pallas_call | solution.py:539
  13.3 3.6 %collective-permute-done.2.refs_2_.refs_12_ = bf16[16,4864]{1,0:T(8,128)(2,1)S(1)} collective-permute-done((bf16[16,4864]{1,0:T(8,128)(2,1)S(1)}, bf16[16,4864]{1,0:T(8,128)(2,1)S(1)}, u32[]{:S(2)}, u32[]{:S(2)}) %collective-permute-start.2) | collective-permute-done | bytes 155680 | tf_op jit(solution)/shard_map/ppermute | solution.py:497
  16.9 1.3 %collective-permute-start.4 = (bf16[16,4864]{1,0:T(8,128)(2,1)S(1)}, bf16[16,4864]{1,0:T(8,128)(2,1)S(1)}, u32[]{:S(2)}, u32[]{:S(2)}) collective-permute-start(bf16[16,4864]{1,0:T(8,128)(2,1)S(1)} %collective-permute-done.refs_0_.refs_10_), channel_id=1, source_target_pairs={{0,8},{8,0},{16,24},{24,16},{1,9},{9,1},{17,25},{25,17},{2,10},{10... | collective-permute-start | bytes 466952 | tf_op jit(solution)/shard_map/ppermute | solution.py:500
  18.2 0.5 collective-permute-start.6
  18.7 1.4 %collective-permute-start.7 = (bf16[16,7936]{1,0:T(8,128)(2,1)S(1)}, bf16[16,7936]{1,0:T(8,128)(2,1)S(1)}, u32[]{:S(2)}, u32[]{:S(2)}) collective-permute-start(bf16[16,7936]{1,0:T(8,128)(2,1)S(1)} %join.1), channel_id=1, source_target_pairs={{0,1},{1,0},{2,3},{3,2},{4,5},{5,4},{6,7},{7,6},{8,9},{9,8},{10,11... | collective-permute-start | bytes 761864 | tf_op jit(solution)/shard_map/ppermute | solution.py:497
  20.2 1.3 %collective-permute-start.9 = (bf16[16,7936]{1,0:T(8,128)(2,1)S(1)}, bf16[16,7936]{1,0:T(8,128)(2,1)S(1)}, u32[]{:S(2)}, u32[]{:S(2)}) collective-permute-start(bf16[16,7936]{1,0:T(8,128)(2,1)S(1)} %join.1), channel_id=1, source_target_pairs={{0,3},{1,2},{2,1},{3,0},{4,7},{5,6},{6,5},{7,4},{8,11},{9,10},{10,... | collective-permute-start | bytes 761864 | tf_op jit(solution)/shard_map/ppermute | solution.py:497
  21.4 1.1 %collective-permute-start.10 = (bf16[16,6784]{1,0:T(8,128)(2,1)S(1)}, bf16[16,6784]{1,0:T(8,128)(2,1)S(1)}, u32[]{:S(2)}, u32[]{:S(2)}) collective-permute-start(bf16[16,6784]{1,0:T(8,128)(2,1)S(1)} %collective-permute-done.3.far_ref.refs_0_), channel_id=1, source_target_pairs={{0,8},{8,0},{16,24},{24,16},{1,9},{9,1},{17,25},{25,17},{2,10},{10... | collective-permute-start | bytes 651272 | tf_op jit(solution)/shard_map/ppermute | solution.py:500
  22.5 6.3 %own.1 = (bf16[512,1152]{1,0:T(8,128)(2,1)S(1)}, bf16[512,1152]{1,0:T(8,128)(2,1)S(1)}, bf16[512,1152]{1,0:T(8,128)(2,1)S(1)}, f32[512,1152]{1,0:T(8,128)S(1)}) custom-call(bf16[16,4864]{1,0:T(8,128)(2,1)S(1)} %collective-permute-done.refs_0_.refs_10_, bf16[16,4864]{1,0:T(8,128)(2,1)S(1)} %collective-permute-done.1.refs_1_.refs_11_, ...), custom_call_target="tpu_custom_call" | custom-call | flops 8000000000 | bytes 8000000 | tf_op jit(solution)/shard_map/own/pallas_call | solution.py:577
  28.8 4.9 %attend.1 = (f32[512,1152]{1,0:T(8,128)S(1)}, f32[512,128]{1,0:T(8,128)S(1)}, bf16[1152,1152]{1,0:T(8,128)(2,1)S(1)}) custom-call(bf16[512,1152]{1,0:T(8,128)(2,1)S(1)} %get-tuple-element.59.q_ref.refs_16_, bf16[512,1152]{1,0:T(8,128)(2,1)S(1)} %get-tuple-element.60.k_ref, bf16[512,1152]{1,0:T(8,128)(2,1)S(1)} %get-tuple-element.61.v_ref, ...), custom_call_target="tpu_custom_call" | custom-call | flops 5000000000 | bytes 5000000 | tf_op jit(solution)/shard_map/attend/pallas_call | solution.py:586
  34.5 2.1 %far.1 = (bf16[128,1152]{1,0:T(8,128)(2,1)S(1)}, bf16[128,1152]{1,0:T(8,128)(2,1)S(1)}) custom-call(bf16[16,6784]{1,0:T(8,128)(2,1)S(1)} %collective-permute-done.3.far_ref.refs_0_, bf16[16,6784]{1,0:T(8,128)(2,1)S(1)} %collective-permute-done.10.refs_1_.refs_4_, bf16[16,1152]{1,0:T(8,128)(2,1)S(1)} %copy-done.1, ...), custom_call_target="tpu_custom_call" | custom-call | flops 2500000000 | bytes 2500000 | tf_op jit(solution)/shard_map/far/pallas_call | solution.py:602
  36.6 14.7 %rest.1 = (f32[16,128]{1,0:T(8,128)S(1)}, f32[16,128]{1,0:T(8,128)S(1)}, f32[16,128]{1,0:T(8,128)S(1)}, f32[16,128]{1,0:T(8,128)S(1)}, f32[16,128]{1,0:T(8,128)S...) custom-call(bf16[16,6784]{1,0:T(8,128)(2,1)S(1)} %collective-permute-done.3.far_ref.refs_0_, ...), custom_call_target="tpu_custom_call" | custom-call | flops 17999998976 | bytes 18000000 | tf_op jit(solution)/shard_map/rest/pallas_call | solution.py:616
  51.3 1.4 %collective-permute-start.14 = (f32[16,128]{1,0:T(8,128)S(1)}, f32[16,128]{1,0:T(8,128)S(1)}, u32[]{:S(2)}, u32[]{:S(2)}) collective-permute-start(f32[16,128]{1,0:T(8,128)S(1)} %get-tuple-element.75), channel_id=1, source_target_pairs={{0,1},{1,0},{2,3},{3,2},{4,5},{5,4},{6,7},{7,6},{8,9},{9,8},{10,11... | collective-permute-start | bytes 24584 | tf_op jit(solution)/shard_map/ppermute | solution.py:497
  52.7 0.6 collective-permute-start.15
  53.3 0.9 %collective-permute-start.16 = (f32[16,128]{1,0:T(8,128)S(1)}, f32[16,128]{1,0:T(8,128)S(1)}, u32[]{:S(2)}, u32[]{:S(2)}) collective-permute-start(f32[16,128]{1,0:T(8,128)S(1)} %get-tuple-element.77), channel_id=1, source_target_pairs={{0,3},{1,2},{2,1},{3,0},{4,7},{5,6},{6,5},{7,4},{8,11},{9,10},{10,... | collective-permute-start | bytes 24584 | tf_op jit(solution)/shard_map/ppermute | solution.py:497
  54.3 2.9 %collective-permute-start.17 = (f32[16,128]{1,0:T(8,128)S(1)}, f32[16,128]{1,0:T(8,128)S(1)}, u32[]{:S(2)}, u32[]{:S(2)}) collective-permute-start(f32[16,128]{1,0:T(8,128)S(1)} %get-tuple-element.78), channel_id=1, source_target_pairs={{8,0},{12,4},{16,8},{20,12},{24,16},{28,20}} | collective-permute-start | bytes 24584 | tf_op jit(solution)/shard_map/ppermute | solution.py:663
  57.2 1.7 %collective-permute-start.18 = (f32[16,128]{1,0:T(8,128)S(1)}, f32[16,128]{1,0:T(8,128)S(1)}, u32[]{:S(2)}, u32[]{:S(2)}) collective-permute-start(f32[16,128]{1,0:T(8,128)S(1)} %get-tuple-element.79), channel_id=1, source_target_pairs={{8,1},{12,5},{16,9},{20,13},{24,17},{28,21}} | collective-permute-start | bytes 24584 | tf_op jit(solution)/shard_map/ppermute | solution.py:663
  58.9 1.3 %collective-permute-start.19 = (f32[16,128]{1,0:T(8,128)S(1)}, f32[16,128]{1,0:T(8,128)S(1)}, u32[]{:S(2)}, u32[]{:S(2)}) collective-permute-start(f32[16,128]{1,0:T(8,128)S(1)} %get-tuple-element.80), channel_id=1, source_target_pairs={{8,2},{12,6},{16,10},{20,14},{24,18},{28,22}} | collective-permute-start | bytes 24584 | tf_op jit(solution)/shard_map/ppermute | solution.py:663
  60.2 1.3 %collective-permute-start.20 = (f32[16,128]{1,0:T(8,128)S(1)}, f32[16,128]{1,0:T(8,128)S(1)}, u32[]{:S(2)}, u32[]{:S(2)}) collective-permute-start(f32[16,128]{1,0:T(8,128)S(1)} %get-tuple-element.81), channel_id=1, source_target_pairs={{8,3},{12,7},{16,11},{20,15},{24,19},{28,23}} | collective-permute-start | bytes 24584 | tf_op jit(solution)/shard_map/ppermute | solution.py:663
  61.5 0.7 %collective-permute-done.20.refs_7_ = f32[16,128]{1,0:T(8,128)S(1)} collective-permute-done((f32[16,128]{1,0:T(8,128)S(1)}, f32[16,128]{1,0:T(8,128)S(1)}, u32[]{:S(2)}, u32[]{:S(2)}) %collective-permute-start.20) | collective-permute-done | bytes 8224 | tf_op jit(solution)/shard_map/ppermute | solution.py:663
  62.3 1.2 %finish.1 = (f32[4,16,128]{2,1,0:T(8,128)}, f32[4,16,128]{2,1,0:T(8,128)}) custom-call(s32[4]{0:T(128)S(1)} %copy-done.7, f32[31]{0:T(128)S(1)} %copy-done.8, f32[4,16,128]{2,1,0:T(8,128)S(1)} %copy-done.3, f32[16,128]{1,0:T(8,128)S(1)} %copy-done.4, f32[16,128]{1,0:T(8,128)S(1)} %get-tuple-element.74.refs_0_, ...), custom_call_target="tpu_custom_call" | custom-call | flops 1000000000 | bytes 1000000 | tf_op jit(solution)/shard_map/finish/pallas_call | solution.py:669
  (44 shorter events, 0.8 us)
Async XLA Ops:
  0.6 7.0 %copy-start = (f32[30,5,1152]{2,0,1:T(8,128)S(1)}, f32[30,5,1152]{2,0,1:T(8,128)}, u32[]{:S(2)}) copy-start(f32[30,5,1152]{2,0,1:T(8,128)} %param.16) | copy-start | bytes 2073604
  1.8 11.5 %collective-permute-start = (bf16[16,4864]{1,0:T(8,128)(2,1)S(1)}, bf16[16,4864]{1,0:T(8,128)(2,1)S(1)}, u32[]{:S(2)}, u32[]{:S(2)}) collective-permute-start(bf16[16,4864]{1,0:T(8,128)(2,1)S(1)} %get-tuple-element.45), channel_id=1, source_target_pairs={{0,1},{1,0},{2,3},{3,2},{4,5},{5,4},{6,7},{7,6},{8,9},{9,8},{10,11... | collective-permute-start | bytes 466952 | tf_op jit(solution)/shard_map/ppermute | solution.py:497
  3.9 9.4 %collective-permute-start.1 = (bf16[16,4864]{1,0:T(8,128)(2,1)S(1)}, bf16[16,4864]{1,0:T(8,128)(2,1)S(1)}, u32[]{:S(2)}, u32[]{:S(2)}) collective-permute-start(bf16[16,4864]{1,0:T(8,128)(2,1)S(1)} %get-tuple-element.46), channel_id=1, source_target_pairs={{0,2},{1,3},{2,0},{3,1},{4,6},{5,7},{6,4},{7,5},{8,10},{9,11},{10,... | collective-permute-start | bytes 466952 | tf_op jit(solution)/shard_map/ppermute | solution.py:497
  5.2 11.6 %collective-permute-start.2 = (bf16[16,4864]{1,0:T(8,128)(2,1)S(1)}, bf16[16,4864]{1,0:T(8,128)(2,1)S(1)}, u32[]{:S(2)}, u32[]{:S(2)}) collective-permute-start(bf16[16,4864]{1,0:T(8,128)(2,1)S(1)} %get-tuple-element.47), channel_id=1, source_target_pairs={{0,3},{1,2},{2,1},{3,0},{4,7},{5,6},{6,5},{7,4},{8,11},{9,10},{10,... | collective-permute-start | bytes 466952 | tf_op jit(solution)/shard_map/ppermute | solution.py:497
  5.2 13.4 %collective-permute-start.3 = (bf16[16,6784]{1,0:T(8,128)(2,1)S(1)}, bf16[16,6784]{1,0:T(8,128)(2,1)S(1)}, u32[]{:S(2)}, u32[]{:S(2)}) collective-permute-start(bf16[16,6784]{1,0:T(8,128)(2,1)S(1)} %get-tuple-element.42.mine.refs_8_), channel_id=1, source_target_pairs={{0,4},{1,5},{2,6},{3,7},{4,0},{5,1},{6,2},{7,3},{8,12},{9,13},{10,... | collective-permute-start | bytes 651272 | tf_op jit(solution)/shard_map/ppermute | solution.py:497
  16.9 3.3 %collective-permute-start.4 = (bf16[16,4864]{1,0:T(8,128)(2,1)S(1)}, bf16[16,4864]{1,0:T(8,128)(2,1)S(1)}, u32[]{:S(2)}, u32[]{:S(2)}) collective-permute-start(bf16[16,4864]{1,0:T(8,128)(2,1)S(1)} %collective-permute-done.refs_0_.refs_10_), channel_id=1, source_target_pairs={{0,8},{8,0},{16,24},{24,16},{1,9},{9,1},{17,25},{25,17},{2,10},{10... | collective-permute-start | bytes 466952 | tf_op jit(solution)/shard_map/ppermute | solution.py:500
  18.2 3.3 %collective-permute-start.5 = (bf16[16,4864]{1,0:T(8,128)(2,1)S(1)}, bf16[16,4864]{1,0:T(8,128)(2,1)S(1)}, u32[]{:S(2)}, u32[]{:S(2)}) collective-permute-start(bf16[16,4864]{1,0:T(8,128)(2,1)S(1)} %collective-permute-done.1.refs_1_.refs_11_), channel_id=1, source_target_pairs={{0,8},{8,0},{16,24},{24,16},{1,9},{9,1},{17,25},{25,17},{2,10},{10... | collective-permute-start | bytes 466952 | tf_op jit(solution)/shard_map/ppermute | solution.py:500
  18.2 4.3 %collective-permute-start.6 = (bf16[16,4864]{1,0:T(8,128)(2,1)S(1)}, bf16[16,4864]{1,0:T(8,128)(2,1)S(1)}, u32[]{:S(2)}, u32[]{:S(2)}) collective-permute-start(bf16[16,4864]{1,0:T(8,128)(2,1)S(1)} %collective-permute-done.2.refs_2_.refs_12_), channel_id=1, source_target_pairs={{0,8},{8,0},{16,24},{24,16},{1,9},{9,1},{17,25},{25,17},{2,10},{10... | collective-permute-start | bytes 466952 | tf_op jit(solution)/shard_map/ppermute | solution.py:500
  18.7 15.1 %collective-permute-start.7 = (bf16[16,7936]{1,0:T(8,128)(2,1)S(1)}, bf16[16,7936]{1,0:T(8,128)(2,1)S(1)}, u32[]{:S(2)}, u32[]{:S(2)}) collective-permute-start(bf16[16,7936]{1,0:T(8,128)(2,1)S(1)} %join.1), channel_id=1, source_target_pairs={{0,1},{1,0},{2,3},{3,2},{4,5},{5,4},{6,7},{7,6},{8,9},{9,8},{10,11... | collective-permute-start | bytes 761864 | tf_op jit(solution)/shard_map/ppermute | solution.py:497
  20.1 13.6 %collective-permute-start.8 = (bf16[16,7936]{1,0:T(8,128)(2,1)S(1)}, bf16[16,7936]{1,0:T(8,128)(2,1)S(1)}, u32[]{:S(2)}, u32[]{:S(2)}) collective-permute-start(bf16[16,7936]{1,0:T(8,128)(2,1)S(1)} %join.1), channel_id=1, source_target_pairs={{0,2},{1,3},{2,0},{3,1},{4,6},{5,7},{6,4},{7,5},{8,10},{9,11},{10,... | collective-permute-start | bytes 761864 | tf_op jit(solution)/shard_map/ppermute | solution.py:497
  20.2 13.6 %collective-permute-start.9 = (bf16[16,7936]{1,0:T(8,128)(2,1)S(1)}, bf16[16,7936]{1,0:T(8,128)(2,1)S(1)}, u32[]{:S(2)}, u32[]{:S(2)}) collective-permute-start(bf16[16,7936]{1,0:T(8,128)(2,1)S(1)} %join.1), channel_id=1, source_target_pairs={{0,3},{1,2},{2,1},{3,0},{4,7},{5,6},{6,5},{7,4},{8,11},{9,10},{10,... | collective-permute-start | bytes 761864 | tf_op jit(solution)/shard_map/ppermute | solution.py:497
  21.4 13.1 %collective-permute-start.10 = (bf16[16,6784]{1,0:T(8,128)(2,1)S(1)}, bf16[16,6784]{1,0:T(8,128)(2,1)S(1)}, u32[]{:S(2)}, u32[]{:S(2)}) collective-permute-start(bf16[16,6784]{1,0:T(8,128)(2,1)S(1)} %collective-permute-done.3.far_ref.refs_0_), channel_id=1, source_target_pairs={{0,8},{8,0},{16,24},{24,16},{1,9},{9,1},{17,25},{25,17},{2,10},{10... | collective-permute-start | bytes 651272 | tf_op jit(solution)/shard_map/ppermute | solution.py:500
  33.8 2.7 %collective-permute-start.11 = (bf16[16,7936]{1,0:T(8,128)(2,1)S(1)}, bf16[16,7936]{1,0:T(8,128)(2,1)S(1)}, u32[]{:S(2)}, u32[]{:S(2)}) collective-permute-start(bf16[16,7936]{1,0:T(8,128)(2,1)S(1)} %collective-permute-done.7.refs_1_), channel_id=1, source_target_pairs={{0,8},{8,0},{16,24},{24,16},{1,9},{9,1},{17,25},{25,17},{2,10},{10... | collective-permute-start | bytes 761864 | tf_op jit(solution)/shard_map/ppermute | solution.py:500
  33.9 2.6 %collective-permute-start.12 = (bf16[16,7936]{1,0:T(8,128)(2,1)S(1)}, bf16[16,7936]{1,0:T(8,128)(2,1)S(1)}, u32[]{:S(2)}, u32[]{:S(2)}) collective-permute-start(bf16[16,7936]{1,0:T(8,128)(2,1)S(1)} %collective-permute-done.8.refs_2_), channel_id=1, source_target_pairs={{0,8},{8,0},{16,24},{24,16},{1,9},{9,1},{17,25},{25,17},{2,10},{10... | collective-permute-start | bytes 761864 | tf_op jit(solution)/shard_map/ppermute | solution.py:500
  34.4 2.2 %collective-permute-start.13 = (bf16[16,7936]{1,0:T(8,128)(2,1)S(1)}, bf16[16,7936]{1,0:T(8,128)(2,1)S(1)}, u32[]{:S(2)}, u32[]{:S(2)}) collective-permute-start(bf16[16,7936]{1,0:T(8,128)(2,1)S(1)} %collective-permute-done.9.refs_3_), channel_id=1, source_target_pairs={{0,8},{8,0},{16,24},{24,16},{1,9},{9,1},{17,25},{25,17},{2,10},{10... | collective-permute-start | bytes 761864 | tf_op jit(solution)/shard_map/ppermute | solution.py:500
  36.6 25.7 %copy-start.3 = (f32[4,16,128]{2,1,0:T(8,128)S(1)}, f32[4,16,128]{2,1,0:T(8,128)}, u32[]{:S(2)}) copy-start(f32[4,16,128]{2,1,0:T(8,128)} %latents_ref.3) | copy-start | bytes 98308
  36.6 25.7 %copy-start.4 = (f32[16,128]{1,0:T(8,128)S(1)}, f32[16,128]{1,0:T(8,128)}, u32[]{:S(2)}) copy-start(f32[16,128]{1,0:T(8,128)} %noise_ref.1) | copy-start | bytes 24580
  51.3 7.5 %collective-permute-start.14 = (f32[16,128]{1,0:T(8,128)S(1)}, f32[16,128]{1,0:T(8,128)S(1)}, u32[]{:S(2)}, u32[]{:S(2)}) collective-permute-start(f32[16,128]{1,0:T(8,128)S(1)} %get-tuple-element.75), channel_id=1, source_target_pairs={{0,1},{1,0},{2,3},{3,2},{4,5},{5,4},{6,7},{7,6},{8,9},{9,8},{10,11... | collective-permute-start | bytes 24584 | tf_op jit(solution)/shard_map/ppermute | solution.py:497
  52.7 7.5 %collective-permute-start.15 = (f32[16,128]{1,0:T(8,128)S(1)}, f32[16,128]{1,0:T(8,128)S(1)}, u32[]{:S(2)}, u32[]{:S(2)}) collective-permute-start(f32[16,128]{1,0:T(8,128)S(1)} %get-tuple-element.76), channel_id=1, source_target_pairs={{0,2},{1,3},{2,0},{3,1},{4,6},{5,7},{6,4},{7,5},{8,10},{9,11},{10,... | collective-permute-start | bytes 24584 | tf_op jit(solution)/shard_map/ppermute | solution.py:497
  53.3 8.1 %collective-permute-start.16 = (f32[16,128]{1,0:T(8,128)S(1)}, f32[16,128]{1,0:T(8,128)S(1)}, u32[]{:S(2)}, u32[]{:S(2)}) collective-permute-start(f32[16,128]{1,0:T(8,128)S(1)} %get-tuple-element.77), channel_id=1, source_target_pairs={{0,3},{1,2},{2,1},{3,0},{4,7},{5,6},{6,5},{7,4},{8,11},{9,10},{10,... | collective-permute-start | bytes 24584 | tf_op jit(solution)/shard_map/ppermute | solution.py:497
  54.3 7.2 %collective-permute-start.17 = (f32[16,128]{1,0:T(8,128)S(1)}, f32[16,128]{1,0:T(8,128)S(1)}, u32[]{:S(2)}, u32[]{:S(2)}) collective-permute-start(f32[16,128]{1,0:T(8,128)S(1)} %get-tuple-element.78), channel_id=1, source_target_pairs={{8,0},{12,4},{16,8},{20,12},{24,16},{28,20}} | collective-permute-start | bytes 24584 | tf_op jit(solution)/shard_map/ppermute | solution.py:663
  57.2 4.3 %collective-permute-start.18 = (f32[16,128]{1,0:T(8,128)S(1)}, f32[16,128]{1,0:T(8,128)S(1)}, u32[]{:S(2)}, u32[]{:S(2)}) collective-permute-start(f32[16,128]{1,0:T(8,128)S(1)} %get-tuple-element.79), channel_id=1, source_target_pairs={{8,1},{12,5},{16,9},{20,13},{24,17},{28,21}} | collective-permute-start | bytes 24584 | tf_op jit(solution)/shard_map/ppermute | solution.py:663
  58.9 2.6 %collective-permute-start.19 = (f32[16,128]{1,0:T(8,128)S(1)}, f32[16,128]{1,0:T(8,128)S(1)}, u32[]{:S(2)}, u32[]{:S(2)}) collective-permute-start(f32[16,128]{1,0:T(8,128)S(1)} %get-tuple-element.80), channel_id=1, source_target_pairs={{8,2},{12,6},{16,10},{20,14},{24,18},{28,22}} | collective-permute-start | bytes 24584 | tf_op jit(solution)/shard_map/ppermute | solution.py:663
  60.2 2.1 %collective-permute-start.20 = (f32[16,128]{1,0:T(8,128)S(1)}, f32[16,128]{1,0:T(8,128)S(1)}, u32[]{:S(2)}, u32[]{:S(2)}) collective-permute-start(f32[16,128]{1,0:T(8,128)S(1)} %get-tuple-element.81), channel_id=1, source_target_pairs={{8,3},{12,7},{16,11},{20,15},{24,19},{28,23}} | collective-permute-start | bytes 24584 | tf_op jit(solution)/shard_map/ppermute | solution.py:663
  (6 other events, 37.9 us)
